TPU v7x, 128 devices: a whole 4x4x4 slice. The times are simulated.
128 devices in a mesh: bulk: 16 (over y, x), seq: 8 (over z, core).
Axes of the slice: x: 4, y: 4, z: 4, core: 2. Of those that a mesh axis runs over, the one named last changes fastest.
Arguments:
- clips: bfloat16 [4096, 4, 4, 4, 192], P(('bulk', 'seq')), may hold values from -6 to 6
- clip_counts: int32 [4096], P(('bulk', 'seq')), may hold values from 1 to 4
- histories: int32 [512, 64], P(('bulk', 'seq')), may hold values from 0 to 4095, as said below
- lengths: int32 [512], P(('bulk', 'seq')), may hold values from 1 to 64
- user_cotangent: float32 [512, 512], P(('bulk', 'seq')), may hold values from -6 to 6
- expand_first: bfloat16 [192, 432], replicated, may hold values from -0.4375 to 0.4375
- spatial_first: bfloat16 [9, 432], replicated, may hold values from -2 to 2
- temporal_first: bfloat16 [3, 432], replicated, may hold values from -3.5 to 3.5
- project_first: bfloat16 [432, 192], replicated, may hold values from -0.3125 to 0.3125
- expand_second: bfloat16 [192, 432], replicated, may hold values from -0.4375 to 0.4375
- spatial_second: bfloat16 [9, 432], replicated, may hold values from -2 to 2
- temporal_second: bfloat16 [3, 432], replicated, may hold values from -3.5 to 3.5
- project_second: bfloat16 [432, 192], replicated, may hold values from -0.3125 to 0.3125
- item_project: bfloat16 [192, 512], replicated, may hold values from -0.4375 to 0.4375
- tower_up: bfloat16 [512, 1024], replicated, may hold values from -0.25 to 0.25
- tower_down: bfloat16 [1024, 512], replicated, may hold values from -0.1875 to 0.1875
Outputs:
- user_vector: float32 [512, 512], P(('bulk', 'seq'))
- grad_expand_first: float32 [192, 432], replicated
- grad_spatial_first: float32 [9, 432], replicated
- grad_temporal_first: float32 [3, 432], replicated
- grad_project_first: float32 [432, 192], replicated
- grad_expand_second: float32 [192, 432], replicated
- grad_spatial_second: float32 [9, 432], replicated
- grad_temporal_second: float32 [3, 432], replicated
- grad_project_second: float32 [432, 192], replicated
- grad_item_project: float32 [192, 512], replicated
- grad_tower_up: float32 [512, 1024], replicated
- grad_tower_down: float32 [1024, 512], replicated
Inputs may be any that keep to these rules, and one draw needn't show every extreme that they name: `histories`: items k * 32 to (k + 1) * 32 - 1 belong to the k-th device in bulk+seq order. Among the 256 entries of one device, at most 4 name items of any one device; in every draw one device's items are named exactly 4 times by the entries of every device. Ids may repeat.
All inputs are finite; a program needn't handle non-finite values.
Results may differ from a plain program's by a relative error of at most 0.02.
Values may be sent and summed in bfloat16 or wider, within the bound.
No kernel may reach another device: no remote copies, remote signals or barrier semaphores. Data moves between devices by JAX's collectives and lax.ppermute only.
A program may use at most 192 MiB of HBM per device.

v0:
```python
import jax
import jax.numpy as jnp
from jax import lax
from jax.sharding import PartitionSpec as P

PRECISE = lax.Precision.HIGHEST


def conv_section(masked, expand, spatial, temporal, project):
    item_count, frames, side_cells, _, channels = masked.shape
    inner_width = expand.shape[1]
    half_side = side_cells // 2
    grown = jnp.dot(masked.reshape(-1, channels), expand, preferred_element_type=jnp.float32)
    grown = (
        jax.nn.silu(grown)
        .astype(jnp.bfloat16)
        .reshape(item_count, frames, side_cells, side_cells, inner_width)
    )
    padded = jnp.pad(grown.astype(jnp.float32), ((0, 0), (0, 0), (1, 1), (1, 1), (0, 0)))
    spatial_taps = spatial.astype(jnp.float32)
    spatial_out = jnp.zeros((item_count, frames, half_side, half_side, inner_width), jnp.float32)
    for offset_row in range(3):
        for offset_col in range(3):
            window = padded[
                :,
                :,
                offset_row : offset_row + 2 * half_side : 2,
                offset_col : offset_col + 2 * half_side : 2,
                :,
            ]
            spatial_out = spatial_out + window * spatial_taps[offset_row * 3 + offset_col]
    framed = jnp.pad(spatial_out, ((0, 0), (1, 1), (0, 0), (0, 0), (0, 0)))
    temporal_taps = temporal.astype(jnp.float32)
    summed = framed[:, 0:frames] * temporal_taps[0] + framed[:, 1 : frames + 1] * temporal_taps[1]
    summed = summed + framed[:, 2 : frames + 2] * temporal_taps[2]
    narrow = jax.nn.silu(summed).astype(jnp.bfloat16)
    projected = jnp.dot(
        narrow.reshape(-1, inner_width), project, preferred_element_type=jnp.float32
    )
    return projected.astype(jnp.bfloat16).reshape(
        item_count, frames, half_side, half_side, channels
    )


def encode_clips(params, clips, counts):
    frames = clips.shape[1]
    live_mask = jnp.arange(frames)[None, :] < counts[:, None]
    masked = jnp.where(live_mask[:, :, None, None, None], clips, jnp.zeros_like(clips))
    section_one = conv_section(masked, params[0], params[1], params[2], params[3])
    section_two = conv_section(section_one, params[4], params[5], params[6], params[7])
    cell_count = section_two.shape[2] * section_two.shape[3]
    weights = live_mask.astype(jnp.float32) / (counts.astype(jnp.float32)[:, None] * cell_count)
    return jnp.einsum("if,ifpqc->ic", weights, section_two.astype(jnp.float32), precision=PRECISE)


def user_tower(fetched, lengths, tower_up, tower_down, cotangent):
    user_count, length, width = fetched.shape
    flat_rows = fetched.reshape(-1, width)
    hidden_pre = jnp.dot(flat_rows, tower_up, preferred_element_type=jnp.float32)
    hidden_act = jax.nn.gelu(hidden_pre).astype(jnp.bfloat16)
    down_out = jnp.dot(hidden_act, tower_down, preferred_element_type=jnp.float32)
    mixed = (flat_rows.astype(jnp.float32) + down_out).reshape(user_count, length, width)
    pool_weights = (jnp.arange(length)[None, :] < lengths[:, None]).astype(jnp.float32)
    pool_weights = pool_weights / lengths.astype(jnp.float32)[:, None]
    user_vec = jnp.einsum("ul,uld->ud", pool_weights, mixed, precision=PRECISE)
    mixed_grad = (pool_weights[:, :, None] * cotangent[:, None, :]).reshape(-1, width)
    mixed_half = mixed_grad.astype(jnp.bfloat16)
    grad_down = jnp.dot(hidden_act.T, mixed_half, preferred_element_type=jnp.float32)
    act_grad = jnp.dot(mixed_half, tower_down.T, preferred_element_type=jnp.float32)
    gelu_slope = jax.jvp(jax.nn.gelu, (hidden_pre,), (jnp.ones_like(hidden_pre),))[1]
    pre_grad = (act_grad * gelu_slope).astype(jnp.bfloat16)
    grad_up = jnp.dot(flat_rows.T, pre_grad, preferred_element_type=jnp.float32)
    rows_grad = mixed_grad + jnp.dot(pre_grad, tower_up.T, preferred_element_type=jnp.float32)
    return (user_vec, grad_up, grad_down, rows_grad)


def local(
    clips,
    clip_counts,
    histories,
    lengths,
    user_cotangent,
    expand_first,
    spatial_first,
    temporal_first,
    project_first,
    expand_second,
    spatial_second,
    temporal_second,
    project_second,
    item_project,
    tower_up,
    tower_down,
):
    params = (
        expand_first,
        spatial_first,
        temporal_first,
        project_first,
        expand_second,
        spatial_second,
        temporal_second,
        project_second,
    )
    bulk_size = lax.axis_size("bulk")
    seq_size = lax.axis_size("seq")
    devices = bulk_size * seq_size
    item_count = clips.shape[0]
    user_count, length = histories.shape
    row_count = user_count * length
    capacity = 2 * row_count // devices
    width = item_project.shape[1]
    pooled, pullback = jax.vjp(lambda weights: encode_clips(weights, clips, clip_counts), params)
    item_vec = jnp.dot(pooled, item_project.astype(jnp.float32), precision=PRECISE).astype(
        jnp.bfloat16
    )
    flat_ids = histories.reshape(-1)
    owners = flat_ids // item_count
    local_ids = flat_ids - owners * item_count
    owner_hot = (owners[:, None] == jnp.arange(devices)[None, :]).astype(jnp.bfloat16)
    lower_ones = (jnp.arange(row_count)[:, None] >= jnp.arange(row_count)[None, :]).astype(
        jnp.bfloat16
    )
    running = jnp.dot(lower_ones, owner_hot, preferred_element_type=jnp.float32)
    position = jnp.take_along_axis(running, owners[:, None], axis=1)[:, 0].astype(jnp.int32) - 1
    slot_index = owners * capacity + position
    request = jnp.full((devices * capacity,), -1, jnp.int32).at[slot_index].set(local_ids)
    asked_ids = lax.all_to_all(
        request.reshape(devices, capacity), ("bulk", "seq"), split_axis=0, concat_axis=0, tiled=True
    )
    picker = asked_ids.reshape(-1)[:, None] == jnp.arange(item_count)[None, :]
    outgoing = jnp.dot(
        picker.astype(jnp.bfloat16), item_vec, preferred_element_type=jnp.float32
    ).astype(jnp.bfloat16)
    arrived = lax.all_to_all(
        outgoing.reshape(devices, capacity, width),
        ("bulk", "seq"),
        split_axis=0,
        concat_axis=0,
        tiled=True,
    )
    fetched = arrived.reshape(devices * capacity, width)[slot_index]
    user_vec, grad_up, grad_down, rows_grad = user_tower(
        fetched.reshape(user_count, length, width), lengths, tower_up, tower_down, user_cotangent
    )
    returning = jnp.zeros((devices * capacity, width), jnp.float32).at[slot_index].set(rows_grad)
    incoming = lax.all_to_all(
        returning.reshape(devices, capacity, width),
        ("bulk", "seq"),
        split_axis=0,
        concat_axis=0,
        tiled=True,
    )
    incoming = incoming.reshape(devices * capacity, width)
    item_grads = jnp.dot(picker.astype(jnp.float32).T, incoming, precision=PRECISE)
    pooled_grads = jnp.dot(item_grads, item_project.astype(jnp.float32).T, precision=PRECISE)
    grad_item = jnp.dot(pooled.T, item_grads, precision=PRECISE)
    encoder_terms = pullback(pooled_grads)[0]
    terms = tuple((term.astype(jnp.float32) for term in encoder_terms))
    every_sum = lax.psum(
        (
            terms[0],
            terms[1],
            terms[2],
            terms[3],
            terms[4],
            terms[5],
            terms[6],
            terms[7],
            grad_item,
            grad_up,
            grad_down,
        ),
        ("bulk", "seq"),
    )
    summed = every_sum[0:9]
    tower_pair = (every_sum[9], every_sum[10])
    return (
        user_vec,
        summed[0],
        summed[1],
        summed[2],
        summed[3],
        summed[4],
        summed[5],
        summed[6],
        summed[7],
        summed[8],
        tower_pair[0],
        tower_pair[1],
    )


def solution(mesh):
    placed = (
        P(("bulk", "seq"), None, None, None, None),
        P(("bulk", "seq")),
        P(("bulk", "seq"), None),
        P(("bulk", "seq")),
        P(("bulk", "seq"), None),
        P(),
        P(),
        P(),
        P(),
        P(),
        P(),
        P(),
        P(),
        P(),
        P(),
        P(),
    )
    return jax.shard_map(
        local,
        mesh=mesh,
        in_specs=placed,
        out_specs=(P(("bulk", "seq"), None), P(), P(), P(), P(), P(), P(), P(), P(), P(), P(), P()),
        check_vma=False,
    )
```

profile of v0, /device:TPU:1, one launch (start us, length us, event | category | flops | bytes accessed | tf_op | source)
XLA Modules:
  0.0 475.5 jit_solution(674538909002775898)
XLA Ops:
  9.9 1.9 gather_fusion.1
  14.0 12.7 %all-to-all-start = ((s32[128,1,4]{2,1,0:T(1,128)}), s32[128,1,4]{2,1,0:T(1,128)}, u32[]{:S(2)}, u32[]{:S(2)}) async-start(s32[128,1,4]{2,1,0:T(1,128)} %bitcast.6), calls=%async_computation | async-start | bytes 131072 | tf_op jit(solution)/shard_map/all_to_all | solution.py:128
  29.2 1.8 broadcast_select_fusion
  31.7 3.5 multiply_convert_fusion
  35.2 2.8 copy.77
  37.9 2.1 convert_element_type.204
  40.0 2.8 copy.78
  45.1 2.7 copy-done.2
  51.1 2.3 fusion.44
  54.7 2.9 reshape.583
  57.6 2.6 fusion.74
  69.2 10.2 %all-to-all-start.1 = ((bf16[128,4,512]{2,1,0:T(4,128)(2,1)}), bf16[128,4,512]{2,1,0:T(4,128)(2,1)}, u32[]{:S(2)}, u32[]{:S(2)}) async-start(bf16[128,4,512]{2,1,0:T(4,128)(2,1)} %reshape.576), calls=%async_computation.1 | async-start | bytes 1048576 | tf_op jit(solution)/shard_map/all_to_all | solution.py:135
  81.8 10.9 %all-to-all-done.1 = bf16[128,4,512]{2,1,0:T(4,128)(2,1)} async-done(((bf16[128,4,512]{2,1,0:T(4,128)(2,1)}), bf16[128,4,512]{2,1,0:T(4,128)(2,1)}, u32[]{:S(2)}, u32[]{:S(2)}) %all-to-all-start.1) | async-done | bytes 524320 | tf_op jit(solution)/shard_map/all_to_all | solution.py:135
  93.8 1.8 gather_fusion
  98.1 2.0 fusion.13
  102.2 3.0 scatter_custom_fusion.1
  105.2 2.5 reshape.579
  107.7 5.7 %all-to-all-start.2 = ((f32[128,4,512]{2,1,0:T(4,128)}), f32[128,4,512]{2,1,0:T(4,128)}, u32[]{:S(2)}, u32[]{:S(2)}) async-start(f32[128,4,512]{2,1,0:T(4,128)} %reshape.579), calls=%async_computation.2 | async-start | bytes 2097152 | tf_op jit(solution)/shard_map/all_to_all | solution.py:147
  113.5 2.8 fusion.83
  116.3 1.9 fusion.50
  118.2 14.1 %all-to-all-done.2 = f32[128,4,512]{2,1,0:T(4,128)} async-done(((f32[128,4,512]{2,1,0:T(4,128)}), f32[128,4,512]{2,1,0:T(4,128)}, u32[]{:S(2)}, u32[]{:S(2)}) %all-to-all-start.2) | async-done | bytes 1048608 | tf_op jit(solution)/shard_map/all_to_all | solution.py:147
  142.2 1.8 copy.90
  144.0 2.0 reshape.585
  156.8 2.4 multiply_reduce_fusion.2
  159.7 5.6 %multiply_reduce_fusion.11 = (f32[432]{0:T(512)S(1)}, f32[432]{0:T(512)S(1)}, f32[432]{0:T(512)S(1)}, f32[432]{0:T(512)S(1)}, f32[432]{0:T(512)S(1)}, /*index=5*...) fusion(f32[32,4,6,6,432]{4,0,3,2,1:T(8,128)} %copy-done.2, ...), kind=kLoop, calls=%fused_computation.82 | loop fusion | flops 4419792 | bytes 11517120 | tf_op jit(solution)/shard_map/transpose(jvp())/reduce_sum | solution.py:31
  165.3 3.2 broadcast_multiply_fusion.4
  168.5 12.5 %pad.212 = f32[32,4,6,6,432]{4,0,3,2,1:T(8,128)} pad(f32[32,4,2,2,432]{4,0,3,2,1:T(8,128)} %get-tuple-element.60, f32[]{:T(128)} %constant.69.clone.1), padding=0_0_0x0_0_0x2_1_1x2_1_1x0_0_0 | pad | bytes 8847364 | tf_op jit(solution)/shard_map/transpose(jvp())/pad | solution.py:24
  181.0 8.7 %pad.213 = f32[32,4,6,6,432]{4,0,3,2,1:T(8,128)} pad(f32[32,4,2,2,432]{4,0,3,2,1:T(8,128)S(1)} %copy-done.12, f32[]{:T(128)} %constant.69.clone.1), padding=0_0_0x0_0_0x2_1_1x1_2_1x0_0_0 | pad | bytes 8847364 | tf_op jit(solution)/shard_map/transpose(jvp())/pad | solution.py:24
  189.8 12.4 %pad.214 = f32[32,4,6,6,432]{4,0,3,2,1:T(8,128)} pad(f32[32,4,2,2,432]{4,0,3,2,1:T(8,128)} %get-tuple-element.59, f32[]{:T(128)} %constant.69.clone.1), padding=0_0_0x0_0_0x2_1_1x0_3_1x0_0_0 | pad | bytes 8847364 | tf_op jit(solution)/shard_map/transpose(jvp())/pad | solution.py:24
  202.2 8.7 %pad.215 = f32[32,4,6,6,432]{4,0,3,2,1:T(8,128)} pad(f32[32,4,2,2,432]{4,0,3,2,1:T(8,128)S(1)} %copy-done.11, f32[]{:T(128)} %constant.69.clone.1), padding=0_0_0x0_0_0x1_2_1x2_1_1x0_0_0 | pad | bytes 8847364 | tf_op jit(solution)/shard_map/transpose(jvp())/pad | solution.py:24
  211.0 11.5 %pad.419 = f32[32,4,5,5,432]{4,0,3,2,1:T(8,128)} pad(f32[32,4,2,2,432]{4,0,3,2,1:T(8,128)} %get-tuple-element.61, f32[]{:T(128)} %constant.69.clone.1), padding=0_0_0x0_0_0x0_2_1x0_2_1x0_0_0 | pad | bytes 6414340
  222.5 7.4 %pad.420 = f32[32,4,5,4,432]{4,0,3,2,1:T(8,128)} pad(f32[32,4,2,2,432]{4,0,3,2,1:T(8,128)S(1)} %copy-done.6, f32[]{:T(128)} %constant.69.clone.1), padding=0_0_0x0_0_0x0_2_1x0_1_1x0_0_0 | pad | bytes 5308420
  229.9 7.4 %pad.421 = f32[32,4,5,4,432]{4,0,3,2,1:T(8,128)} pad(f32[32,4,2,2,432]{4,0,3,2,1:T(8,128)S(1)} %get-tuple-element.55, f32[]{:T(128)} %constant.69.clone.1), padding=0_0_0x0_0_0x0_2_1x1_0_1x0_0_0 | pad | bytes 5308420
  237.3 7.4 %pad.422 = f32[32,4,4,5,432]{4,0,3,2,1:T(8,128)} pad(f32[32,4,2,2,432]{4,0,3,2,1:T(8,128)S(1)} %get-tuple-element.56, f32[]{:T(128)} %constant.69.clone.1), padding=0_0_0x0_0_0x0_1_1x0_2_1x0_0_0 | pad | bytes 5308420
  244.7 7.2 %pad.262 = f32[32,4,4,4,432]{4,0,3,2,1:T(8,128)} pad(f32[32,4,2,2,432]{4,0,3,2,1:T(8,128)S(1)} %copy-done.10, f32[]{:T(128)} %constant.69.clone.1), padding=0_0_0x0_0_0x0_1_1x0_1_1x0_0_0 | pad | bytes 4423684 | tf_op jit(solution)/shard_map/transpose(jvp(jit(_pad)))/pad | solution.py:19
  251.9 13.9 %add_add_fusion = f32[32,4,6,6,432]{4,0,3,2,1:T(8,128)S(1)} fusion(f32[32,4,6,6,432]{4,0,3,2,1:T(8,128)} %pad.215, f32[32,4,6,6,432]{4,0,3,2,1:T(8,128)} %pad.214, f32[32,4,6,6,432]{4,0,3,2,1:T(8,128)} %pad.212, f32[32,4,6,6,432]{4,0,3,2,1:T(8,128)} %pad.213), kind=kLoop, calls=%fused_computation.4 | loop fusion | flops 5971968 | bytes 39813120 | tf_op jit(solution)/shard_map/transpose(jvp())/add_any | solution.py:24
  266.5 7.7 %fusion.11 = f32[32,4,4,4,432]{4,0,3,2,1:T(8,128)} fusion(f32[32,4,4,4,432]{4,0,3,2,1:T(8,128)} %pad.262, f32[32,4,6,6,432]{4,0,3,2,1:T(8,128)S(1)} %add_add_fusion, f32[32,4,4,5,432]{4,0,3,2,1:T(8,128)S(1)} %copy-done.3, f32[32,4,5,4,432]{4,0,3,2,1:T(8,128)} %pad.421, f32[32,4,5,4,432]{4,0,3,2,1:T(8,128)} %pad.420, f32[32,4,5,5,432]{4,0,3,2,1:T(8,128)S(1)} %bitcast.116), kind=kLoop, calls=%fused_computation.21 | loop fusion | flops 6193152 | bytes 24772608 | tf_op jit(solution)/shard_map/transpose(jvp())/convert_element_type | solution.py:16
  274.2 6.8 %copy.96 = f32[32,4,4,4,432]{4,3,2,1,0:T(4,128)} copy(f32[32,4,4,4,432]{4,0,3,2,1:T(8,128)} %fusion.11) | data formatting | bytes 7077888 | tf_op jit(solution)/shard_map/transpose(jvp())/convert_element_type | solution.py:16
  281.0 5.4 %reshape.587 = f32[2048,432]{1,0:T(8,128)} reshape(f32[32,4,4,4,432]{4,3,2,1,0:T(4,128)} %copy.96) | data formatting | bytes 7077888 | tf_op jit(solution)/shard_map/transpose(jvp())/convert_element_type | solution.py:16
  286.4 5.6 %copy.97 = f32[2048,432]{0,1:T(8,128)} copy(f32[2048,432]{1,0:T(8,128)} %reshape.587) | data formatting | bytes 7077888 | tf_op jit(solution)/shard_map/transpose(jvp())/convert_element_type | solution.py:16
  292.1 5.4 %fusion.22 = f32[192,432]{1,0:T(8,128)} fusion(bf16[2048,192]{1,0:T(8,128)(2,1)S(1)} %copy-done.28, f32[2048,432]{0,1:T(8,128)} %get-tuple-element.106, f32[2048,432]{0,1:T(8,128)} %copy.97), kind=kOutput, calls=%fused_computation.46 | convolution fusion | flops 347867136 | bytes 8196096 | tf_op jit(solution)/shard_map/transpose(jvp())/dot_general | solution.py:13
  300.8 64.8 %all-reduce.51 = (f32[9,432]{1,0:T(8,128)}, f32[3,432]{1,0:T(4,128)}, f32[9,432]{1,0:T(8,128)}, f32[3,432]{1,0:T(4,128)}) all-reduce(f32[9,432]{1,0:T(8,128)S(1)} %fusion.63, f32[3,432]{1,0:T(4,128)S(1)} %fusion.64, f32[9,432]{1,0:T(8,128)S(1)} %fusion.62, f32[3,432]{1,0:T(4,128)S(1)} %fusion.65), channel_id=1, replica_groups=mesh['bulk'=16,'seq'=8] {'bulk','seq'}, use_global_device_ids=true, to_apply=%region_12.13 | all-reduce | flops 10368 | bytes 82944 | tf_op jit(solution)/shard_map/psum | solution.py:160
  365.6 89.2 %all-reduce.55.cloned.1.call-done = (f32[192,432]{1,0:T(8,128)}, f32[432,192]{0,1:T(8,128)}, f32[192,432]{1,0:T(8,128)}, f32[432,192]{0,1:T(8,128)}, f32[192,512...) async-done(((f32[192,432]{1,0:T(8,128)}, f32[432,192]{0,1:T(8,128)}, f32[192,432]{1,0:T(8,128)}, f32[432,192]{0,1:T(8,128)}, f32[192,512]{1,0:T(8,128)}, ...) | async-done | bytes 5914640 | tf_op jit(solution)/shard_map/psum | solution.py:160
  454.9 1.9 copy.139
  456.8 1.8 copy.140
  458.6 1.8 copy.141
  462.1 1.9 copy.143
  464.0 3.2 copy.144
  (235 shorter events, 59.3 us)
Async XLA Ops:
  7.2 88.5 %copy-start = (bf16[512,1024]{1,0:T(8,128)(2,1)S(1)}, bf16[512,1024]{1,0:T(8,128)(2,1)}, u32[]{:S(2)}) copy-start(bf16[512,1024]{1,0:T(8,128)(2,1)} %param.30) | copy-start | bytes 3145732
  7.2 24.5 %copy-start.71 = (bf16[192,432]{1,0:T(8,128)(2,1)S(1)}, bf16[192,432]{1,0:T(8,128)(2,1)}, u32[]{:S(2)}) copy-start(bf16[192,432]{1,0:T(8,128)(2,1)} %param.21) | copy-start | bytes 497668
  11.9 16.2 %copy-start.67 = (s32[256,1]{0,1:T(1,128)}, s32[256,1]{0,1:T(1,128)S(1)}, u32[]{:S(2)}) copy-start(s32[256,1]{0,1:T(1,128)S(1)} %compare_select_fusion) | copy-start | bytes 3076
  14.0 51.6 %all-to-all-start = ((s32[128,1,4]{2,1,0:T(1,128)}), s32[128,1,4]{2,1,0:T(1,128)}, u32[]{:S(2)}, u32[]{:S(2)}) async-start(s32[128,1,4]{2,1,0:T(1,128)} %bitcast.6), calls=%async_computation | async-start | bytes 131072 | tf_op jit(solution)/shard_map/all_to_all | solution.py:128
  29.1 15.0 %copy-start.39 = (f32[1,432]{1,0:T(1,128)}, f32[1,432]{1,0:T(1,128)S(1)}, u32[]{:S(2)}) copy-start(f32[1,432]{1,0:T(1,128)S(1)} %get-tuple-element.90) | copy-start | bytes 5188
  29.1 15.0 %copy-start.41 = (f32[1,432]{1,0:T(1,128)}, f32[1,432]{1,0:T(1,128)S(1)}, u32[]{:S(2)}) copy-start(f32[1,432]{1,0:T(1,128)S(1)} %get-tuple-element.91) | copy-start | bytes 5188
  29.1 15.0 %copy-start.43 = (f32[1,432]{1,0:T(1,128)}, f32[1,432]{1,0:T(1,128)S(1)}, u32[]{:S(2)}) copy-start(f32[1,432]{1,0:T(1,128)S(1)} %get-tuple-element.92) | copy-start | bytes 5188
  29.1 15.0 %copy-start.45 = (f32[1,432]{1,0:T(1,128)}, f32[1,432]{1,0:T(1,128)S(1)}, u32[]{:S(2)}) copy-start(f32[1,432]{1,0:T(1,128)S(1)} %get-tuple-element.93) | copy-start | bytes 5188
  29.1 15.0 %copy-start.47 = (f32[1,432]{1,0:T(1,128)}, f32[1,432]{1,0:T(1,128)S(1)}, u32[]{:S(2)}) copy-start(f32[1,432]{1,0:T(1,128)S(1)} %get-tuple-element.94) | copy-start | bytes 5188
  29.1 15.0 %copy-start.49 = (f32[1,432]{1,0:T(1,128)}, f32[1,432]{1,0:T(1,128)S(1)}, u32[]{:S(2)}) copy-start(f32[1,432]{1,0:T(1,128)S(1)} %get-tuple-element.95) | copy-start | bytes 5188
  29.1 15.0 %copy-start.51 = (f32[1,432]{1,0:T(1,128)}, f32[1,432]{1,0:T(1,128)S(1)}, u32[]{:S(2)}) copy-start(f32[1,432]{1,0:T(1,128)S(1)} %get-tuple-element.96) | copy-start | bytes 5188
  29.1 15.0 %copy-start.53 = (f32[1,432]{1,0:T(1,128)}, f32[1,432]{1,0:T(1,128)S(1)}, u32[]{:S(2)}) copy-start(f32[1,432]{1,0:T(1,128)S(1)} %get-tuple-element.97) | copy-start | bytes 5188
  29.2 15.0 %copy-start.55 = (f32[1,432]{1,0:T(1,128)}, f32[1,432]{1,0:T(1,128)S(1)}, u32[]{:S(2)}) copy-start(f32[1,432]{1,0:T(1,128)S(1)} %get-tuple-element.98) | copy-start | bytes 5188
  50.1 7.5 %copy-start.4 = (bf16[512,432]{1,0:T(8,128)(2,1)}, bf16[512,432]{1,0:T(8,128)(2,1)S(1)}, u32[]{:S(2)}) copy-start(bf16[512,432]{1,0:T(8,128)(2,1)S(1)} %reshape.574) | copy-start | bytes 1327108
  51.1 9.1 %copy-start.36 = (bf16[9,432]{1,0:T(8,128)(2,1)S(1)}, bf16[9,432]{1,0:T(8,128)(2,1)}, u32[]{:S(2)}) copy-start(bf16[9,432]{1,0:T(8,128)(2,1)} %param.26) | copy-start | bytes 23332
  51.1 9.2 %copy-start.58 = (bf16[3,432]{1,0:T(4,128)(2,1)S(1)}, bf16[3,432]{1,0:T(4,128)(2,1)}, u32[]{:S(2)}) copy-start(bf16[3,432]{1,0:T(4,128)(2,1)} %param.27) | copy-start | bytes 7780
  54.7 9.5 %copy-start.68 = (s32[32]{0:T(128)S(1)}, s32[32]{0:T(128)}, u32[]{:S(2)}) copy-start(s32[32]{0:T(128)} %param.17) | copy-start | bytes 388
  57.6 21.8 %copy-start.69 = (s32[4]{0:T(128)S(1)}, s32[4]{0:T(128)}, u32[]{:S(2)}) copy-start(s32[4]{0:T(128)} %param.19) | copy-start | bytes 52
  60.2 19.9 %copy-start.15 = (f32[32,4,1,1,432]{4,3,2,1,0:T(1,128)}, f32[32,4,1,1,432]{4,3,2,1,0:T(1,128)S(1)}, u32[]{:S(2)}) copy-start(f32[32,4,1,1,432]{4,3,2,1,0:T(1,128)S(1)} %get-tuple-element.65) | copy-start | bytes 663556
  60.3 19.9 %copy-start.17 = (f32[32,4,1,1,432]{4,3,2,1,0:T(1,128)}, f32[32,4,1,1,432]{4,3,2,1,0:T(1,128)S(1)}, u32[]{:S(2)}) copy-start(f32[32,4,1,1,432]{4,3,2,1,0:T(1,128)S(1)} %get-tuple-element.66) | copy-start | bytes 663556
  69.2 23.5 %all-to-all-start.1 = ((bf16[128,4,512]{2,1,0:T(4,128)(2,1)}), bf16[128,4,512]{2,1,0:T(4,128)(2,1)}, u32[]{:S(2)}, u32[]{:S(2)}) async-start(bf16[128,4,512]{2,1,0:T(4,128)(2,1)} %reshape.576), calls=%async_computation.1 | async-start | bytes 1048576 | tf_op jit(solution)/shard_map/all_to_all | solution.py:135
  100.9 12.5 %copy-start.13 = (bf16[256,512]{1,0:T(8,128)(2,1)S(1)}, bf16[256,512]{1,0:T(8,128)(2,1)}, u32[]{:S(2)}) copy-start(bf16[256,512]{1,0:T(8,128)(2,1)} %gather_fusion) | copy-start | bytes 786436
  102.2 14.1 %copy-start.8 = (f32[256,1024]{1,0:T(8,128)S(1)}, f32[256,1024]{1,0:T(8,128)}, u32[]{:S(2)}) copy-start(f32[256,1024]{1,0:T(8,128)} %copy-done.7) | copy-start | bytes 3145732
  107.7 24.6 %all-to-all-start.2 = ((f32[128,4,512]{2,1,0:T(4,128)}), f32[128,4,512]{2,1,0:T(4,128)}, u32[]{:S(2)}, u32[]{:S(2)}) async-start(f32[128,4,512]{2,1,0:T(4,128)} %reshape.579), calls=%async_computation.2 | async-start | bytes 2097152 | tf_op jit(solution)/shard_map/all_to_all | solution.py:147
  113.4 341.5 %all-reduce.55.cloned.1.call-start = ((), (), s32[]{:S(2)}) async-start(), calls=%async_computation.3 | async-start | bytes 12320768 | tf_op jit(solution)/shard_map/psum | solution.py:160
  118.2 22.1 %copy-start.16 = (f32[32,4,1,1,432]{4,3,2,1,0:T(1,128)S(1)}, f32[32,4,1,1,432]{4,3,2,1,0:T(1,128)}, u32[]{:S(2)}) copy-start(f32[32,4,1,1,432]{4,3,2,1,0:T(1,128)} %copy-done.15) | copy-start | bytes 663556
  118.2 22.1 %copy-start.18 = (f32[32,4,1,1,432]{4,3,2,1,0:T(1,128)S(1)}, f32[32,4,1,1,432]{4,3,2,1,0:T(1,128)}, u32[]{:S(2)}) copy-start(f32[32,4,1,1,432]{4,3,2,1,0:T(1,128)} %copy-done.17) | copy-start | bytes 663556
  118.2 22.1 %copy-start.20 = (f32[32,4,1,1,432]{4,3,2,1,0:T(1,128)S(1)}, f32[32,4,1,1,432]{4,3,2,1,0:T(1,128)}, u32[]{:S(2)}) copy-start(f32[32,4,1,1,432]{4,3,2,1,0:T(1,128)} %copy-done.19) | copy-start | bytes 663556
  118.2 22.2 %copy-start.22 = (f32[32,4,1,1,432]{4,3,2,1,0:T(1,128)S(1)}, f32[32,4,1,1,432]{4,3,2,1,0:T(1,128)}, u32[]{:S(2)}) copy-start(f32[32,4,1,1,432]{4,3,2,1,0:T(1,128)} %copy-done.21) | copy-start | bytes 663556
  133.9 7.4 %copy-start.38 = (f32[1,432]{1,0:T(1,128)S(1)}, f32[1,432]{1,0:T(1,128)}, u32[]{:S(2)}) copy-start(f32[1,432]{1,0:T(1,128)} %copy-done.37) | copy-start | bytes 5188
  144.0 6.4 %copy-start.5 = (bf16[512,432]{1,0:T(8,128)(2,1)S(1)}, bf16[512,432]{1,0:T(8,128)(2,1)}, u32[]{:S(2)}) copy-start(bf16[512,432]{1,0:T(8,128)(2,1)} %copy-done.4) | copy-start | bytes 1327108
  146.3 6.2 %copy-start.33 = (f32[32,512]{1,0:T(8,128)S(1)}, f32[32,512]{1,0:T(8,128)}, u32[]{:S(2)}) copy-start(f32[32,512]{1,0:T(8,128)} %copy-done.32) | copy-start | bytes 196612
  146.3 7.4 %copy-start.26 = (bf16[32,4,1,1,432]{4,0,3,2,1:T(8,128)(2,1)S(1)}, bf16[32,4,1,1,432]{4,0,3,2,1:T(8,128)(2,1)}, u32[]{:S(2)}) copy-start(bf16[32,4,1,1,432]{4,0,3,2,1:T(8,128)(2,1)} %copy-done.25) | copy-start | bytes 331780
  146.4 7.4 %copy-start.35 = (bf16[32,4,192]{2,1,0:T(4,128)(2,1)S(1)}, bf16[32,4,192]{2,1,0:T(4,128)(2,1)}, u32[]{:S(2)}) copy-start(bf16[32,4,192]{2,1,0:T(4,128)(2,1)} %copy-done.34) | copy-start | bytes 147460
  159.6 5.7 %copy-start.40 = (f32[1,432]{1,0:T(1,128)S(1)}, f32[1,432]{1,0:T(1,128)}, u32[]{:S(2)}) copy-start(f32[1,432]{1,0:T(1,128)} %copy-done.39) | copy-start | bytes 5188
  159.6 5.7 %copy-start.42 = (f32[1,432]{1,0:T(1,128)S(1)}, f32[1,432]{1,0:T(1,128)}, u32[]{:S(2)}) copy-start(f32[1,432]{1,0:T(1,128)} %copy-done.41) | copy-start | bytes 5188
  159.6 5.7 %copy-start.44 = (f32[1,432]{1,0:T(1,128)S(1)}, f32[1,432]{1,0:T(1,128)}, u32[]{:S(2)}) copy-start(f32[1,432]{1,0:T(1,128)} %copy-done.43) | copy-start | bytes 5188
  159.6 5.7 %copy-start.46 = (f32[1,432]{1,0:T(1,128)S(1)}, f32[1,432]{1,0:T(1,128)}, u32[]{:S(2)}) copy-start(f32[1,432]{1,0:T(1,128)} %copy-done.45) | copy-start | bytes 5188
  159.6 5.7 %copy-start.48 = (f32[1,432]{1,0:T(1,128)S(1)}, f32[1,432]{1,0:T(1,128)}, u32[]{:S(2)}) copy-start(f32[1,432]{1,0:T(1,128)} %copy-done.47) | copy-start | bytes 5188
  168.5 12.5 %copy-start.12 = (f32[32,4,2,2,432]{4,0,3,2,1:T(8,128)S(1)}, f32[32,4,2,2,432]{4,0,3,2,1:T(8,128)}, u32[]{:S(2)}) copy-start(f32[32,4,2,2,432]{4,0,3,2,1:T(8,128)} %get-tuple-element.53) | copy-start | bytes 2654212
  189.8 12.4 %copy-start.11 = (f32[32,4,2,2,432]{4,0,3,2,1:T(8,128)S(1)}, f32[32,4,2,2,432]{4,0,3,2,1:T(8,128)}, u32[]{:S(2)}) copy-start(f32[32,4,2,2,432]{4,0,3,2,1:T(8,128)} %get-tuple-element.58) | copy-start | bytes 2654212
  211.0 11.5 %copy-start.6 = (f32[32,4,2,2,432]{4,0,3,2,1:T(8,128)S(1)}, f32[32,4,2,2,432]{4,0,3,2,1:T(8,128)}, u32[]{:S(2)}) copy-start(f32[32,4,2,2,432]{4,0,3,2,1:T(8,128)} %get-tuple-element.54) | copy-start | bytes 2654212
  237.3 7.4 %copy-start.10 = (f32[32,4,2,2,432]{4,0,3,2,1:T(8,128)S(1)}, f32[32,4,2,2,432]{4,0,3,2,1:T(8,128)}, u32[]{:S(2)}) copy-start(f32[32,4,2,2,432]{4,0,3,2,1:T(8,128)} %get-tuple-element.57) | copy-start | bytes 2654212
  244.7 21.1 %slice-start = ((s8[6553600]{0:T(1024)(128)(4,1)}), s8[2359296]{0:T(1024)(128)(4,1)S(1)}, s32[]{:S(2)}) async-start(s8[6553600]{0:T(1024)(128)(4,1)} %bitcast.115), calls=%async_computation.4 | async-start | bytes 4718592
  251.9 13.9 %slice-start.1 = ((s8[6553600]{0:T(1024)(128)(4,1)}), s8[4194304]{0:T(1024)(128)(4,1)S(1)}, s32[]{:S(2)}) async-start(s8[6553600]{0:T(1024)(128)(4,1)} %bitcast.115), calls=%async_computation.5 | async-start | bytes 8388608
  251.9 14.6 %copy-start.3 = (f32[32,4,4,5,432]{4,0,3,2,1:T(8,128)S(1)}, f32[32,4,4,5,432]{4,0,3,2,1:T(8,128)}, u32[]{:S(2)}) copy-start(f32[32,4,4,5,432]{4,0,3,2,1:T(8,128)} %pad.422) | copy-start | bytes 13271044
  454.9 12.2 %copy-start.23 = (f32[1024,512]{1,0:T(8,128)S(1)}, f32[1024,512]{1,0:T(8,128)}, u32[]{:S(2)}) copy-start(f32[1024,512]{1,0:T(8,128)} %get-tuple-element.122) | copy-start | bytes 6291460
  462.1 6.3 %copy-start.1 = (bf16[512,1024]{1,0:T(8,128)(2,1)S(1)}, bf16[512,1024]{1,0:T(8,128)(2,1)}, u32[]{:S(2)}) copy-start(bf16[512,1024]{1,0:T(8,128)(2,1)} %param.30) | copy-start | bytes 3145732
  (30 other events, 83.5 us)
Sparse Core Ops, SparseCore 0:
  297.7 157.1 all-reduce.54
where the time goes:
time: 481 us; the launch traced here: 476 us
  local copies, waits for them, and re-layouts  167 us (35%)
  waiting for transfers between devices  114 us (24%)
  blocking collectives  64.8 us (13%)
  other arithmetic  50.4 us (10%)
  matrix products  34.7 us (7%)
  starting transfers between devices  28.6 us (6%)
  between operations  15.5 us (3%)
    psum x1, waiting for transfers between devices, local(): lax.psum((terms[0], terms[1], terms[2], terms[3], terms[4], terms[5], ter...  89.2 us
    psum x1, blocking collectives, local(): lax.psum((terms[0], terms[1], terms[2], terms[3], terms[4], terms[5], ter...  64.8 us
    unnamed x160, local copies, waits for them, and re-layouts  57.2 us
    pad x4, local copies, waits for them, and re-layouts, conv_section(): padded[:, :, offset_row:offset_row + 2 * half_side:2, offset_col:offset_c...  42.4 us
    convert_element_type x7, local copies, waits for them, and re-layouts, conv_section(): grown = jax.nn.silu(grown).astype(jnp.bfloat16).reshape(item_count, frame...  24.8 us
    add_any x2, other arithmetic, conv_section(): padded[:, :, offset_row:offset_row + 2 * half_side:2, offset_col:offset_c...  14.4 us
    all_to_all x1, waiting for transfers between devices, local(): lax.all_to_all(returning.reshape(devices, capacity, width), ('bulk', 'seq...  14.1 us
    dot_general x5, matrix products, conv_section(): jnp.dot(masked.reshape(-1, channels), expand, preferred_element_type=jnp....  13.4 us
  transfers between devices with their start and end apart: 4, of which 3 were waited for; matrix products, arithmetic and copies ran while one was open for 9% of the time, Pallas kernels for 0%

commit v1 on v0

v1 whole, which is shorter than its diff:
```python
import jax
import jax.numpy as jnp
from jax import lax
from jax.experimental import pallas as pl
from jax.experimental.pallas import tpu as pltpu
from jax.sharding import PartitionSpec as P

BF = jnp.bfloat16
F32 = jnp.float32
AXES = ("bulk", "seq")
C, E, D, FH = 192, 432, 512, 1024
FRAMES, SIDE, ITEMS_HERE, USERS_HERE, LENGTH = 4, 4, 32, 4, 64
DEVICES, CHIPS, CAPACITY = 128, 64, 4
ROWS = USERS_HERE * LENGTH
CELLS = SIDE * SIDE
HALF = 2
LINKS_FIRST = [
    (HALF * p + q, SIDE * (2 * p + a - 1) + 2 * q + b - 1, 3 * a + b)
    for p in range(HALF)
    for q in range(HALF)
    for a in range(3)
    for b in range(3)
    if 0 <= 2 * p + a - 1 < SIDE and 0 <= 2 * q + b - 1 < SIDE
]
LINKS_SECOND = [(0, 4), (1, 5), (2, 7), (3, 8)]


def dot_nn(a, b):
    return lax.dot_general(a, b, (((1,), (0,)), ((), ())), preferred_element_type=F32)


def dot_nt(a, b):
    return lax.dot_general(a, b, (((1,), (1,)), ((), ())), preferred_element_type=F32)


def dot_tn(a, b):
    return lax.dot_general(a, b, (((0,), (0,)), ((), ())), preferred_element_type=F32)


def silu_and_slope(v):
    gate = 0.5 * jnp.tanh(0.5 * v) + 0.5
    value = v * gate
    return value, gate + value - value * gate


def conv_forward(
    x, counts, e1, s1, t1, p1, e2, s2, t2, p2,
    block, g1, d1, sp1, n1, h1, o1, g2, d2, sp2, n2, h2,
    framed1, framed2,
):
    zero4 = jnp.zeros((HALF * HALF, ITEMS_HERE, E), F32)
    framed1[0] = zero4
    framed1[FRAMES + 1] = zero4
    zero1 = jnp.zeros((ITEMS_HERE, E), F32)
    framed2[0] = zero1
    framed2[FRAMES + 1] = zero1
    taps1 = s1[...].astype(F32)
    taps2 = s2[...].astype(F32)
    frame1 = t1[...].astype(F32)
    frame2 = t2[...].astype(F32)

    def grow(f, _):
        live = f < counts[...]
        x_f = x[pl.ds(f * CELLS, CELLS)]
        x_f = jnp.where(live[None], x_f, jnp.zeros_like(x_f))
        pre = dot_nn(x_f.reshape(CELLS * ITEMS_HERE, C), e1[...])
        value, slope = silu_and_slope(pre)
        value = value.astype(BF).reshape(CELLS, ITEMS_HERE, E)
        g1[pl.ds(f * CELLS, CELLS)] = value
        d1[pl.ds(f * CELLS, CELLS)] = slope.astype(BF).reshape(CELLS, ITEMS_HERE, E)
        outs = [jnp.zeros((ITEMS_HERE, E), F32)] * 4
        for out_cell, in_cell, tap in LINKS_FIRST:
            outs[out_cell] = outs[out_cell] + value[in_cell].astype(F32) * taps1[tap]
        for out_cell in range(4):
            framed1[f + 1, out_cell] = outs[out_cell]
            sp1[f, out_cell] = outs[out_cell].astype(BF)
        return 0

    lax.fori_loop(0, FRAMES, grow, 0)

    def narrow_first(f, _):
        summed = framed1[f] * frame1[0] + framed1[f + 1] * frame1[1] + framed1[f + 2] * frame1[2]
        value, slope = silu_and_slope(summed)
        n1[pl.ds(f * 4, 4)] = value.astype(BF)
        h1[pl.ds(f * 4, 4)] = slope.astype(BF)
        return 0

    lax.fori_loop(0, FRAMES, narrow_first, 0)
    first = dot_nn(n1[...].reshape(FRAMES * 4 * ITEMS_HERE, E), p1[...]).astype(BF)
    o1[...] = first
    value, slope = silu_and_slope(dot_nn(first, e2[...]))
    value = value.astype(BF).reshape(FRAMES * 4, ITEMS_HERE, E)
    g2[...] = value
    d2[...] = slope.astype(BF).reshape(FRAMES * 4, ITEMS_HERE, E)
    for f in range(FRAMES):
        total = jnp.zeros((ITEMS_HERE, E), F32)
        for cell, tap in LINKS_SECOND:
            total = total + value[f * 4 + cell].astype(F32) * taps2[tap]
        framed2[f + 1] = total
        sp2[f] = total.astype(BF)
    for f in range(FRAMES):
        summed = framed2[f] * frame2[0] + framed2[f + 1] * frame2[1] + framed2[f + 2] * frame2[2]
        value, slope = silu_and_slope(summed)
        n2[f] = value.astype(BF)
        h2[f] = slope.astype(BF)
    second = dot_nn(n2[...].reshape(FRAMES * ITEMS_HERE, E), p2[...]).astype(BF)
    pooled = jnp.zeros((ITEMS_HERE, C), F32)
    for f in range(FRAMES):
        live = (f < counts[...]).astype(F32)
        pooled = pooled + live * second[f * ITEMS_HERE : (f + 1) * ITEMS_HERE].astype(F32)
    pooled = (pooled / counts[...].astype(F32)).astype(BF)
    block[0:32] = pooled[:, 0:128]
    block[32:64] = jnp.concatenate([pooled[:, 128:192], jnp.zeros((ITEMS_HERE, 64), BF)], axis=1)


def tower(
    core, lengths, own, other, ids_col, ids_row, cot, project, up, down,
    sent, factors, user_vec,
):
    ids = ids_col[...]
    owner = ids // ITEMS_HERE
    within = ids - owner * ITEMS_HERE
    chip = owner // 2
    place = chip * ITEMS_HERE + within
    mine = (owner - chip * 2) == core[0]
    lanes = lax.broadcasted_iota(jnp.int32, (ROWS, CHIPS * ITEMS_HERE), 1)
    pick_own = (lanes == jnp.where(mine, place, -1)).astype(F32).astype(BF)
    pick_other = (lanes == jnp.where(mine, -1, place)).astype(F32).astype(BF)

    def rows_of(ref, at):
        return ref[:, at : at + 32, :].reshape(CHIPS * ITEMS_HERE, 128)

    picked_low = (dot_nn(pick_own, rows_of(own, 0)) + dot_nn(pick_other, rows_of(other, 0))).astype(BF)
    picked_high = (dot_nn(pick_own, rows_of(own, 32)) + dot_nn(pick_other, rows_of(other, 32))).astype(BF)
    fetched = dot_nn(picked_low, project[0:128]) + dot_nn(picked_high[:, 0:64], project[128:192])
    fetched = fetched.astype(BF)
    pre = dot_nn(fetched, up[...])
    scale = 0.7978845608028654
    square = pre * pre
    bent = jnp.tanh(scale * pre * (1.0 + 0.044715 * square))
    gate = 0.5 * (1.0 + bent)
    act = (pre * gate).astype(BF)
    slope = gate + 0.5 * pre * (1.0 - bent * bent) * (scale * (1.0 + 3 * 0.044715 * square))

    user = lax.broadcasted_iota(jnp.int32, (8, 1), 0)
    length = jnp.ones((8, 1), jnp.int32)
    for u in range(USERS_HERE):
        length = jnp.where(user == u, lengths[u], length)
    at = lax.broadcasted_iota(jnp.int32, (8, ROWS), 1)
    live = ((at // LENGTH == user) & (at - user * LENGTH < length)).astype(F32)
    live_half = live.astype(BF)
    act_sum = dot_nn(live_half, act)
    low_sum = dot_nn(live_half, picked_low)
    high_sum = dot_nn(live_half, picked_high)
    count = length.astype(F32)
    shared = cot[...] / count[0:4]
    shared_half = shared.astype(BF)
    factors[:, 0:FH] = act_sum[0:4].astype(BF)
    factors[:, FH : FH + 128] = low_sum[0:4].astype(BF)
    factors[:, FH + 128 : FH + 256] = high_sum[0:4].astype(BF)
    factors[:, FH + 256 : FH + 256 + D] = shared_half
    coarse = act_sum.astype(BF)
    fine = (act_sum - coarse.astype(F32)).astype(BF)
    mixed = dot_nn(live_half, fetched) + dot_nn(coarse, down[...]) + dot_nn(fine, down[...])
    user_vec[...] = (mixed / count)[0:4]

    act_grad = dot_nt(jnp.concatenate([shared_half, shared_half], axis=0), down[...])
    position = lax.broadcasted_iota(jnp.int32, (LENGTH, 1), 0)
    pre_parts, base_parts = [], []
    for u in range(USERS_HERE):
        alive = (position < lengths[u]).astype(F32)
        pre_parts.append(alive * act_grad[u : u + 1] * slope[u * LENGTH : (u + 1) * LENGTH])
        base_parts.append(alive * shared[u : u + 1])
    pre_grad = jnp.concatenate(pre_parts, axis=0).astype(BF)
    rows_grad = jnp.concatenate(base_parts, axis=0) + dot_nt(pre_grad, up[...])
    rows_coarse = rows_grad.astype(BF)
    rows_fine = (rows_grad - rows_coarse.astype(F32)).astype(BF)
    low = dot_nt(rows_coarse, project[0:128]) + dot_nt(rows_fine, project[0:128])
    high = dot_nt(rows_coarse, project[64:192]) + dot_nt(rows_fine, project[64:192])
    lane = lax.broadcasted_iota(jnp.int32, (ROWS, 128), 1)
    tag = within.astype(F32)
    low = jnp.where(lane < 96, low, jnp.where(lane == 96, tag, 0.0)).astype(BF)
    high = jnp.where(lane >= 32, high, jnp.where(lane == 0, tag, 0.0)).astype(BF)

    owner_row = ids_row[...] // ITEMS_HERE
    earlier = lax.broadcasted_iota(jnp.int32, (ROWS, ROWS), 0) < lax.broadcasted_iota(jnp.int32, (ROWS, ROWS), 1)
    rank = jnp.sum(((owner == owner_row) & earlier).astype(F32), axis=0, keepdims=True).astype(jnp.int32)
    slot = owner_row * 8 + rank
    sent_at = lax.broadcasted_iota(jnp.int32, (DEVICES * 8, ROWS), 0)
    put_low = (sent_at == slot).astype(F32).astype(BF)
    put_high = (sent_at == slot + CAPACITY).astype(F32).astype(BF)
    back = (dot_nn(put_low, low) + dot_nn(put_high, high)).astype(BF)
    sent[:, 0:8, :] = back.reshape(DEVICES, 8, 128)
    up_low = dot_tn(picked_low, pre_grad).astype(BF)
    up_high = dot_tn(picked_high, pre_grad).astype(BF)
    for j in range(FH // 128):
        cut = slice(j * 128, (j + 1) * 128)
        sent[j * 16 : j * 16 + 8, 8:24, :] = up_low[:, cut].reshape(8, 16, 128)
        sent[j * 16 + 8 : j * 16 + 16, 8:24, :] = up_high[:, cut].reshape(8, 16, 128)


def conv_backward(
    back, x, counts, s1, t1, p1, e2, s2, t2, p2, g1, d1, sp1, n1, h1, o1, g2, d2, sp2, n2, h2,
    packed,
    spatial_grad, wide, small,
):
    taps1 = s1[...].astype(F32)
    taps2 = s2[...].astype(F32)
    frame1 = t1[...].astype(F32)
    frame2 = t2[...].astype(F32)

    def tile_sum(v):
        return jnp.sum(v.reshape(-1, 8, E), axis=0)

    small[...] = jnp.zeros(small.shape, F32)
    wide[...] = jnp.zeros(wide.shape, F32)
    got = back[:, 0:8, :].reshape(DEVICES * 8, 128)
    row = lax.broadcasted_iota(jnp.int32, (DEVICES * 8, 1), 0)
    is_low = (row & 7) < CAPACITY
    got_f = got.astype(F32)
    tag = jnp.where(is_low, got_f[:, 96:97], got_f[:, 0:1]).astype(jnp.int32)
    named = tag == lax.broadcasted_iota(jnp.int32, (DEVICES * 8, ITEMS_HERE), 1)
    low = dot_tn((named & is_low).astype(F32).astype(BF), got)
    high = dot_tn((named & ~is_low).astype(F32).astype(BF), got)
    pooled_grad = jnp.concatenate([low[:, 0:96], high[:, 32:128]], axis=1)
    shared = pooled_grad / counts[...].astype(F32)
    out_grad = jnp.concatenate(
        [(shared * (f < counts[...]).astype(F32)).astype(BF) for f in range(FRAMES)], axis=0
    )
    wide[576:768, 0:E] = dot_tn(out_grad, n2[...].reshape(FRAMES * ITEMS_HERE, E))
    summed_grad = dot_nt(out_grad, p2[...]).reshape(FRAMES, ITEMS_HERE, E) * h2[...].astype(F32)
    spread = []
    for f in range(FRAMES):
        total = summed_grad[f] * frame2[1]
        if f + 1 < FRAMES:
            total = total + summed_grad[f + 1] * frame2[0]
        if f > 0:
            total = total + summed_grad[f - 1] * frame2[2]
        spread.append(total)
    for k in range(3):
        total = jnp.zeros((8, E), F32)
        for f in range(FRAMES):
            if 0 <= f + k - 1 < FRAMES:
                total = total + tile_sum(sp2[f + k - 1].astype(F32) * summed_grad[f])
        small[21 + k] = total
    parts = []
    for f in range(FRAMES):
        for cell, tap in LINKS_SECOND:
            small[12 + tap] += tile_sum(g2[f * 4 + cell].astype(F32) * spread[f])
            parts.append((spread[f] * taps2[tap] * d2[f * 4 + cell].astype(F32)).astype(BF))
    grown_grad = jnp.concatenate(parts, axis=0)
    wide[384:576, 0:E] = dot_tn(o1[...], grown_grad)
    first_grad = dot_nt(grown_grad, e2[...]).astype(BF)
    wide[192:384, 0:E] = dot_tn(first_grad, n1[...].reshape(FRAMES * 4 * ITEMS_HERE, E))
    narrow_grad = dot_nt(first_grad, p1[...]).reshape(FRAMES, 4, ITEMS_HERE, E)
    summed_grad = [narrow_grad[f] * h1[f * 4 : f * 4 + 4].astype(F32) for f in range(FRAMES)]
    for k in range(3):
        total = jnp.zeros((8, E), F32)
        for f in range(FRAMES):
            if 0 <= f + k - 1 < FRAMES:
                total = total + tile_sum(sp1[f + k - 1].astype(F32) * summed_grad[f])
        small[9 + k] = total
    for f in range(FRAMES):
        total = summed_grad[f] * frame1[1]
        if f + 1 < FRAMES:
            total = total + summed_grad[f + 1] * frame1[0]
        if f > 0:
            total = total + summed_grad[f - 1] * frame1[2]
        spatial_grad[f] = total

    def grow_back(f, _):
        live = f < counts[...]
        x_f = x[pl.ds(f * CELLS, CELLS)]
        x_f = jnp.where(live[None], x_f, jnp.zeros_like(x_f)).reshape(CELLS * ITEMS_HERE, C)
        sums = [jnp.zeros((8, E), F32)] * 9
        grads = [jnp.zeros((ITEMS_HERE, E), F32)] * CELLS
        for out_cell, in_cell, tap in LINKS_FIRST:
            from_out = spatial_grad[f, out_cell]
            grads[in_cell] = grads[in_cell] + from_out * taps1[tap]
            sums[tap] = sums[tap] + tile_sum(g1[f * CELLS + in_cell].astype(F32) * from_out)
        for tap in range(9):
            small[tap] += sums[tap]
        grads = [(grads[cell] * d1[f * CELLS + cell].astype(F32)).astype(BF) for cell in range(CELLS)]
        wide[0:192, 0:E] += dot_tn(x_f, jnp.concatenate(grads, axis=0))
        return 0

    lax.fori_loop(0, FRAMES, grow_back, 0)
    sums = jnp.sum(small[...], axis=1).astype(BF)
    put = lax.broadcasted_iota(jnp.int32, (32, 128), 1) == lax.broadcasted_iota(jnp.int32, (32, 128), 0) + 64
    wide[0:E, 384:512] += dot_tn(sums, put.astype(F32).astype(BF))
    for j in range(4):
        packed[j * 768 : (j + 1) * 768] = wide[:, j * 128 : (j + 1) * 128].astype(BF)


def finish_tower(factors, up_total, project, up, grad_item, grad_up, grad_down):
    shared = factors[:, FH + 256 : FH + 256 + D]
    grad_down[...] = dot_tn(factors[:, 0:FH], shared)
    item = dot_tn(factors[:, FH : FH + C], shared)
    for j in range(FH // 128):
        part = up_total[j * 16 : j * 16 + 16].reshape(256, 128)[0:C]
        cut = slice(j * 128, (j + 1) * 128)
        grad_up[:, cut] = dot_tn(project[...], part)
        item = item + dot_nt(part, up[:, cut])
    grad_item[...] = item


def finish_conv(packed, ge1, gs1, gt1, gp1, ge2, gs2, gt2, gp2):
    def unit(n):
        same = lax.broadcasted_iota(jnp.int32, (n, n), 0) == lax.broadcasted_iota(jnp.int32, (n, n), 1)
        return same.astype(F32).astype(BF)

    turn = unit(C)
    for j in range(4):
        width = min(128, E - j * 128)
        at = j * 768
        cut = slice(j * 128, j * 128 + width)
        ge1[:, cut] = packed[at : at + 192].astype(F32)[:, 0:width]
        gp1[cut, :] = dot_tn(packed[at + 192 : at + 384], turn)[0:width]
        ge2[:, cut] = packed[at + 384 : at + 576].astype(F32)[:, 0:width]
        gp2[cut, :] = dot_tn(packed[at + 576 : at + 768], turn)[0:width]
    small = dot_tn(packed[3 * 768 : 3 * 768 + E], unit(E))
    gs1[...] = small[64:73]
    gt1[...] = small[73:76]
    gs2[...] = small[76:85]
    gt2[...] = small[85:88]


def shape(dims, dtype=BF):
    return jax.ShapeDtypeStruct(dims, dtype)


def call(kernel, outs, scratch=(), smem=0):
    def run(*args):
        return pl.pallas_call(
            kernel,
            out_shape=outs,
            in_specs=[
                pl.BlockSpec(memory_space=pltpu.SMEM if i < smem else pltpu.VMEM)
                for i in range(len(args))
            ],
            out_specs=[pl.BlockSpec(memory_space=pltpu.VMEM)] * len(outs),
            scratch_shapes=list(scratch),
            compiler_params=pltpu.CompilerParams(vmem_limit_bytes=56 * 1024 * 1024),
        )(*args)

    return run


def local(
    clips, clip_counts, histories, lengths, user_cotangent,
    expand_first, spatial_first, temporal_first, project_first,
    expand_second, spatial_second, temporal_second, project_second,
    item_project, tower_up, tower_down,
):
    same_core = [[i for i in range(DEVICES) if i % 2 == c] for c in range(2)]
    other_core = [(i, i ^ 1) for i in range(8)]
    core = lax.axis_index("seq") % 2

    def exchange(v):
        return lax.all_to_all(v, AXES, 0, 0, tiled=True)

    x = clips.reshape(ITEMS_HERE, FRAMES * CELLS, C).transpose(1, 0, 2)
    counts = clip_counts.reshape(ITEMS_HERE, 1)
    weights = (
        spatial_first, temporal_first, project_first,
        expand_second, spatial_second, temporal_second, project_second,
    )
    n = ITEMS_HERE
    block, *kept = call(
        conv_forward,
        [
            shape((64, 128)),
            shape((64, n, E)), shape((64, n, E)), shape((4, 4, n, E)), shape((16, n, E)), shape((16, n, E)),
            shape((512, C)), shape((16, n, E)), shape((16, n, E)), shape((4, n, E)), shape((4, n, E)), shape((4, n, E)),
        ],
        [pltpu.VMEM((FRAMES + 2, 4, n, E), F32), pltpu.VMEM((FRAMES + 2, n, E), F32)],
    )(x, counts, expand_first, *weights)
    own = lax.all_to_all(
        jnp.broadcast_to(block[None], (CHIPS, 64, 128)), AXES, 0, 0, axis_index_groups=same_core, tiled=True
    )
    other = lax.ppermute(own, "seq", other_core)
    sent, factors, user_vec = call(
        tower,
        [shape((DEVICES, 24, 128)), shape((USERS_HERE, FH + 256 + D)), shape((USERS_HERE, D), F32)],
        smem=2,
    )(
        core.reshape(1), lengths, own, other, histories.reshape(ROWS, 1), histories.reshape(1, ROWS),
        user_cotangent, item_project, tower_up, tower_down,
    )
    factors = lax.all_gather(factors, AXES, tiled=True)
    back = exchange(sent)
    (packed,) = call(
        conv_backward,
        [shape((3072, 128))],
        [pltpu.VMEM((4, 4, n, E), F32), pltpu.VMEM((768, 512), F32), pltpu.VMEM((32, 8, E), F32)],
    )(back, x, counts, *weights, *kept)
    up_sum = jnp.sum(back[:, 8:24].astype(F32), axis=0).astype(BF)
    third = exchange(
        jnp.concatenate([packed.reshape(DEVICES, 24, 128), jnp.broadcast_to(up_sum[None], (DEVICES, 16, 128))], axis=1)
    )
    conv_sum = jnp.sum(third[:, 0:24].astype(F32), axis=0).astype(BF)
    fourth = exchange(jnp.broadcast_to(conv_sum[None], (DEVICES, 24, 128)))
    grad_item, grad_up, grad_down = call(
        finish_tower, [shape((C, D), F32), shape((D, FH), F32), shape((FH, D), F32)]
    )(factors, third[:, 24:40], item_project, tower_up)
    conv_grads = call(
        finish_conv,
        [shape((C, E), F32), shape((9, E), F32), shape((3, E), F32), shape((E, C), F32)] * 2,
    )(fourth.reshape(3072, 128))
    return (user_vec, *conv_grads, grad_item, grad_up, grad_down)


def solution(mesh):
    spread = P(AXES)
    return jax.shard_map(
        local,
        mesh=mesh,
        in_specs=(spread,) * 5 + (P(),) * 11,
        out_specs=(spread,) + (P(),) * 11,
        check_vma=False,
    )
```

time: 481 us -> 171 us (0.36)
  local copies, waits for them, and re-layouts: 167 us -> 19.2 us
  waiting for transfers between devices: 114 us -> 17.4 us
  other arithmetic: 50.4 us -> 1.55 us
  matrix products: 34.7 us -> 0 us
  Pallas kernels: 0 us -> 34.2 us
  starting transfers between devices: 28.6 us -> 7.11 us
  blocking collectives: 64.8 us -> 76.6 us
    psum x1 -> x0, waiting for transfers between devices: 89.2 us -> none  [local(): lax.psum((terms[0], terms[1], terms[2], terms[3], terms[4], terms[5], ter...]
    all_to_all x0 -> x3, blocking collectives: none -> 76.6 us  [the longest x2 47.7 us: exchange(): return lax.all_to_all(v, AXES, 0, 0, tiled=True)]
    psum x1 -> x0, blocking collectives: 64.8 us -> none  [local(): lax.psum((terms[0], terms[1], terms[2], terms[3], terms[4], terms[5], ter...]
    pad x5 -> x0, local copies, waits for them, and re-layouts: 49.6 us -> none  [the longest x4 42.4 us: conv_section(): padded[:, :, offset_row:offset_row + 2 * half_side:2, offset_col:offset_c...]
    unnamed x160 -> x22, local copies, waits for them, and re-layouts: 57.2 us -> 14.3 us
    convert_element_type x18 -> x0, local copies, waits for them, and re-layouts: 36.8 us -> none  [the longest x7 24.8 us: conv_section(): grown = jax.nn.silu(grown).astype(jnp.bfloat16).reshape(item_count, frame...]
    dot_general x25 -> x0, matrix products: 34.7 us -> none  [the longest x5 13.4 us: conv_section(): jnp.dot(masked.reshape(-1, channels), expand, preferred_element_type=jnp....]
    pallas_call x0 -> x5, Pallas kernels: none -> 34.2 us  [run(): pl.pallas_call(kernel, out_shape=outs, in_specs=[pl.BlockSpec(memory_spac...]
  transfers between devices with their start and end apart: 4 -> 3, of which waited for: 3 -> 2; matrix products, arithmetic and copies ran while one was open for 9% -> 5% of each run, Pallas kernels for 0% -> 7%
where the time goes in v1:
time: 171 us; the launch traced here: 170 us
  blocking collectives  76.6 us (45%)
  Pallas kernels  34.2 us (20%)
  local copies, waits for them, and re-layouts  19.2 us (11%)
  waiting for transfers between devices  17.4 us (10%)
  between operations  14.1 us (8%)
  starting transfers between devices  7.11 us (4%)
    all_to_all x2, blocking collectives, exchange(): return lax.all_to_all(v, AXES, 0, 0, tiled=True)  47.7 us
    pallas_call x5, Pallas kernels, run(): pl.pallas_call(kernel, out_shape=outs, in_specs=[pl.BlockSpec(memory_spac...  34.2 us
    all_to_all x1, blocking collectives, local(): lax.all_to_all(jnp.broadcast_to(block[None], (CHIPS, 64, 128)), AXES, 0,...  29 us
    all_to_all x1, waiting for transfers between devices, exchange(): return lax.all_to_all(v, AXES, 0, 0, tiled=True)  16.6 us
    unnamed x22, local copies, waits for them, and re-layouts  14.3 us
    all_to_all x1, starting transfers between devices, exchange(): return lax.all_to_all(v, AXES, 0, 0, tiled=True)  4.61 us
  transfers between devices with their start and end apart: 3, of which 2 were waited for; matrix products, arithmetic and copies ran while one was open for 5% of the time, Pallas kernels for 7%

profile of v1, /device:TPU:1, one launch (start us, length us, event | category | flops | bytes accessed | tf_op | source)
XLA Modules:
  0.0 170.3 jit_solution(14360516528825714705)
XLA Ops:
  7.2 0.0 copy-start.4
  7.2 0.0 copy-start.5
  7.2 0.0 copy-start.7
  7.2 0.0 all-gather.3.cloned.1.call-start
  7.3 2.9 %copy.47 = bf16[32,4,4,4,192]{4,0,3,2,1:T(8,128)(2,1)} copy(bf16[32,4,4,4,192]{4,3,2,1,0:T(4,128)(2,1)} %param.16) | data formatting | bytes 1572864 | tf_op args[0]
  10.1 0.0 copy-done.4
  10.1 0.8 copy.49.p1
  11.0 0.0 copy-done.5
  11.0 0.8 copy.50.p2
  11.8 0.0 copy-done.7
  11.8 0.7 copy.48.counts
  12.5 7.9 %shard_map.247 = (bf16[64,128]{1,0:T(8,128)(2,1)}, bf16[64,32,432]{2,1,0:T(8,128)(2,1)}, bf16[64,32,432]{2,1,0:T(8,128)(2,1)}, bf16[4,4,32,432]{3,2,1,0:T(8,128)...) custom-call(bf16[64,32,192]{2,1,0:T(8,128)(2,1)} %bitcast.8, ...), custom_call_target="tpu_custom_call" | custom-call | tf_op jit(solution)/shard_map/pallas_call | solution.py:334
  20.3 0.0 copy-start.6
  20.4 1.0 broadcast_in_dim.6
  21.3 29.0 %all_to_all.20.own = bf16[64,64,128]{2,1,0:T(8,128)(2,1)S(1)} all-to-all(bf16[64,64,128]{2,1,0:T(8,128)(2,1)S(1)} %broadcast_in_dim.6), channel_id=1, replica_groups={{0,2,4,6,8,10,12,14,16,18,20,22,24,26,28,30,32,34,36,38,40,42,44,46,48,..., dimensions={0} | all-to-all | bytes 2097152 | tf_op jit(solution)/shard_map/all_to_all | solution.py:378
  50.3 0.0 copy-start.1
  50.3 2.5 %collective-permute-start = (bf16[64,64,128]{2,1,0:T(8,128)(2,1)S(1)}, bf16[64,64,128]{2,1,0:T(8,128)(2,1)S(1)}, u32[]{:S(2)}, u32[]{:S(2)}) collective-permute-start(bf16[64,64,128]{2,1,0:T(8,128)(2,1)S(1)} %all_to_all.20.own), channel_id=1, source_target_pairs={{0,1},{1,0},{2,3},{3,2},{4,5},{5,4},{6,7},{7,6},{8,9},{9,8},{10,11... | collective-permute-start | bytes 3145736 | tf_op jit(solution)/shard_map/ppermute | solution.py:381
  52.8 0.0 copy-done.6
  52.8 0.8 reshape.57.ids_col
  53.6 0.6 reshape.52.ids_row
  54.2 0.8 collective-permute-done.other
  55.0 0.0 copy-start.3
  55.0 0.0 copy-done.1
  55.1 1.0 copy-done.3
  56.0 7.8 %shard_map.248 = (bf16[128,24,128]{2,1,0:T(8,128)(2,1)}, bf16[4,1792]{1,0:T(4,128)(2,1)}, f32[4,512]{1,0:T(4,128)}) custom-call(s32[1]{0:T(128)} %bitcast.core, s32[4]{0:T(128)} %lengths.1, bf16[64,64,128]{2,1,0:T(8,128)(2,1)} %copy-done.1, bf16[64,64,128]{2,1,0:T(8,128)(2,1)} %copy-done.3, s32[256,1]{1,0:T(8,128)} %reshape.57.ids_col, ...), custom_call_target="tpu_custom_call" | custom-call | tf_op jit(solution)/shard_map/pallas_call | solution.py:334
  63.8 0.0 all-gather.3.cloned.1.call-update
  63.8 21.3 %all_to_all.21.back = bf16[128,24,128]{2,1,0:T(8,128)(2,1)} all-to-all(bf16[128,24,128]{2,1,0:T(8,128)(2,1)} %get-tuple-element.40), channel_id=1, replica_groups=mesh['bulk'=16,'seq'=8] {'bulk','seq'}, dimensions={0} | all-to-all | bytes 1572864 | tf_op jit(solution)/shard_map/all_to_all | solution.py:360
  85.2 0.0 copy-start
  85.2 10.0 %shard_map.249 = bf16[3072,128]{1,0:T(8,128)(2,1)} custom-call(bf16[128,24,128]{2,1,0:T(8,128)(2,1)} %all_to_all.21.back, bf16[64,32,192]{2,1,0:T(8,128)(2,1)} %bitcast.9, s32[32,1]{1,0:T(8,128)} %copy.48.counts, bf16[9,432]{1,0:T(8,128)(2,1)} %s1_.3, bf16[3,432]{1,0:T(4,128)(2,1)} %t1.3, bf16[432,192]{1,0:T(8,128)(2,1)} %copy.49.p1, bf16[192,432]{1,0:T(8,128)(2,1)} %e2.3, ...), custom_call_target="tpu_custom_call" | custom-call | tf_op jit(solution)/shard_map/pallas_call | solution.py:334
  95.2 0.0 copy-done
  95.2 0.1 slice_reduce_fusion.1
  95.3 0.1 broadcast_in_dim.7
  95.4 1.3 pad_maximum_fusion
  96.7 26.3 %all_to_all.22 = bf16[128,40,128]{2,1,0:T(8,128)(2,1)S(1)} all-to-all(bf16[128,40,128]{2,1,0:T(8,128)(2,1)S(1)} %pad_maximum_fusion), channel_id=1, replica_groups=mesh['bulk'=16,'seq'=8] {'bulk','seq'}, dimensions={0} | all-to-all | bytes 2621440 | tf_op jit(solution)/shard_map/all_to_all | solution.py:360
  123.0 0.2 slice_reduce_fusion
  123.2 1.0 broadcast_in_dim.8
  124.1 4.6 %all-to-all-start.3 = ((bf16[128,24,128]{2,1,0:T(8,128)(2,1)}), bf16[128,24,128]{2,1,0:T(8,128)(2,1)S(1)}, u32[]{:S(2)}, u32[]{:S(2)}) async-start(bf16[128,24,128]{2,1,0:T(8,128)(2,1)} %broadcast_in_dim.8), calls=%async_computation.3 | async-start | bytes 1572864 | tf_op jit(solution)/shard_map/all_to_all | solution.py:360
  128.8 0.8 slice.14.up_total
  129.6 16.6 %all-to-all-done.3 = bf16[128,24,128]{2,1,0:T(8,128)(2,1)S(1)} async-done(((bf16[128,24,128]{2,1,0:T(8,128)(2,1)}), bf16[128,24,128]{2,1,0:T(8,128)(2,1)S(1)}, u32[]{:S(2)}, u32[]{:S(2)}) %all-to-all-start.3) | async-done | bytes 786464 | tf_op jit(solution)/shard_map/all_to_all | solution.py:360
  146.2 0.0 copy-start.2
  146.2 0.9 copy-done.2
  147.0 2.6 %shard_map.250 = (f32[192,432]{1,0:T(8,128)}, f32[9,432]{1,0:T(8,128)}, f32[3,432]{1,0:T(4,128)}, f32[432,192]{1,0:T(8,128)}, f32[192,432]{1,0:T(8,128)}, /*inde...) custom-call(bf16[3072,128]{1,0:T(8,128)(2,1)} %bitcast.11), custom_call_target="tpu_custom_call" | custom-call | tf_op jit(solution)/shard_map/pallas_call | solution.py:334
  149.7 1.9 %copy.55 = f32[432,192]{0,1:T(8,128)} copy(f32[432,192]{1,0:T(8,128)} %get-tuple-element.92) | data formatting | bytes 663552
  151.6 1.9 %copy.56 = f32[432,192]{0,1:T(8,128)} copy(f32[432,192]{1,0:T(8,128)} %get-tuple-element.96) | data formatting | bytes 663552
  153.6 0.0 all-gather.3.cloned.1.call-done
  153.6 4.0 %reshape.56.factors = bf16[512,1792]{1,0:T(8,128)(2,1)} reshape(bf16[128,4,1792]{2,1,0:T(4,128)(2,1)} %all-gather.3.cloned.1.call-done) | data formatting | bytes 3670016
  157.5 6.0 %shard_map.251 = (f32[192,512]{1,0:T(8,128)}, f32[512,1024]{1,0:T(8,128)}, f32[1024,512]{1,0:T(8,128)}) custom-call(bf16[512,1792]{1,0:T(8,128)(2,1)} %reshape.56.factors, bf16[128,16,128]{2,1,0:T(8,128)(2,1)} %slice.14.up_total, bf16[192,512]{1,0:T(8,128)(2,1)} %project.3, bf16[512,1024]{1,0:T(8,128)(2,1)} %up.3), custom_call_target="tpu_custom_call" | custom-call | tf_op jit(solution)/shard_map/pallas_call | solution.py:334
Async XLA Ops:
  7.2 3.0 %copy-start.4 = (bf16[432,192]{0,1:T(8,128)(2,1)S(1)}, bf16[432,192]{0,1:T(8,128)(2,1)}, u32[]{:S(2)}) copy-start(bf16[432,192]{0,1:T(8,128)(2,1)} %param.24) | copy-start | bytes 497668
  7.2 3.8 %copy-start.5 = (bf16[432,192]{0,1:T(8,128)(2,1)S(1)}, bf16[432,192]{0,1:T(8,128)(2,1)}, u32[]{:S(2)}) copy-start(bf16[432,192]{0,1:T(8,128)(2,1)} %param.28) | copy-start | bytes 497668
  7.2 4.6 %copy-start.7 = (s32[32]{0:T(128)S(1)}, s32[32]{0:T(128)}, u32[]{:S(2)}) copy-start(s32[32]{0:T(128)} %param.17) | copy-start | bytes 388
  7.2 146.4 %all-gather.3.cloned.1.call-start = ((), (), s32[]{:S(2)}) async-start(), calls=%async_computation.4 | async-start | bytes 1849344 | tf_op jit(solution)/shard_map/all_gather | solution.py:390
  20.3 32.4 %copy-start.6 = (s32[4,64]{1,0:T(4,128)S(1)}, s32[4,64]{1,0:T(4,128)}, u32[]{:S(2)}) copy-start(s32[4,64]{1,0:T(4,128)} %param.18) | copy-start | bytes 3076
  50.3 4.8 %copy-start.1 = (bf16[64,64,128]{2,1,0:T(8,128)(2,1)}, bf16[64,64,128]{2,1,0:T(8,128)(2,1)S(1)}, u32[]{:S(2)}) copy-start(bf16[64,64,128]{2,1,0:T(8,128)(2,1)S(1)} %all_to_all.20.own) | copy-start | bytes 3145732
  50.3 4.7 %collective-permute-start = (bf16[64,64,128]{2,1,0:T(8,128)(2,1)S(1)}, bf16[64,64,128]{2,1,0:T(8,128)(2,1)S(1)}, u32[]{:S(2)}, u32[]{:S(2)}) collective-permute-start(bf16[64,64,128]{2,1,0:T(8,128)(2,1)S(1)} %all_to_all.20.own), channel_id=1, source_target_pairs={{0,1},{1,0},{2,3},{3,2},{4,5},{5,4},{6,7},{7,6},{8,9},{9,8},{10,11... | collective-permute-start | bytes 3145736 | tf_op jit(solution)/shard_map/ppermute | solution.py:381
  55.0 1.0 copy-start.3
  85.2 10.0 %copy-start = (bf16[128,24,128]{2,1,0:T(8,128)(2,1)S(1)}, bf16[128,24,128]{2,1,0:T(8,128)(2,1)}, u32[]{:S(2)}) copy-start(bf16[128,24,128]{2,1,0:T(8,128)(2,1)} %all_to_all.21.back) | copy-start | bytes 2359300
  124.1 22.0 %all-to-all-start.3 = ((bf16[128,24,128]{2,1,0:T(8,128)(2,1)}), bf16[128,24,128]{2,1,0:T(8,128)(2,1)S(1)}, u32[]{:S(2)}, u32[]{:S(2)}) async-start(bf16[128,24,128]{2,1,0:T(8,128)(2,1)} %broadcast_in_dim.8), calls=%async_computation.3 | async-start | bytes 1572864 | tf_op jit(solution)/shard_map/all_to_all | solution.py:360
  146.2 0.9 copy-start.2
Sparse Core Ops, SparseCore 0:
  64.0 79.1 all-gather.2

commit v2 on v1

v2 whole, which is shorter than its diff:
```python
import jax
import jax.numpy as jnp
from jax import lax
from jax.experimental import pallas as pl
from jax.experimental.pallas import tpu as pltpu
from jax.sharding import PartitionSpec as P

BF = jnp.bfloat16
F32 = jnp.float32
AXES = ("bulk", "seq")
C, E, D, FH = 192, 432, 512, 1024
FRAMES, SIDE, ITEMS_HERE, USERS_HERE, LENGTH = 4, 4, 32, 4, 64
DEVICES, CHIPS, CAPACITY = 128, 64, 4
ROWS = USERS_HERE * LENGTH
CELLS = SIDE * SIDE
HALF = 2
LINKS_FIRST = [
    (HALF * p + q, SIDE * (2 * p + a - 1) + 2 * q + b - 1, 3 * a + b)
    for p in range(HALF)
    for q in range(HALF)
    for a in range(3)
    for b in range(3)
    if 0 <= 2 * p + a - 1 < SIDE and 0 <= 2 * q + b - 1 < SIDE
]
LINKS_SECOND = [(0, 4), (1, 5), (2, 7), (3, 8)]


def dot_nn(a, b):
    return lax.dot_general(a, b, (((1,), (0,)), ((), ())), preferred_element_type=F32)


def dot_nt(a, b):
    return lax.dot_general(a, b, (((1,), (1,)), ((), ())), preferred_element_type=F32)


def dot_tn(a, b):
    return lax.dot_general(a, b, (((0,), (0,)), ((), ())), preferred_element_type=F32)


def silu_and_slope(v):
    gate = 0.5 * jnp.tanh(0.5 * v) + 0.5
    value = v * gate
    return value, gate + value - value * gate


def column_of(row):
    n = row.shape[1]
    same = lax.broadcasted_iota(jnp.int32, (n, n), 0) == lax.broadcasted_iota(jnp.int32, (n, n), 1)
    return jnp.sum(jnp.where(same, row.astype(F32), 0.0), axis=1, keepdims=True).astype(jnp.int32)


def per_user(lengths):
    user = lax.broadcasted_iota(jnp.int32, (8, 1), 0)
    length = jnp.ones((8, 1), jnp.int32)
    for u in range(USERS_HERE):
        length = jnp.where(user == u, lengths[u], length)
    return user, length


def conv_forward(
    lengths, x, counts_row, cot, e1, s1, t1, p1, e2, s2, t2, p2, *rest,
):
    *kept, framed1, framed2 = rest
    block = None
    if len(kept) == 1:
        (block,) = kept
    else:
        g1, d1, sp1, n1, h1, o1, g2, d2, sp2, n2, h2 = kept
    counts = column_of(counts_row[...])
    zero4 = jnp.zeros((HALF * HALF, ITEMS_HERE, E), F32)
    framed1[0] = zero4
    framed1[FRAMES + 1] = zero4
    zero1 = jnp.zeros((ITEMS_HERE, E), F32)
    framed2[0] = zero1
    framed2[FRAMES + 1] = zero1
    taps1 = s1[...].astype(F32)
    taps2 = s2[...].astype(F32)
    frame1 = t1[...].astype(F32)
    frame2 = t2[...].astype(F32)

    def grow(f, _):
        live = f < counts
        x_f = x[pl.ds(f * CELLS, CELLS)]
        x_f = jnp.where(live[None], x_f, jnp.zeros_like(x_f))
        pre = dot_nn(x_f.reshape(CELLS * ITEMS_HERE, C), e1[...])
        value, slope = silu_and_slope(pre)
        value = value.astype(BF).reshape(CELLS, ITEMS_HERE, E)
        if block is None:
            g1[pl.ds(f * CELLS, CELLS)] = value
            d1[pl.ds(f * CELLS, CELLS)] = slope.astype(BF).reshape(CELLS, ITEMS_HERE, E)
        outs = [jnp.zeros((ITEMS_HERE, E), F32)] * 4
        for out_cell, in_cell, tap in LINKS_FIRST:
            outs[out_cell] = outs[out_cell] + value[in_cell].astype(F32) * taps1[tap]
        for out_cell in range(4):
            framed1[f + 1, out_cell] = outs[out_cell]
            if block is None:
                sp1[f, out_cell] = outs[out_cell].astype(BF)
        return 0

    lax.fori_loop(0, FRAMES, grow, 0)
    narrow = []
    for f in range(FRAMES):
        summed = framed1[f] * frame1[0] + framed1[f + 1] * frame1[1] + framed1[f + 2] * frame1[2]
        value, slope = silu_and_slope(summed)
        narrow.append(value.astype(BF))
        if block is None:
            h1[f * 4 : f * 4 + 4] = slope.astype(BF)
    narrow = jnp.concatenate(narrow, axis=0)
    first = dot_nt(narrow.reshape(FRAMES * 4 * ITEMS_HERE, E), p1[...]).astype(BF)
    value, slope = silu_and_slope(dot_nn(first, e2[...]))
    value = value.astype(BF).reshape(FRAMES * 4, ITEMS_HERE, E)
    if block is None:
        n1[...] = narrow
        o1[...] = first
        g2[...] = value
        d2[...] = slope.astype(BF).reshape(FRAMES * 4, ITEMS_HERE, E)
    for f in range(FRAMES):
        total = jnp.zeros((ITEMS_HERE, E), F32)
        for cell, tap in LINKS_SECOND:
            total = total + value[f * 4 + cell].astype(F32) * taps2[tap]
        framed2[f + 1] = total
        if block is None:
            sp2[f] = total.astype(BF)
    narrow = []
    for f in range(FRAMES):
        summed = framed2[f] * frame2[0] + framed2[f + 1] * frame2[1] + framed2[f + 2] * frame2[2]
        value, slope = silu_and_slope(summed)
        narrow.append(value.astype(BF))
        if block is None:
            n2[f] = value.astype(BF)
            h2[f] = slope.astype(BF)
    if block is None:
        return
    second = dot_nt(jnp.concatenate(narrow, axis=0), p2[...]).astype(BF)
    pooled = jnp.zeros((ITEMS_HERE, C), F32)
    for f in range(FRAMES):
        live = (f < counts).astype(F32)
        pooled = pooled + live * second[f * ITEMS_HERE : (f + 1) * ITEMS_HERE].astype(F32)
    pooled = pooled / counts.astype(F32)
    _, length = per_user(lengths)
    shared = cot[...] / length[0:4].astype(F32)
    pieces = []
    for k in range(8):
        piece = shared[:, (k // 2) * 128 : (k // 2 + 1) * 128]
        pieces.append(piece if k % 2 else pltpu.roll(piece, 64, 1))
    lane = lax.broadcasted_iota(jnp.int32, (ITEMS_HERE, 128), 1)
    shared = jnp.concatenate(pieces, axis=0)
    high = jnp.concatenate([pooled[:, 128:192], pooled[:, 0:64]], axis=1)
    rows = jnp.concatenate([pooled[:, 0:128], jnp.where(lane < 64, high, shared)], axis=0).astype(BF)
    block[...] = jnp.broadcast_to(rows[None], block.shape)


def tower(
    core, lengths, own, other, ids_ref, cot, project, up, down,
    sent, picked_out, fetched_out, act_out, pre_grad_out,
):
    ids = jnp.concatenate([column_of(ids_ref[u : u + 1]) for u in range(USERS_HERE)], axis=0)
    owner = ids // ITEMS_HERE
    within = ids - owner * ITEMS_HERE
    chip = owner // 2
    place = chip * ITEMS_HERE + within
    mine = (owner - chip * 2) == core[0]
    lanes = lax.broadcasted_iota(jnp.int32, (ROWS, CHIPS * ITEMS_HERE), 1)
    pick_own = (lanes == jnp.where(mine, place, -1)).astype(F32).astype(BF)
    pick_other = (lanes == jnp.where(mine, -1, place)).astype(F32).astype(BF)

    def rows_of(ref):
        low = ref[:, 0:32, :].reshape(CHIPS * ITEMS_HERE, 128)
        high = ref[:, 32:64, :].reshape(CHIPS * ITEMS_HERE, 128)
        return jnp.concatenate([low, high], axis=1)

    picked = (dot_nn(pick_own, rows_of(own)) + dot_nn(pick_other, rows_of(other))).astype(BF)
    fetched = dot_nn(picked[:, 0:C], project[...]).astype(BF)
    pre = dot_nn(fetched, up[...])
    scale = 0.7978845608028654
    square = pre * pre
    bent = jnp.tanh(scale * pre * (1.0 + 0.044715 * square))
    gate = 0.5 * (1.0 + bent)
    picked_out[...] = picked
    fetched_out[...] = fetched
    act_out[...] = (pre * gate).astype(BF)
    slope = gate + 0.5 * pre * (1.0 - bent * bent) * (scale * (1.0 + 3 * 0.044715 * square))
    _, length = per_user(lengths)
    shared = cot[...] / length[0:4].astype(F32)
    shared_half = shared.astype(BF)
    act_grad = dot_nt(jnp.concatenate([shared_half, shared_half], axis=0), down[...])
    position = lax.broadcasted_iota(jnp.int32, (LENGTH, 1), 0)
    pre_parts, base_parts = [], []
    for u in range(USERS_HERE):
        alive = (position < lengths[u]).astype(F32)
        pre_parts.append(alive * act_grad[u : u + 1] * slope[u * LENGTH : (u + 1) * LENGTH])
        base_parts.append(alive * shared[u : u + 1])
    pre_grad = jnp.concatenate(pre_parts, axis=0).astype(BF)
    pre_grad_out[...] = pre_grad
    rows_grad = jnp.concatenate(base_parts, axis=0) + dot_nt(pre_grad, up[...])
    rows_coarse = rows_grad.astype(BF)
    rows_fine = (rows_grad - rows_coarse.astype(F32)).astype(BF)
    low = dot_nt(rows_coarse, project[0:128]) + dot_nt(rows_fine, project[0:128])
    high = dot_nt(rows_coarse, project[64:192]) + dot_nt(rows_fine, project[64:192])
    lane = lax.broadcasted_iota(jnp.int32, (ROWS, 128), 1)
    tag = within.astype(F32)
    low = jnp.where(lane < 96, low, jnp.where(lane == 96, tag, 0.0)).astype(BF)
    high = jnp.where(lane >= 32, high, jnp.where(lane == 0, tag, 0.0)).astype(BF)

    across = lax.broadcasted_iota(jnp.int32, (ROWS, ROWS), 1)
    down_rows = lax.broadcasted_iota(jnp.int32, (ROWS, ROWS), 0)
    owner_row = jnp.sum(jnp.where(across == down_rows, owner.astype(F32), 0.0), axis=0, keepdims=True).astype(jnp.int32)
    earlier = down_rows < across
    rank = jnp.sum(((owner == owner_row) & earlier).astype(F32), axis=0, keepdims=True).astype(jnp.int32)
    slot = owner_row * 8 + rank
    sent_at = lax.broadcasted_iota(jnp.int32, (DEVICES * 8, ROWS), 0)
    put_low = (sent_at == slot).astype(F32).astype(BF)
    put_high = (sent_at == slot + CAPACITY).astype(F32).astype(BF)
    back = (dot_nn(put_low, low) + dot_nn(put_high, high)).astype(BF)
    sent[...] = back.reshape(DEVICES, 8, 128)


def tower_sums(
    core, lengths, picked, fetched, act, pre_grad, down,
    up_keep, up_send, factors, user_vec,
    halves,
):
    user, length = per_user(lengths)
    at = lax.broadcasted_iota(jnp.int32, (8, ROWS), 1)
    live = ((at // LENGTH == user) & (at - user * LENGTH < length)).astype(F32).astype(BF)
    act_sum = dot_nn(live, act[...])
    picked_sum = dot_nn(live, picked[...])
    pieces = [act_sum[0:4, j * 128 : (j + 1) * 128] for j in range(8)]
    pieces += [picked_sum[0:4, j * 128 : (j + 1) * 128] for j in range(2)]
    factors[...] = jnp.concatenate(pieces, axis=0).astype(BF)
    coarse = act_sum.astype(BF)
    fine = (act_sum - coarse.astype(F32)).astype(BF)
    mixed = dot_nn(live, fetched[...]) + dot_nn(coarse, down[...]) + dot_nn(fine, down[...])
    user_vec[...] = (mixed / length.astype(F32))[0:4]
    up_grad = dot_tn(picked[...], pre_grad[...]).astype(BF)
    for j in range(FH // 128):
        halves[j // 4, (j % 4) * 256 : (j % 4 + 1) * 256] = up_grad[:, j * 128 : (j + 1) * 128]
    up_keep[...] = halves[core[0]]
    up_send[...] = halves[1 - core[0]]


def conv_backward(
    core, back, x, counts_row, s1, t1, p1, e2, s2, t2, p2, g1, d1, sp1, n1, h1, o1, g2, d2, sp2, n2, h2,
    keep, send,
    spatial_grad, wide, small, halves,
):
    counts = column_of(counts_row[...])
    taps1 = s1[...].astype(F32)
    taps2 = s2[...].astype(F32)
    frame1 = t1[...].astype(F32)
    frame2 = t2[...].astype(F32)

    def tile_sum(v):
        return jnp.sum(v.reshape(-1, 8, E), axis=0)

    small[...] = jnp.zeros(small.shape, F32)
    wide[...] = jnp.zeros(wide.shape, F32)
    got = back[...].reshape(DEVICES * 8, 128)
    row = lax.broadcasted_iota(jnp.int32, (DEVICES * 8, 1), 0)
    is_low = (row & 7) < CAPACITY
    got_f = got.astype(F32)
    tag = jnp.where(is_low, got_f[:, 96:97], got_f[:, 0:1]).astype(jnp.int32)
    named = tag == lax.broadcasted_iota(jnp.int32, (DEVICES * 8, ITEMS_HERE), 1)
    low = dot_tn((named & is_low).astype(F32).astype(BF), got)
    high = dot_tn((named & ~is_low).astype(F32).astype(BF), got)
    pooled_grad = jnp.concatenate([low[:, 0:96], high[:, 32:128]], axis=1)
    shared = pooled_grad / counts.astype(F32)
    out_grad = jnp.concatenate(
        [(shared * (f < counts).astype(F32)).astype(BF) for f in range(FRAMES)], axis=0
    )
    wide[576:768, 0:E] = dot_tn(out_grad, n2[...].reshape(FRAMES * ITEMS_HERE, E))
    summed_grad = dot_nn(out_grad, p2[...]).reshape(FRAMES, ITEMS_HERE, E) * h2[...].astype(F32)
    spread = []
    for f in range(FRAMES):
        total = summed_grad[f] * frame2[1]
        if f + 1 < FRAMES:
            total = total + summed_grad[f + 1] * frame2[0]
        if f > 0:
            total = total + summed_grad[f - 1] * frame2[2]
        spread.append(total)
    for k in range(3):
        total = jnp.zeros((8, E), F32)
        for f in range(FRAMES):
            if 0 <= f + k - 1 < FRAMES:
                total = total + tile_sum(sp2[f + k - 1].astype(F32) * summed_grad[f])
        small[21 + k] = total
    parts = []
    for f in range(FRAMES):
        for cell, tap in LINKS_SECOND:
            small[12 + tap] += tile_sum(g2[f * 4 + cell].astype(F32) * spread[f])
            parts.append((spread[f] * taps2[tap] * d2[f * 4 + cell].astype(F32)).astype(BF))
    grown_grad = jnp.concatenate(parts, axis=0)
    wide[384:576, 0:E] = dot_tn(o1[...], grown_grad)
    first_grad = dot_nt(grown_grad, e2[...]).astype(BF)
    wide[192:384, 0:E] = dot_tn(first_grad, n1[...].reshape(FRAMES * 4 * ITEMS_HERE, E))
    narrow_grad = dot_nn(first_grad, p1[...]).reshape(FRAMES, 4, ITEMS_HERE, E)
    summed_grad = [narrow_grad[f] * h1[f * 4 : f * 4 + 4].astype(F32) for f in range(FRAMES)]
    for k in range(3):
        total = jnp.zeros((8, E), F32)
        for f in range(FRAMES):
            if 0 <= f + k - 1 < FRAMES:
                total = total + tile_sum(sp1[f + k - 1].astype(F32) * summed_grad[f])
        small[9 + k] = total
    for f in range(FRAMES):
        total = summed_grad[f] * frame1[1]
        if f + 1 < FRAMES:
            total = total + summed_grad[f + 1] * frame1[0]
        if f > 0:
            total = total + summed_grad[f - 1] * frame1[2]
        spatial_grad[f] = total

    def grow_back(f, _):
        live = f < counts
        x_f = x[pl.ds(f * CELLS, CELLS)]
        x_f = jnp.where(live[None], x_f, jnp.zeros_like(x_f)).reshape(CELLS * ITEMS_HERE, C)
        sums = [jnp.zeros((8, E), F32)] * 9
        grads = [jnp.zeros((ITEMS_HERE, E), F32)] * CELLS
        for out_cell, in_cell, tap in LINKS_FIRST:
            from_out = spatial_grad[f, out_cell]
            grads[in_cell] = grads[in_cell] + from_out * taps1[tap]
            sums[tap] = sums[tap] + tile_sum(g1[f * CELLS + in_cell].astype(F32) * from_out)
        for tap in range(9):
            small[tap] += sums[tap]
        grads = [(grads[cell] * d1[f * CELLS + cell].astype(F32)).astype(BF) for cell in range(CELLS)]
        wide[0:192, 0:E] += dot_tn(x_f, jnp.concatenate(grads, axis=0))
        return 0

    lax.fori_loop(0, FRAMES, grow_back, 0)
    sums = jnp.sum(small[...], axis=1).astype(BF)
    put = lax.broadcasted_iota(jnp.int32, (32, 128), 1) == lax.broadcasted_iota(jnp.int32, (32, 128), 0) + 64
    wide[0:E, 384:512] += dot_tn(sums, put.astype(F32).astype(BF))
    for j in range(4):
        halves[j // 2, (j % 2) * 768 : (j % 2 + 1) * 768] = wide[:, j * 128 : (j + 1) * 128].astype(BF)
    keep[...] = halves[core[0]]
    send[...] = halves[1 - core[0]]


def merge(conv_a, conv_b, up_a, up_b, factors, out):
    conv = (conv_a[...].astype(F32) + conv_b[...].astype(F32)).astype(BF)
    up = (up_a[...].astype(F32) + up_b[...].astype(F32)).astype(BF)
    rows = [conv.reshape(CHIPS, 24, 128), up.reshape(CHIPS, 16, 128)]
    rows.append(jnp.broadcast_to(factors[...][None], (CHIPS, 40, 128)))
    out[...] = jnp.concatenate(rows, axis=1)


def sum_chips(third, out):
    total = jnp.sum(third[:, 0:40, :].astype(F32), axis=0).astype(BF)
    out[...] = jnp.broadcast_to(total[None], out.shape)


def finish_low_rank(own, other, third, third_other, grad_down, item_base):
    row = lax.broadcasted_iota(jnp.int32, (CHIPS * 8, 128), 0) & 7
    lane = lax.broadcasted_iota(jnp.int32, (CHIPS * 8, 128), 1)
    even = []
    for src in (own, other):
        parts = []
        for k in range(4):
            got = src[:, 32 + 8 * k : 40 + 8 * k, :].reshape(CHIPS * 8, 128).astype(F32)
            left = pltpu.roll(got, 64, 1)
            right = pltpu.roll(got, CHIPS * 8 - 4, 0)
            parts.append(jnp.where(row < 4, jnp.where(lane < 64, left, right), 0.0))
        even.append(jnp.concatenate(parts, axis=1))
    odd = jnp.concatenate([pltpu.roll(v, 4, 0) for v in even], axis=0).astype(BF)
    even = jnp.concatenate(even, axis=0).astype(BF)
    for j in range(5):
        cut = slice(40 + 8 * j, 48 + 8 * j)
        left = jnp.concatenate(
            [src[:, cut, :].reshape(CHIPS * 8, 128) for src in (third, third_other)], axis=0
        )
        first, second = dot_tn(left, even), dot_tn(left, odd)
        if j < 4:
            grad_down[j * 256 : j * 256 + 128] = first
            grad_down[j * 256 + 128 : j * 256 + 256] = second
        else:
            item_base[0:128] = first
            item_base[128:C] = second[0:64]


def finish(
    core, mine, theirs, item_base, project, up,
    ge1, gs1, gt1, gp1, ge2, gs2, gt2, gp2, grad_item, grad_up,
    halves,
):
    halves[core[0]] = mine[...]
    halves[1 - core[0]] = theirs[...]
    for j in range(4):
        width = min(128, E - j * 128)
        part = halves[j // 2, :, 0:24, :].reshape(1536, 128)[(j % 2) * 768 : (j % 2 + 1) * 768].astype(F32)
        cut = slice(j * 128, j * 128 + width)
        for i, out in enumerate((ge1, gp1, ge2, gp2)):
            out[:, cut] = part[i * 192 : (i + 1) * 192, 0:width]
    same = lax.broadcasted_iota(jnp.int32, (E, E), 0) == lax.broadcasted_iota(jnp.int32, (E, E), 1)
    small = dot_tn(part[0:E].astype(BF), same.astype(F32).astype(BF))
    gs1[...] = small[64:73]
    gt1[...] = small[73:76]
    gs2[...] = small[76:85]
    gt2[...] = small[85:88]
    item = item_base[...]
    for j in range(FH // 128):
        part = halves[j // 4, :, 24:40, :].reshape(1024, 128)[(j % 4) * 256 : (j % 4) * 256 + C]
        cut = slice(j * 128, (j + 1) * 128)
        grad_up[:, cut] = dot_tn(project[...], part)
        item = item + dot_nt(part, up[:, cut])
    grad_item[...] = item


def shape(dims, dtype=BF):
    return jax.ShapeDtypeStruct(dims, dtype)


def call(kernel, outs, scratch=(), smem=0, flops=10**9, moved=10**7):
    def run(*args):
        return pl.pallas_call(
            kernel,
            out_shape=outs,
            in_specs=[
                pl.BlockSpec(memory_space=pltpu.SMEM if i < smem else pltpu.VMEM)
                for i in range(len(args))
            ],
            out_specs=[pl.BlockSpec(memory_space=pltpu.VMEM)] * len(outs),
            scratch_shapes=list(scratch),
            cost_estimate=pl.CostEstimate(flops=flops, bytes_accessed=moved, transcendentals=10**6),
            compiler_params=pltpu.CompilerParams(vmem_limit_bytes=32 * 1024 * 1024),
        )(*args)

    return run


def local(
    clips, clip_counts, histories, lengths, user_cotangent,
    expand_first, spatial_first, temporal_first, project_first,
    expand_second, spatial_second, temporal_second, project_second,
    item_project, tower_up, tower_down,
):
    same_core = [[i for i in range(DEVICES) if i % 2 == c] for c in range(2)]
    core = (lax.axis_index("seq") % 2).reshape(1)

    def across_chips(v):
        return lax.all_to_all(v, AXES, 0, 0, axis_index_groups=same_core, tiled=True)

    def swap(v):
        return lax.ppermute(v, "seq", [(i, i ^ 1) for i in range(8)])

    x = clips.reshape(ITEMS_HERE, FRAMES * CELLS, C).transpose(1, 0, 2)
    counts = clip_counts.reshape(1, ITEMS_HERE)
    weights = (
        spatial_first, temporal_first, project_first.T,
        expand_second, spatial_second, temporal_second, project_second.T,
    )
    n = ITEMS_HERE
    framed = [pltpu.VMEM((FRAMES + 2, 4, n, E), F32), pltpu.VMEM((FRAMES + 2, n, E), F32)]
    (block,) = call(conv_forward, [shape((CHIPS, 64, 128))], framed, 1)(
        lengths, x, counts, user_cotangent, expand_first, *weights
    )
    kept = call(
        conv_forward,
        [
            shape((64, n, E)), shape((64, n, E)), shape((4, 4, n, E)), shape((16, n, E)), shape((16, n, E)),
            shape((512, C)), shape((16, n, E)), shape((16, n, E)), shape((4, n, E)), shape((4, n, E)), shape((4, n, E)),
        ],
        framed,
        1,
    )(lengths, x, counts, user_cotangent, expand_first, *weights)
    own = across_chips(block)
    other = swap(own)
    sent, *seen = call(
        tower,
        [shape((DEVICES, 8, 128)), shape((ROWS, 256)), shape((ROWS, D)), shape((ROWS, FH)), shape((ROWS, FH))],
        smem=2,
    )(core, lengths, own, other, histories, user_cotangent, item_project, tower_up, tower_down)
    back = lax.all_to_all(sent, AXES, 0, 0, tiled=True)
    up_keep, up_send, factors, user_vec = call(
        tower_sums,
        [shape((1024, 128)), shape((1024, 128)), shape((40, 128)), shape((USERS_HERE, D), F32)],
        [pltpu.VMEM((2, 1024, 128), BF)],
        2,
    )(core, lengths, *seen, tower_down)
    up_other = swap(up_send)
    conv_keep, conv_send = call(
        conv_backward,
        [shape((1536, 128)), shape((1536, 128))],
        [
            pltpu.VMEM((4, 4, n, E), F32),
            pltpu.VMEM((768, 512), F32),
            pltpu.VMEM((32, 8, E), F32),
            pltpu.VMEM((2, 1536, 128), BF),
        ],
        1,
    )(core, back, x, counts, *weights, *kept)
    (third,) = call(merge, [shape((CHIPS, 80, 128))])(conv_keep, swap(conv_send), up_keep, up_other, factors)
    third = across_chips(third)
    (fourth,) = call(sum_chips, [shape((CHIPS, 40, 128))])(third)
    fourth = across_chips(fourth)
    grad_down, item_base = call(finish_low_rank, [shape((FH, D), F32), shape((C, D), F32)])(
        own, other, third, swap(third)
    )
    *conv_grads, grad_item, grad_up = call(
        finish,
        [shape((C, E), F32), shape((9, E), F32), shape((3, E), F32), shape((C, E), F32)] * 2
        + [shape((C, D), F32), shape((D, FH), F32)],
        [pltpu.VMEM((2, CHIPS, 40, 128), BF)],
        1,
    )(core, fourth, swap(fourth), item_base, item_project, tower_up)
    conv_grads[3] = conv_grads[3].T
    conv_grads[7] = conv_grads[7].T
    return (user_vec, *conv_grads, grad_item, grad_up, grad_down)


def solution(mesh):
    spread = P(AXES)
    return jax.shard_map(
        local,
        mesh=mesh,
        in_specs=(spread,) * 5 + (P(),) * 11,
        out_specs=(spread,) + (P(),) * 11,
        check_vma=False,
    )
```

time: 171 us -> 163 us (0.953)
  local copies, waits for them, and re-layouts: 19.2 us -> 41.3 us
  waiting for transfers between devices: 17.4 us -> 3.79 us
  between operations: 14.1 us -> 1 us
  Pallas kernels: 34.2 us -> 26.5 us
  starting transfers between devices: 7.11 us -> 11.4 us
    unnamed x22 -> x131, local copies, waits for them, and re-layouts: 14.3 us -> 41.3 us
    all_to_all x1, waiting for transfers between devices: 16.6 us -> 0.01 us  [local(): back = lax.all_to_all(sent, AXES, 0, 0, tiled=True)]
    pallas_call x5 -> x9, Pallas kernels: 34.2 us -> 26.5 us  [run(): pl.pallas_call(kernel, out_shape=outs, in_specs=[pl.BlockSpec(memory_spac...]
    ppermute x1 -> x5, starting transfers between devices: 2.46 us -> 7.59 us  [swap(): return lax.ppermute(v, 'seq', [(i, i ^ 1) for i in range(8)])]
    ppermute x1 -> x5, waiting for transfers between devices: 0.85 us -> 3.79 us  [swap(): return lax.ppermute(v, 'seq', [(i, i ^ 1) for i in range(8)])]
    reshape x3 -> x0, local copies, waits for them, and re-layouts: 2.13 us -> none  [the longest x1 0.79 us: local(): histories.reshape(ROWS, 1)]
    broadcast_in_dim x3 -> x0, local copies, waits for them, and re-layouts: 2.02 us -> none  [the longest x1 0.98 us: local(): fourth = exchange(jnp.broadcast_to(conv_sum[None], (DEVICES, 24, 128)))]
  transfers between devices with their start and end apart: 3 -> 6, of which waited for: 2 -> 2; matrix products, arithmetic and copies ran while one was open for 5% -> 0% of each run, Pallas kernels for 7% -> 6%
where the time goes in v2:
time: 163 us; the launch traced here: 161 us
  blocking collectives  77.3 us (47%)
  local copies, waits for them, and re-layouts  41.3 us (25%)
  Pallas kernels  26.5 us (16%)
  starting transfers between devices  11.4 us (7%)
  waiting for transfers between devices  3.79 us (2%)
    all_to_all x3, blocking collectives, across_chips(): lax.all_to_all(v, AXES, 0, 0, axis_index_groups=same_core, tiled=True)  77.3 us
    unnamed x131, local copies, waits for them, and re-layouts  41.3 us
    pallas_call x9, Pallas kernels, run(): pl.pallas_call(kernel, out_shape=outs, in_specs=[pl.BlockSpec(memory_spac...  26.5 us
    ppermute x5, starting transfers between devices, swap(): return lax.ppermute(v, 'seq', [(i, i ^ 1) for i in range(8)])  7.59 us
    ppermute x5, waiting for transfers between devices, swap(): return lax.ppermute(v, 'seq', [(i, i ^ 1) for i in range(8)])  3.79 us
    all_to_all x1, starting transfers between devices, local(): back = lax.all_to_all(sent, AXES, 0, 0, tiled=True)  3.79 us
  transfers between devices with their start and end apart: 6, of which 2 were waited for; matrix products, arithmetic and copies ran while one was open for 0% of the time, Pallas kernels for 6%

profile of v2, /device:TPU:1, one launch (start us, length us, event | category | flops | bytes accessed | tf_op | source)
XLA Modules:
  0.0 161.3 jit_solution(6800090255774873351)
XLA Ops:
  0.8 2.0 %copy.28 = bf16[32,4,4,4,192]{4,0,3,2,1:T(8,128)(2,1)S(1)} copy(bf16[32,4,4,4,192]{4,3,2,1,0:T(4,128)(2,1)} %param.16) | data formatting | bytes 1572864 | tf_op args[0]
  2.9 3.8 %shard_map.247 = bf16[64,64,128]{2,1,0:T(8,128)(2,1)S(1)} custom-call(s32[4]{0:T(128)S(1)} %copy-done.52, bf16[64,32,192]{2,1,0:T(8,128)(2,1)S(1)} %bitcast.9, s32[1,32]{1,0:T(1,128)S(1)} %bitcast.18, f32[4,512]{1,0:T(4,128)S(1)} %copy-done.40, bf16[192,432]{1,0:T(8,128)(2,1)S(1)} %copy-done.61, bf16[9,432]{1,0:T(8,128)(2,1)S(1)} %copy-done.36, ...), custom_call_target="tpu_custom_call" | custom-call | flops 1000000000 | bytes 10000000 | tf_op jit(solution)/shard_map/pallas_call | solution.py:413
  6.7 29.0 %all_to_all.20.own = bf16[64,64,128]{2,1,0:T(8,128)(2,1)S(1)} all-to-all(bf16[64,64,128]{2,1,0:T(8,128)(2,1)S(1)} %shard_map.247), channel_id=1, replica_groups={{0,2,4,6,8,10,12,14,16,18,20,22,24,26,28,30,32,34,36,38,40,42,44,46,48,..., dimensions={0} | all-to-all | bytes 2097152 | tf_op jit(solution)/shard_map/all_to_all | solution.py:439
  35.6 2.5 %collective-permute-start = (bf16[64,64,128]{2,1,0:T(8,128)(2,1)S(1)}, bf16[64,64,128]{2,1,0:T(8,128)(2,1)S(1)}, u32[]{:S(2)}, u32[]{:S(2)}) collective-permute-start(bf16[64,64,128]{2,1,0:T(8,128)(2,1)S(1)} %all_to_all.20.own), channel_id=1, source_target_pairs={{0,1},{1,0},{2,3},{3,2},{4,5},{5,4},{6,7},{7,6},{8,9},{9,8},{10,11... | collective-permute-start | bytes 3145736 | tf_op jit(solution)/shard_map/ppermute | solution.py:442
  38.1 2.3 %collective-permute-done.other = bf16[64,64,128]{2,1,0:T(8,128)(2,1)S(1)} collective-permute-done((bf16[64,64,128]{2,1,0:T(8,128)(2,1)S(1)}, bf16[64,64,128]{2,1,0:T(8,128)(2,1)S(1)}, u32[]{:S(2)}, u32[]{:S(2)}) %collective-permute-start) | collective-permute-done | bytes 1048608 | tf_op jit(solution)/shard_map/ppermute | solution.py:442
  40.4 1.2 copy-done.4
  41.6 1.2 copy-done.6
  42.9 4.4 %shard_map.248 = (bf16[128,8,128]{2,1,0:T(8,128)(2,1)S(1)}, bf16[256,256]{1,0:T(8,128)(2,1)S(1)}, bf16[256,512]{1,0:T(8,128)(2,1)S(1)}, bf16[256,1024]{1,0:T(8,128)(2,1)S(1)}, bf16[256,1024]{1,0:T(8,128)(2,1)S(1)}) custom-call(s32[1]{0:T(128)} %bitcast.core, s32[4]{0:T(128)S(1)} %copy-done.52, bf16[64,64,128]{2,1,0:T(8,128)(2,1)S(1)} %all_to_all.20.own, ...), custom_call_target="tpu_custom_call" | custom-call | flops 1000000000 | bytes 10000000 | tf_op jit(solution)/shard_map/pallas_call | solution.py:413
  48.0 0.8 copy-done.55
  48.8 0.8 copy-done.57
  51.0 3.8 %all-to-all-start.1 = ((bf16[128,8,128]{2,1,0:T(8,128)(2,1)}), bf16[128,8,128]{2,1,0:T(8,128)(2,1)S(1)}, u32[]{:S(2)}, u32[]{:S(2)}) async-start(bf16[128,8,128]{2,1,0:T(8,128)(2,1)} %copy-done.20), calls=%async_computation.1 | async-start | bytes 524288 | tf_op jit(solution)/shard_map/all_to_all | solution.py:471
  54.8 0.9 copy-done.24
  55.7 0.9 copy-done.27
  56.6 0.9 copy-done.30
  57.6 0.7 copy-done.38
  61.7 0.9 copy-done.62
  62.6 4.5 %shard_map.250 = (bf16[64,32,432]{2,1,0:T(8,128)(2,1)S(1)}, bf16[64,32,432]{2,1,0:T(8,128)(2,1)S(1)}, bf16[4,4,32,432]{3,2,1,0:T(8,128)(2,1)S(1)}, bf16[16,32,43...) custom-call(s32[4]{0:T(128)S(1)} %copy-done.53, ...), custom_call_target="tpu_custom_call" | custom-call | flops 1000000000 | bytes 10000000 | tf_op jit(solution)/shard_map/pallas_call | solution.py:413
  67.1 1.3 copy-done
  68.4 1.3 copy-done.2
  69.7 0.8 copy-done.8
  70.5 0.8 copy-done.10
  71.3 0.8 copy-done.12
  72.1 0.8 copy-done.14
  72.9 0.8 copy-done.16
  75.7 1.6 copy-done.1
  77.3 1.6 copy-done.3
  78.9 1.0 copy-done.9
  79.9 1.0 copy-done.11
  81.0 1.0 copy-done.13
  82.0 1.0 copy-done.15
  83.1 1.0 copy-done.17
  84.1 0.9 copy-done.19
  85.1 0.9 copy-done.25
  86.0 0.9 copy-done.28
  86.9 0.9 copy-done.31
  87.8 0.9 copy-done.33
  88.7 0.9 copy-done.35
  89.7 0.7 copy-done.39
  92.4 5.0 %shard_map.251 = (bf16[1536,128]{1,0:T(8,128)(2,1)S(1)}, bf16[1536,128]{1,0:T(8,128)(2,1)S(1)}) custom-call(s32[1]{0:T(128)} %bitcast.core, bf16[128,8,128]{2,1,0:T(8,128)(2,1)S(1)} %all-to-all-done.1.back, bf16[64,32,192]{2,1,0:T(8,128)(2,1)S(1)} %bitcast.11, s32[1,32]{1,0:T(1,128)S(1)} %bitcast.20, bf16[9,432]{1,0:T(8,128)(2,1)S(1)} %copy-done.36, ...), custom_call_target="tpu_custom_call" | custom-call | flops 1000000000 | bytes 10000000 | tf_op jit(solution)/shard_map/pallas_call | solution.py:413
  97.4 1.5 collective-permute-start.1
  98.9 1.7 %shard_map.249 = (bf16[1024,128]{1,0:T(8,128)(2,1)S(1)}, bf16[1024,128]{1,0:T(8,128)(2,1)S(1)}, bf16[40,128]{1,0:T(8,128)(2,1)S(1)}, f32[4,512]{1,0:T(4,128)}) custom-call(s32[1]{0:T(128)} %bitcast.core, s32[4]{0:T(128)S(1)} %copy-done.54, bf16[256,256]{1,0:T(8,128)(2,1)S(1)} %copy-done.64, bf16[256,512]{1,0:T(8,128)(2,1)S(1)} %copy-done.60, ...), custom_call_target="tpu_custom_call" | custom-call | flops 1000000000 | bytes 10000000 | tf_op jit(solution)/shard_map/pallas_call | solution.py:413
  100.7 1.5 collective-permute-done.2.up_b
  102.4 29.8 %all_to_all.21.third = bf16[64,80,128]{2,1,0:T(8,128)(2,1)S(1)} all-to-all(bf16[64,80,128]{2,1,0:T(8,128)(2,1)S(1)} %shard_map.252), channel_id=1, replica_groups={{0,2,4,6,8,10,12,14,16,18,20,22,24,26,28,30,32,34,36,38,40,42,44,46,48,..., dimensions={0} | all-to-all | bytes 2621440 | tf_op jit(solution)/shard_map/all_to_all | solution.py:439
  132.3 2.0 %collective-permute-start.4 = (bf16[64,80,128]{2,1,0:T(8,128)(2,1)S(1)}, bf16[64,80,128]{2,1,0:T(8,128)(2,1)S(1)}, u32[]{:S(2)}, u32[]{:S(2)}) collective-permute-start(bf16[64,80,128]{2,1,0:T(8,128)(2,1)S(1)} %all_to_all.21.third), channel_id=1, source_target_pairs={{0,1},{1,0},{2,3},{3,2},{4,5},{5,4},{6,7},{7,6},{8,9},{9,8},{10,11... | collective-permute-start | bytes 3932168 | tf_op jit(solution)/shard_map/ppermute | solution.py:442
  134.4 18.5 %all_to_all.22.mine = bf16[64,40,128]{2,1,0:T(8,128)(2,1)S(1)} all-to-all(bf16[64,40,128]{2,1,0:T(8,128)(2,1)S(1)} %shard_map.253), channel_id=1, replica_groups={{0,2,4,6,8,10,12,14,16,18,20,22,24,26,28,30,32,34,36,38,40,42,44,46,48,..., dimensions={0} | all-to-all | bytes 1310720 | tf_op jit(solution)/shard_map/all_to_all | solution.py:439
  152.9 1.6 %collective-permute-start.3 = (bf16[64,40,128]{2,1,0:T(8,128)(2,1)S(1)}, bf16[64,40,128]{2,1,0:T(8,128)(2,1)S(1)}, u32[]{:S(2)}, u32[]{:S(2)}) collective-permute-start(bf16[64,40,128]{2,1,0:T(8,128)(2,1)S(1)} %all_to_all.22.mine), channel_id=1, source_target_pairs={{0,1},{1,0},{2,3},{3,2},{4,5},{5,4},{6,7},{7,6},{8,9},{9,8},{10,11... | collective-permute-start | bytes 1966088 | tf_op jit(solution)/shard_map/ppermute | solution.py:442
  154.6 3.4 %shard_map.254 = (f32[1024,512]{1,0:T(8,128)}, f32[192,512]{1,0:T(8,128)S(1)}) custom-call(bf16[64,64,128]{2,1,0:T(8,128)(2,1)S(1)} %all_to_all.20.own, bf16[64,64,128]{2,1,0:T(8,128)(2,1)S(1)} %collective-permute-done.other, bf16[64,80,128]{2,1,0:T(8,128)(2,1)S(1)} %all_to_all.21.third, bf16[64,80,128]{2,1,0:T(8,128)(2,1)S(1)} %collective-permute-done.4.third_other), custom_call_target="tpu_custom_call" | custom-call | flops 1000000000 | bytes 10000000 | tf_op jit(solution)/shard_map/pallas_call | solution.py:413
  158.0 3.3 %shard_map.255 = (f32[192,432]{1,0:T(8,128)}, f32[9,432]{1,0:T(8,128)}, f32[3,432]{1,0:T(4,128)}, f32[192,432]{1,0:T(8,128)}, f32[192,432]{1,0:T(8,128)}, /*inde...) custom-call(s32[1]{0:T(128)} %bitcast.core, ...), custom_call_target="tpu_custom_call" | custom-call | flops 1000000000 | bytes 10000000 | tf_op jit(solution)/shard_map/pallas_call | solution.py:413
  (107 shorter events, 10.1 us)
Async XLA Ops:
  0.6 2.1 %copy-start.52 = (s32[4]{0:T(128)S(1)}, s32[4]{0:T(128)}, u32[]{:S(2)}) copy-start(s32[4]{0:T(128)} %lengths.7) | copy-start | bytes 52
  0.7 2.1 %copy-start.45 = (bf16[3,432]{1,0:T(4,128)(2,1)S(1)}, bf16[3,432]{1,0:T(4,128)(2,1)}, u32[]{:S(2)}) copy-start(bf16[3,432]{1,0:T(4,128)(2,1)} %t2.5) | copy-start | bytes 7780
  0.7 2.1 %copy-start.37 = (bf16[9,432]{1,0:T(8,128)(2,1)S(1)}, bf16[9,432]{1,0:T(8,128)(2,1)}, u32[]{:S(2)}) copy-start(bf16[9,432]{1,0:T(8,128)(2,1)} %s2_.5) | copy-start | bytes 23332
  0.7 2.1 %copy-start.26 = (bf16[192,432]{1,0:T(8,128)(2,1)S(1)}, bf16[192,432]{1,0:T(8,128)(2,1)}, u32[]{:S(2)}) copy-start(bf16[192,432]{1,0:T(8,128)(2,1)} %e2.5) | copy-start | bytes 497668
  0.7 2.1 %copy-start.42 = (bf16[3,432]{1,0:T(4,128)(2,1)S(1)}, bf16[3,432]{1,0:T(4,128)(2,1)}, u32[]{:S(2)}) copy-start(bf16[3,432]{1,0:T(4,128)(2,1)} %t1.5) | copy-start | bytes 7780
  0.7 2.1 %copy-start.36 = (bf16[9,432]{1,0:T(8,128)(2,1)S(1)}, bf16[9,432]{1,0:T(8,128)(2,1)}, u32[]{:S(2)}) copy-start(bf16[9,432]{1,0:T(8,128)(2,1)} %s1_.5) | copy-start | bytes 23332
  0.7 2.1 %copy-start.40 = (f32[4,512]{1,0:T(4,128)S(1)}, f32[4,512]{1,0:T(4,128)}, u32[]{:S(2)}) copy-start(f32[4,512]{1,0:T(4,128)} %cot.5) | copy-start | bytes 24580
  0.7 2.1 %copy-start.61 = (bf16[192,432]{1,0:T(8,128)(2,1)S(1)}, bf16[192,432]{1,0:T(8,128)(2,1)}, u32[]{:S(2)}) copy-start(bf16[192,432]{1,0:T(8,128)(2,1)} %e1.3) | copy-start | bytes 497668
  0.7 2.1 %copy-start.29 = (bf16[432,192]{0,1:T(8,128)(2,1)S(1)}, bf16[432,192]{0,1:T(8,128)(2,1)}, u32[]{:S(2)}) copy-start(bf16[432,192]{0,1:T(8,128)(2,1)} %param.28) | copy-start | bytes 497668
  0.8 2.1 %copy-start.23 = (bf16[432,192]{0,1:T(8,128)(2,1)S(1)}, bf16[432,192]{0,1:T(8,128)(2,1)}, u32[]{:S(2)}) copy-start(bf16[432,192]{0,1:T(8,128)(2,1)} %param.24) | copy-start | bytes 497668
  0.8 2.1 %copy-start.49 = (s32[32]{0:T(128)S(1)}, s32[32]{0:T(128)}, u32[]{:S(2)}) copy-start(s32[32]{0:T(128)} %param.17) | copy-start | bytes 388
  2.9 37.5 %copy-start.21 = (bf16[192,512]{1,0:T(8,128)(2,1)S(1)}, bf16[192,512]{1,0:T(8,128)(2,1)}, u32[]{:S(2)}) copy-start(bf16[192,512]{1,0:T(8,128)(2,1)} %project.3) | copy-start | bytes 589828
  2.9 37.5 %copy-start.48 = (s32[4,64]{1,0:T(4,128)S(1)}, s32[4,64]{1,0:T(4,128)}, u32[]{:S(2)}) copy-start(s32[4,64]{1,0:T(4,128)} %ids_ref.1) | copy-start | bytes 3076
  35.6 4.8 %collective-permute-start = (bf16[64,64,128]{2,1,0:T(8,128)(2,1)S(1)}, bf16[64,64,128]{2,1,0:T(8,128)(2,1)S(1)}, u32[]{:S(2)}, u32[]{:S(2)}) collective-permute-start(bf16[64,64,128]{2,1,0:T(8,128)(2,1)S(1)} %all_to_all.20.own), channel_id=1, source_target_pairs={{0,1},{1,0},{2,3},{3,2},{4,5},{5,4},{6,7},{7,6},{8,9},{9,8},{10,11... | collective-permute-start | bytes 3145736 | tf_op jit(solution)/shard_map/ppermute | solution.py:442
  40.4 1.2 copy-start.4
  41.6 1.2 copy-start.6
  51.0 24.7 %all-to-all-start.1 = ((bf16[128,8,128]{2,1,0:T(8,128)(2,1)}), bf16[128,8,128]{2,1,0:T(8,128)(2,1)S(1)}, u32[]{:S(2)}, u32[]{:S(2)}) async-start(bf16[128,8,128]{2,1,0:T(8,128)(2,1)} %copy-done.20), calls=%async_computation.1 | async-start | bytes 524288 | tf_op jit(solution)/shard_map/all_to_all | solution.py:471
  54.8 0.9 copy-start.24
  55.7 0.9 copy-start.27
  56.6 0.9 copy-start.30
  61.7 0.9 copy-start.62
  67.1 1.3 copy-start
  68.4 1.3 copy-start.2
  75.7 1.6 copy-start.1
  77.3 1.6 copy-start.3
  78.9 1.0 copy-start.9
  79.9 1.0 copy-start.11
  81.0 1.0 copy-start.13
  82.0 1.0 copy-start.15
  83.1 1.0 copy-start.17
  84.1 0.9 copy-start.19
  85.1 0.9 copy-start.25
  86.0 0.9 copy-start.28
  86.9 0.9 copy-start.31
  87.8 0.9 copy-start.33
  88.7 0.9 copy-start.35
  92.4 6.5 %copy-start.5 = (bf16[1024,512]{1,0:T(8,128)(2,1)S(1)}, bf16[1024,512]{1,0:T(8,128)(2,1)}, u32[]{:S(2)}) copy-start(bf16[1024,512]{1,0:T(8,128)(2,1)} %down.3) | copy-start | bytes 3145732
  92.4 6.5 %copy-start.54 = (s32[4]{0:T(128)S(1)}, s32[4]{0:T(128)}, u32[]{:S(2)}) copy-start(s32[4]{0:T(128)} %lengths.7) | copy-start | bytes 52
  92.4 6.5 %copy-start.56 = (bf16[256,1024]{1,0:T(8,128)(2,1)S(1)}, bf16[256,1024]{1,0:T(8,128)(2,1)}, u32[]{:S(2)}) copy-start(bf16[256,1024]{1,0:T(8,128)(2,1)} %copy-done.55) | copy-start | bytes 1572868
  92.4 6.5 %copy-start.58 = (bf16[256,1024]{1,0:T(8,128)(2,1)S(1)}, bf16[256,1024]{1,0:T(8,128)(2,1)}, u32[]{:S(2)}) copy-start(bf16[256,1024]{1,0:T(8,128)(2,1)} %copy-done.57) | copy-start | bytes 1572868
  92.4 6.5 %copy-start.60 = (bf16[256,512]{1,0:T(8,128)(2,1)S(1)}, bf16[256,512]{1,0:T(8,128)(2,1)}, u32[]{:S(2)}) copy-start(bf16[256,512]{1,0:T(8,128)(2,1)} %copy-done.59) | copy-start | bytes 786436
  92.4 6.5 %copy-start.64 = (bf16[256,256]{1,0:T(8,128)(2,1)S(1)}, bf16[256,256]{1,0:T(8,128)(2,1)}, u32[]{:S(2)}) copy-start(bf16[256,256]{1,0:T(8,128)(2,1)} %copy-done.63) | copy-start | bytes 393220
  97.4 4.7 %collective-permute-start.1 = (bf16[1536,128]{1,0:T(8,128)(2,1)S(1)}, bf16[1536,128]{1,0:T(8,128)(2,1)S(1)}, u32[]{:S(2)}, u32[]{:S(2)}) collective-permute-start(bf16[1536,128]{1,0:T(8,128)(2,1)S(1)} %get-tuple-element.64), channel_id=1, source_target_pairs={{0,1},{1,0},{2,3},{3,2},{4,5},{5,4},{6,7},{7,6},{8,9},{9,8},{10,11... | collective-permute-start | bytes 1179656 | tf_op jit(solution)/shard_map/ppermute | solution.py:442
  100.6 1.5 collective-permute-start.2
  132.3 22.3 %collective-permute-start.4 = (bf16[64,80,128]{2,1,0:T(8,128)(2,1)S(1)}, bf16[64,80,128]{2,1,0:T(8,128)(2,1)S(1)}, u32[]{:S(2)}, u32[]{:S(2)}) collective-permute-start(bf16[64,80,128]{2,1,0:T(8,128)(2,1)S(1)} %all_to_all.21.third), channel_id=1, source_target_pairs={{0,1},{1,0},{2,3},{3,2},{4,5},{5,4},{6,7},{7,6},{8,9},{9,8},{10,11... | collective-permute-start | bytes 3932168 | tf_op jit(solution)/shard_map/ppermute | solution.py:442
  152.9 5.0 %copy-start.7 = (bf16[512,1024]{1,0:T(8,128)(2,1)S(1)}, bf16[512,1024]{1,0:T(8,128)(2,1)}, u32[]{:S(2)}) copy-start(bf16[512,1024]{1,0:T(8,128)(2,1)} %up.3) | copy-start | bytes 3145732
  152.9 5.0 %copy-start.22 = (bf16[192,512]{1,0:T(8,128)(2,1)S(1)}, bf16[192,512]{1,0:T(8,128)(2,1)}, u32[]{:S(2)}) copy-start(bf16[192,512]{1,0:T(8,128)(2,1)} %project.3) | copy-start | bytes 589828
  152.9 5.0 %collective-permute-start.3 = (bf16[64,40,128]{2,1,0:T(8,128)(2,1)S(1)}, bf16[64,40,128]{2,1,0:T(8,128)(2,1)S(1)}, u32[]{:S(2)}, u32[]{:S(2)}) collective-permute-start(bf16[64,40,128]{2,1,0:T(8,128)(2,1)S(1)} %all_to_all.22.mine), channel_id=1, source_target_pairs={{0,1},{1,0},{2,3},{3,2},{4,5},{5,4},{6,7},{7,6},{8,9},{9,8},{10,11... | collective-permute-start | bytes 1966088 | tf_op jit(solution)/shard_map/ppermute | solution.py:442
  (23 other events, 16.5 us)

commit v3 on v2

--- a/solution.py
+++ b/solution.py
@@ -65,7 +65,7 @@
     if len(kept) == 1:
         (block,) = kept
     else:
-        g1, d1, sp1, n1, h1, o1, g2, d2, sp2, n2, h2 = kept
+        taps, g1, d1, sp1, n1, h1, o1, g2, d2, sp2, n2, h2 = kept
     counts = column_of(counts_row[...])
     zero4 = jnp.zeros((HALF * HALF, ITEMS_HERE, E), F32)
     framed1[0] = zero4
@@ -77,6 +77,14 @@
     taps2 = s2[...].astype(F32)
     frame1 = t1[...].astype(F32)
     frame2 = t2[...].astype(F32)
+    if block is None:
+        taps[...] = jnp.zeros((56, E), F32)
+        for at, ref in ((0, s1), (9, t1), (12, s2), (21, t2)):
+            taps[at : at + ref.shape[0]] = ref[...].astype(F32)
+        taps[24:56, 0:128] = jnp.broadcast_to(counts.astype(F32), (ITEMS_HERE, 128))
+
+    if block is None:
+        x.ready(), e1.ready()
 
     def grow(f, _):
         live = f < counts
@@ -147,12 +155,12 @@
     shared = jnp.concatenate(pieces, axis=0)
     high = jnp.concatenate([pooled[:, 128:192], pooled[:, 0:64]], axis=1)
     rows = jnp.concatenate([pooled[:, 0:128], jnp.where(lane < 64, high, shared)], axis=0).astype(BF)
-    block[...] = jnp.broadcast_to(rows[None], block.shape)
+    block[...] = jnp.broadcast_to(rows[None], (CHIPS, 64, 128))
 
 
 def tower(
     core, lengths, own, other, ids_ref, cot, project, up, down,
-    sent, picked_out, fetched_out, act_out, pre_grad_out,
+    sent, picked_out, fetched_out, act_out, pre_grad_out, mixed_own, mixed_other,
 ):
     ids = jnp.concatenate([column_of(ids_ref[u : u + 1]) for u in range(USERS_HERE)], axis=0)
     owner = ids // ITEMS_HERE
@@ -169,6 +177,11 @@
         high = ref[:, 32:64, :].reshape(CHIPS * ITEMS_HERE, 128)
         return jnp.concatenate([low, high], axis=1)
 
+    own, other = own.ready(), other.ready()
+    for late in (project, up, down):
+        late.begin()
+    mixed_own.leave(own.at[:, 32:64, :])
+    mixed_other.leave(other.at[:, 32:64, :])
     picked = (dot_nn(pick_own, rows_of(own)) + dot_nn(pick_other, rows_of(other))).astype(BF)
     fetched = dot_nn(picked[:, 0:C], project[...]).astype(BF)
     pre = dot_nn(fetched, up[...])
@@ -179,6 +192,8 @@
     picked_out[...] = picked
     fetched_out[...] = fetched
     act_out[...] = (pre * gate).astype(BF)
+    for out in (picked_out, fetched_out, act_out):
+        out.leave()
     slope = gate + 0.5 * pre * (1.0 - bent * bent) * (scale * (1.0 + 3 * 0.044715 * square))
     _, length = per_user(lengths)
     shared = cot[...] / length[0:4].astype(F32)
@@ -192,6 +207,7 @@
         base_parts.append(alive * shared[u : u + 1])
     pre_grad = jnp.concatenate(pre_parts, axis=0).astype(BF)
     pre_grad_out[...] = pre_grad
+    pre_grad_out.leave()
     rows_grad = jnp.concatenate(base_parts, axis=0) + dot_nt(pre_grad, up[...])
     rows_coarse = rows_grad.astype(BF)
     rows_fine = (rows_grad - rows_coarse.astype(F32)).astype(BF)
@@ -227,7 +243,7 @@
     picked_sum = dot_nn(live, picked[...])
     pieces = [act_sum[0:4, j * 128 : (j + 1) * 128] for j in range(8)]
     pieces += [picked_sum[0:4, j * 128 : (j + 1) * 128] for j in range(2)]
-    factors[...] = jnp.concatenate(pieces, axis=0).astype(BF)
+    factors[...] = jnp.concatenate(pieces + [jnp.zeros((8, 128), F32)], axis=0).astype(BF)
     coarse = act_sum.astype(BF)
     fine = (act_sum - coarse.astype(F32)).astype(BF)
     mixed = dot_nn(live, fetched[...]) + dot_nn(coarse, down[...]) + dot_nn(fine, down[...])
@@ -235,20 +251,21 @@
     up_grad = dot_tn(picked[...], pre_grad[...]).astype(BF)
     for j in range(FH // 128):
         halves[j // 4, (j % 4) * 256 : (j % 4 + 1) * 256] = up_grad[:, j * 128 : (j + 1) * 128]
-    up_keep[...] = halves[core[0]]
-    up_send[...] = halves[1 - core[0]]
+    up_keep.leave(halves.at[core[0]])
+    up_send.leave(halves.at[1 - core[0]])
 
 
 def conv_backward(
-    core, back, x, counts_row, s1, t1, p1, e2, s2, t2, p2, g1, d1, sp1, n1, h1, o1, g2, d2, sp2, n2, h2,
+    core, back, taps, n2, p2, h2, sp2, g2, d2, o1, e2, n1, p1, h1, sp1, x, g1, d1,
     keep, send,
     spatial_grad, wide, small, halves,
 ):
-    counts = column_of(counts_row[...])
-    taps1 = s1[...].astype(F32)
-    taps2 = s2[...].astype(F32)
-    frame1 = t1[...].astype(F32)
-    frame2 = t2[...].astype(F32)
+    taps1, frame1, taps2, frame2 = taps[0:9], taps[9:12], taps[12:21], taps[21:24]
+    counts = taps[24:56, 0:1]
+    for late in (n2, p2, h2, sp2, g2, d2, o1, e2):
+        late.ready()
+    for late in (x, g1, d1):
+        late.begin()
 
     def tile_sum(v):
         return jnp.sum(v.reshape(-1, 8, E), axis=0)
@@ -264,9 +281,9 @@
     low = dot_tn((named & is_low).astype(F32).astype(BF), got)
     high = dot_tn((named & ~is_low).astype(F32).astype(BF), got)
     pooled_grad = jnp.concatenate([low[:, 0:96], high[:, 32:128]], axis=1)
-    shared = pooled_grad / counts.astype(F32)
+    shared = pooled_grad / counts
     out_grad = jnp.concatenate(
-        [(shared * (f < counts).astype(F32)).astype(BF) for f in range(FRAMES)], axis=0
+        [(shared * (counts > f).astype(F32)).astype(BF) for f in range(FRAMES)], axis=0
     )
     wide[576:768, 0:E] = dot_tn(out_grad, n2[...].reshape(FRAMES * ITEMS_HERE, E))
     summed_grad = dot_nn(out_grad, p2[...]).reshape(FRAMES, ITEMS_HERE, E) * h2[...].astype(F32)
@@ -309,8 +326,10 @@
             total = total + summed_grad[f - 1] * frame1[2]
         spatial_grad[f] = total
 
+    x.ready(), g1.ready(), d1.ready()
+
     def grow_back(f, _):
-        live = f < counts
+        live = counts > lax.convert_element_type(f, F32)
         x_f = x[pl.ds(f * CELLS, CELLS)]
         x_f = jnp.where(live[None], x_f, jnp.zeros_like(x_f)).reshape(CELLS * ITEMS_HERE, C)
         sums = [jnp.zeros((8, E), F32)] * 9
@@ -338,24 +357,26 @@
 def merge(conv_a, conv_b, up_a, up_b, factors, out):
     conv = (conv_a[...].astype(F32) + conv_b[...].astype(F32)).astype(BF)
     up = (up_a[...].astype(F32) + up_b[...].astype(F32)).astype(BF)
-    rows = [conv.reshape(CHIPS, 24, 128), up.reshape(CHIPS, 16, 128)]
-    rows.append(jnp.broadcast_to(factors[...][None], (CHIPS, 40, 128)))
-    out[...] = jnp.concatenate(rows, axis=1)
-
-
-def sum_chips(third, out):
+    out[:, 0:24, :] = conv.reshape(CHIPS, 24, 128)
+    out[:, 24:40, :] = up.reshape(CHIPS, 16, 128)
+    out[:, 40:80, :] = jnp.broadcast_to(factors[0:40][None], (CHIPS, 40, 128))
+
+
+def sum_chips(third, out, factors):
+    factors[...] = third[:, 40:80, :]
+    factors.leave()
     total = jnp.sum(third[:, 0:40, :].astype(F32), axis=0).astype(BF)
-    out[...] = jnp.broadcast_to(total[None], out.shape)
-
-
-def finish_low_rank(own, other, third, third_other, grad_down, item_base):
+    out[...] = jnp.broadcast_to(total[None], (CHIPS, 40, 128))
+
+
+def finish_low_rank(own, other, factors, factors_other, grad_down, item_base):
     row = lax.broadcasted_iota(jnp.int32, (CHIPS * 8, 128), 0) & 7
     lane = lax.broadcasted_iota(jnp.int32, (CHIPS * 8, 128), 1)
     even = []
     for src in (own, other):
         parts = []
         for k in range(4):
-            got = src[:, 32 + 8 * k : 40 + 8 * k, :].reshape(CHIPS * 8, 128).astype(F32)
+            got = src[:, 8 * k : 8 * k + 8, :].reshape(CHIPS * 8, 128).astype(F32)
             left = pltpu.roll(got, 64, 1)
             right = pltpu.roll(got, CHIPS * 8 - 4, 0)
             parts.append(jnp.where(row < 4, jnp.where(lane < 64, left, right), 0.0))
@@ -363,9 +384,9 @@
     odd = jnp.concatenate([pltpu.roll(v, 4, 0) for v in even], axis=0).astype(BF)
     even = jnp.concatenate(even, axis=0).astype(BF)
     for j in range(5):
-        cut = slice(40 + 8 * j, 48 + 8 * j)
+        cut = slice(8 * j, 8 * j + 8)
         left = jnp.concatenate(
-            [src[:, cut, :].reshape(CHIPS * 8, 128) for src in (third, third_other)], axis=0
+            [src[:, cut, :].reshape(CHIPS * 8, 128) for src in (factors, factors_other)], axis=0
         )
         first, second = dot_tn(left, even), dot_tn(left, odd)
         if j < 4:
@@ -390,6 +411,8 @@
         for i, out in enumerate((ge1, gp1, ge2, gp2)):
             out[:, cut] = part[i * 192 : (i + 1) * 192, 0:width]
     same = lax.broadcasted_iota(jnp.int32, (E, E), 0) == lax.broadcasted_iota(jnp.int32, (E, E), 1)
+    for out in (ge1, gp1, ge2, gp2):
+        out.leave()
     small = dot_tn(part[0:E].astype(BF), same.astype(F32).astype(BF))
     gs1[...] = small[64:73]
     gt1[...] = small[73:76]
@@ -408,19 +431,78 @@
     return jax.ShapeDtypeStruct(dims, dtype)
 
 
-def call(kernel, outs, scratch=(), smem=0, flops=10**9, moved=10**7):
+class Arriving:
+    def __init__(self, copy, ref):
+        self.copy, self.ref, self.begun = copy, ref, False
+
+    def begin(self):
+        if not self.begun:
+            self.copy.start()
+            self.begun = True
+
+    def ready(self):
+        if self.copy is not None:
+            self.begin()
+            self.copy.wait()
+            self.copy = None
+        return self.ref
+
+    def __getitem__(self, index):
+        return self.ready()[index]
+
+
+class Leaving:
+    def __init__(self, ref, target, semaphore):
+        self.ref, self.target, self.semaphore, self.copy = ref, target, semaphore, None
+
+    def __setitem__(self, index, value):
+        self.ref[index] = value
+
+    def leave(self, source=None):
+        source = self.ref if source is None else source
+        self.copy = pltpu.make_async_copy(source, self.target, self.semaphore)
+        self.copy.start()
+
+
+def call(kernel, outs, places, out_places, scratch=(), unstaged=(), megabytes=58):
+    staged_in = [i for i, p in enumerate(places) if p in "hw"]
+    staged_out = [i for i, p in enumerate(out_places) if p == "h"]
+    spaces = {"s": pltpu.SMEM, "v": pltpu.VMEM, "h": pl.ANY, "w": pl.ANY}
+
     def run(*args):
+        stages = [pltpu.VMEM(args[i].shape, args[i].dtype) for i in staged_in]
+        stages += [pltpu.VMEM((16, 128) if i in unstaged else outs[i].shape, outs[i].dtype) for i in staged_out]
+        sems = [pltpu.SemaphoreType.DMA((max(len(v), 1),)) for v in (staged_in, staged_out)]
+
+        def body(*refs):
+            ins, rest = list(refs[: len(args)]), list(refs[len(args) :])
+            results, rest = rest[: len(outs)], rest[len(outs) :]
+            own, rest = rest[: len(scratch)], rest[len(scratch) :]
+            sem_in, sem_out = rest[-2:]
+            for k, i in enumerate(staged_in):
+                copy = pltpu.make_async_copy(ins[i], rest[k], sem_in.at[k])
+                ins[i] = Arriving(copy, rest[k])
+                if places[i] == "h":
+                    ins[i].begin()
+            for k, i in enumerate(staged_out):
+                results[i] = Leaving(rest[len(staged_in) + k], results[i], sem_out.at[k])
+            kernel(*ins, *results, *own)
+            for i in staged_in:
+                ins[i].ready()
+            for i in staged_out:
+                if results[i].copy is None:
+                    results[i].leave()
+            for i in staged_out:
+                results[i].copy.wait()
+
         return pl.pallas_call(
-            kernel,
+            body,
             out_shape=outs,
-            in_specs=[
-                pl.BlockSpec(memory_space=pltpu.SMEM if i < smem else pltpu.VMEM)
-                for i in range(len(args))
-            ],
-            out_specs=[pl.BlockSpec(memory_space=pltpu.VMEM)] * len(outs),
-            scratch_shapes=list(scratch),
-            cost_estimate=pl.CostEstimate(flops=flops, bytes_accessed=moved, transcendentals=10**6),
-            compiler_params=pltpu.CompilerParams(vmem_limit_bytes=32 * 1024 * 1024),
+            in_specs=[pl.BlockSpec(memory_space=spaces[p]) for p in places],
+            out_specs=[pl.BlockSpec(memory_space=spaces[p]) for p in out_places],
+            scratch_shapes=list(scratch) + stages + sems,
+            cost_estimate=pl.CostEstimate(flops=10**9, bytes_accessed=10**7, transcendentals=10**6),
+            compiler_params=pltpu.CompilerParams(vmem_limit_bytes=megabytes * 1024 * 1024),
         )(*args)
 
     return run
@@ -449,57 +531,77 @@
     )
     n = ITEMS_HERE
     framed = [pltpu.VMEM((FRAMES + 2, 4, n, E), F32), pltpu.VMEM((FRAMES + 2, n, E), F32)]
-    (block,) = call(conv_forward, [shape((CHIPS, 64, 128))], framed, 1)(
+    (block,) = call(conv_forward, [shape((CHIPS, 64, 128))], "svvvvvvvvvvv", "v", framed, megabytes=24)(
         lengths, x, counts, user_cotangent, expand_first, *weights
     )
-    kept = call(
+    taps, g1, d1, sp1, n1, h1, o1, g2, d2, sp2, n2, h2 = call(
         conv_forward,
         [
+            shape((56, E), F32),
             shape((64, n, E)), shape((64, n, E)), shape((4, 4, n, E)), shape((16, n, E)), shape((16, n, E)),
             shape((512, C)), shape((16, n, E)), shape((16, n, E)), shape((4, n, E)), shape((4, n, E)), shape((4, n, E)),
         ],
+        "shvvhvvhhvvh",
+        "h" * 12,
         framed,
-        1,
     )(lengths, x, counts, user_cotangent, expand_first, *weights)
     own = across_chips(block)
-    other = swap(own)
-    sent, *seen = call(
+    own, taps = lax.optimization_barrier((own, taps))
+    sent, *seen, mixed_own, mixed_other = call(
         tower,
-        [shape((DEVICES, 8, 128)), shape((ROWS, 256)), shape((ROWS, D)), shape((ROWS, FH)), shape((ROWS, FH))],
-        smem=2,
-    )(core, lengths, own, other, histories, user_cotangent, item_project, tower_up, tower_down)
+        [
+            shape((DEVICES, 8, 128)), shape((ROWS, 256)), shape((ROWS, D)), shape((ROWS, FH)), shape((ROWS, FH)),
+            shape((CHIPS, 32, 128)), shape((CHIPS, 32, 128)),
+        ],
+        "sshhvvwww",
+        "hhhhhhh",
+        unstaged=(5, 6),
+    )(core, lengths, own, swap(own), histories, user_cotangent, item_project, tower_up, tower_down)
     back = lax.all_to_all(sent, AXES, 0, 0, tiled=True)
     up_keep, up_send, factors, user_vec = call(
         tower_sums,
-        [shape((1024, 128)), shape((1024, 128)), shape((40, 128)), shape((USERS_HERE, D), F32)],
+        [shape((1024, 128)), shape((1024, 128)), shape((48, 128)), shape((USERS_HERE, D), F32)],
+        "sshhhhh",
+        "hhhv",
         [pltpu.VMEM((2, 1024, 128), BF)],
-        2,
+        unstaged=(0, 1),
     )(core, lengths, *seen, tower_down)
+    back, up_send = lax.optimization_barrier((back, up_send))
     up_other = swap(up_send)
     conv_keep, conv_send = call(
         conv_backward,
         [shape((1536, 128)), shape((1536, 128))],
+        "sv" + "h" * 13 + "www",
+        "vv",
         [
             pltpu.VMEM((4, 4, n, E), F32),
             pltpu.VMEM((768, 512), F32),
             pltpu.VMEM((32, 8, E), F32),
             pltpu.VMEM((2, 1536, 128), BF),
         ],
-        1,
-    )(core, back, x, counts, *weights, *kept)
-    (third,) = call(merge, [shape((CHIPS, 80, 128))])(conv_keep, swap(conv_send), up_keep, up_other, factors)
+    )(
+        core, back, taps, n2, weights[6], h2, sp2, g2, d2, o1, weights[3], n1, weights[2], h1, sp1, x, g1, d1,
+    )
+    (third,) = call(merge, [shape((CHIPS, 80, 128))], "vvvvv", "v", megabytes=16)(
+        conv_keep, swap(conv_send), up_keep, up_other, factors
+    )
     third = across_chips(third)
-    (fourth,) = call(sum_chips, [shape((CHIPS, 40, 128))])(third)
+    fourth, factors = call(
+        sum_chips, [shape((CHIPS, 40, 128)), shape((CHIPS, 40, 128))], "v", "vh", megabytes=16
+    )(third)
     fourth = across_chips(fourth)
-    grad_down, item_base = call(finish_low_rank, [shape((FH, D), F32), shape((C, D), F32)])(
-        own, other, third, swap(third)
+    grad_down, item_base = call(finish_low_rank, [shape((FH, D), F32), shape((C, D), F32)], "hhhh", "hh")(
+        mixed_own, mixed_other, factors, swap(factors)
     )
+    fourth, item_base = lax.optimization_barrier((fourth, item_base))
     *conv_grads, grad_item, grad_up = call(
         finish,
         [shape((C, E), F32), shape((9, E), F32), shape((3, E), F32), shape((C, E), F32)] * 2
         + [shape((C, D), F32), shape((D, FH), F32)],
+        "svvhhh",
+        "hvvhhvvhhh",
         [pltpu.VMEM((2, CHIPS, 40, 128), BF)],
-        1,
+        megabytes=32,
     )(core, fourth, swap(fourth), item_base, item_project, tower_up)
     conv_grads[3] = conv_grads[3].T
     conv_grads[7] = conv_grads[7].T

time: 163 us -> 136 us (0.83)
  blocking collectives: 77.3 us -> 24.5 us
  local copies, waits for them, and re-layouts: 41.3 us -> 6.61 us
  waiting for transfers between devices: 3.79 us -> 28.1 us
  Pallas kernels: 26.5 us -> 46.5 us
  starting transfers between devices: 11.4 us -> 28.1 us
    all_to_all x3 -> x1, blocking collectives: 77.3 us -> 24.5 us  [across_chips(): lax.all_to_all(v, AXES, 0, 0, axis_index_groups=same_core, tiled=True)]
    unnamed x131 -> x49, local copies, waits for them, and re-layouts: 41.3 us -> 6.61 us
    pallas_call x9, Pallas kernels: 26.5 us -> 46.5 us  [run(): pl.pallas_call(body, out_shape=outs, in_specs=[pl.BlockSpec(memory_space=...]
    all_to_all x0 -> x2, starting transfers between devices: none -> 16.6 us  [across_chips(): lax.all_to_all(v, AXES, 0, 0, axis_index_groups=same_core, tiled=True)]
    all_to_all x0 -> x2, waiting for transfers between devices: none -> 16 us  [across_chips(): lax.all_to_all(v, AXES, 0, 0, axis_index_groups=same_core, tiled=True)]
    all_to_all x1, waiting for transfers between devices: 0.01 us -> 6.42 us  [local(): back = lax.all_to_all(sent, AXES, 0, 0, tiled=True)]
    ppermute x5, waiting for transfers between devices: 3.79 us -> 5.64 us  [swap(): return lax.ppermute(v, 'seq', [(i, i ^ 1) for i in range(8)])]
  transfers between devices with their start and end apart: 6 -> 8, of which waited for: 2 -> 6; matrix products, arithmetic and copies ran while one was open for 0% -> 0% of each run, Pallas kernels for 6% -> 14%
where the time goes in v3:
time: 136 us; the launch traced here: 135 us
  Pallas kernels  46.5 us (34%)
  starting transfers between devices  28.1 us (21%)
  waiting for transfers between devices  28.1 us (21%)
  blocking collectives  24.5 us (18%)
  local copies, waits for them, and re-layouts  6.61 us (5%)
    pallas_call x9, Pallas kernels, run(): pl.pallas_call(body, out_shape=outs, in_specs=[pl.BlockSpec(memory_space=...  46.5 us
    all_to_all x1, blocking collectives, across_chips(): lax.all_to_all(v, AXES, 0, 0, axis_index_groups=same_core, tiled=True)  24.5 us
    all_to_all x2, starting transfers between devices, across_chips(): lax.all_to_all(v, AXES, 0, 0, axis_index_groups=same_core, tiled=True)  16.6 us
    all_to_all x2, waiting for transfers between devices, across_chips(): lax.all_to_all(v, AXES, 0, 0, axis_index_groups=same_core, tiled=True)  16 us
    ppermute x5, starting transfers between devices, swap(): return lax.ppermute(v, 'seq', [(i, i ^ 1) for i in range(8)])  7.67 us
    unnamed x49, local copies, waits for them, and re-layouts  6.61 us
    all_to_all x1, waiting for transfers between devices, local(): back = lax.all_to_all(sent, AXES, 0, 0, tiled=True)  6.42 us
    ppermute x5, waiting for transfers between devices, swap(): return lax.ppermute(v, 'seq', [(i, i ^ 1) for i in range(8)])  5.64 us
  transfers between devices with their start and end apart: 8, of which 6 were waited for; matrix products, arithmetic and copies ran while one was open for 0% of the time, Pallas kernels for 14%

profile of v3, /device:TPU:1, one launch (start us, length us, event | category | flops | bytes accessed | tf_op | source)
XLA Modules:
  0.0 134.9 jit_solution(17549271224283276153)
XLA Ops:
  0.6 0.0 copy-start.7
  0.7 0.0 copy-start.4
  0.7 0.0 copy-start.6
  0.7 0.0 copy-start.14
  0.7 0.0 copy-start.12
  0.7 0.0 copy-start.13
  0.7 0.0 copy-start.11
  0.7 0.0 copy-start.10
  0.7 0.0 copy-start.5
  0.8 0.0 copy-start.3
  0.8 0.0 copy-start.15
  0.8 2.0 %copy.28 = bf16[32,4,4,4,192]{4,0,3,2,1:T(8,128)(2,1)S(1)} copy(bf16[32,4,4,4,192]{4,3,2,1,0:T(4,128)(2,1)} %param.16) | data formatting | bytes 1572864 | tf_op args[0]
  2.8 0.0 copy-start
  2.8 0.0 copy-done.7
  2.9 4.8 %shard_map.247 = bf16[64,64,128]{2,1,0:T(8,128)(2,1)} custom-call(s32[4]{0:T(128)S(1)} %copy-done.7, bf16[64,32,192]{2,1,0:T(8,128)(2,1)S(1)} %bitcast.9, s32[1,32]{1,0:T(1,128)S(1)} %bitcast.19, f32[4,512]{1,0:T(4,128)S(1)} %copy-done.6, bf16[192,432]{1,0:T(8,128)(2,1)S(1)} %copy-done.10, bf16[9,432]{1,0:T(8,128)(2,1)S(1)} %copy-done.11, ...), custom_call_target="tpu_custom_call" | custom-call | flops 1000000000 | bytes 10000000 | tf_op jit(solution)/shard_map/pallas_call | solution.py:498
  7.7 0.0 copy-done
  7.7 12.0 %all-to-all-start = ((bf16[64,64,128]{2,1,0:T(8,128)(2,1)}), bf16[64,64,128]{2,1,0:T(8,128)(2,1)S(1)}, u32[]{:S(2)}, u32[]{:S(2)}) async-start(bf16[64,64,128]{2,1,0:T(8,128)(2,1)} %shard_map.247), calls=%async_computation | async-start | bytes 2097152 | tf_op jit(solution)/shard_map/all_to_all | solution.py:521
  19.7 9.6 %shard_map.248 = (f32[56,432]{1,0:T(8,128)}, bf16[64,32,432]{2,1,0:T(8,128)(2,1)}, bf16[64,32,432]{2,1,0:T(8,128)(2,1)}, bf16[4,4,32,432]{3,2,1,0:T(8,128)(2,1)}...) custom-call(s32[4]{0:T(128)} %refs_1_.3, ...), custom_call_target="tpu_custom_call" | custom-call | flops 1000000000 | bytes 10000000 | tf_op jit(solution)/shard_map/pallas_call | solution.py:498
  29.2 7.6 %all-to-all-done.refs_2_ = bf16[64,64,128]{2,1,0:T(8,128)(2,1)S(1)} async-done(((bf16[64,64,128]{2,1,0:T(8,128)(2,1)}), bf16[64,64,128]{2,1,0:T(8,128)(2,1)S(1)}, u32[]{:S(2)}, u32[]{:S(2)}) %all-to-all-start) | async-done | bytes 1048608 | tf_op jit(solution)/shard_map/all_to_all | solution.py:521
  36.9 2.5 %collective-permute-start = (bf16[64,64,128]{2,1,0:T(8,128)(2,1)S(1)}, bf16[64,64,128]{2,1,0:T(8,128)(2,1)S(1)}, u32[]{:S(2)}, u32[]{:S(2)}) collective-permute-start(bf16[64,64,128]{2,1,0:T(8,128)(2,1)S(1)} %all-to-all-done.refs_2_), channel_id=1, source_target_pairs={{0,1},{1,0},{2,3},{3,2},{4,5},{5,4},{6,7},{7,6},{8,9},{9,8},{10,11... | collective-permute-start | bytes 3145736 | tf_op jit(solution)/shard_map/ppermute | solution.py:524
  39.3 2.3 %collective-permute-done.refs_3_ = bf16[64,64,128]{2,1,0:T(8,128)(2,1)S(1)} collective-permute-done((bf16[64,64,128]{2,1,0:T(8,128)(2,1)S(1)}, bf16[64,64,128]{2,1,0:T(8,128)(2,1)S(1)}, u32[]{:S(2)}, u32[]{:S(2)}) %collective-permute-start) | collective-permute-done | bytes 1048608 | tf_op jit(solution)/shard_map/ppermute | solution.py:524
  41.6 1.0 copy-done.20
  42.6 7.6 %shard_map.249 = (bf16[128,8,128]{2,1,0:T(8,128)(2,1)}, bf16[256,256]{1,0:T(8,128)(2,1)}, bf16[256,512]{1,0:T(8,128)(2,1)}, bf16[256,1024]{1,0:T(8,128)(2,1)}, b...) custom-call(s32[1]{0:T(128)} %bitcast.refs_0_, s32[4]{0:T(128)} %refs_1_.3, ...), custom_call_target="tpu_custom_call" | custom-call | flops 1000000000 | bytes 10000000 | tf_op jit(solution)/shard_map/pallas_call | solution.py:498
  50.2 3.8 %all-to-all-start.1 = ((bf16[128,8,128]{2,1,0:T(8,128)(2,1)}), bf16[128,8,128]{2,1,0:T(8,128)(2,1)S(1)}, u32[]{:S(2)}, u32[]{:S(2)}) async-start(bf16[128,8,128]{2,1,0:T(8,128)(2,1)} %get-tuple-element.64), calls=%async_computation.1 | async-start | bytes 524288 | tf_op jit(solution)/shard_map/all_to_all | solution.py:560
  54.0 4.6 %shard_map.250 = (bf16[1024,128]{1,0:T(8,128)(2,1)}, bf16[1024,128]{1,0:T(8,128)(2,1)}, bf16[48,128]{1,0:T(8,128)(2,1)}, f32[4,512]{1,0:T(4,128)}) custom-call(s32[1]{0:T(128)} %bitcast.refs_0_, s32[4]{0:T(128)} %refs_1_.3, bf16[256,256]{1,0:T(8,128)(2,1)} %get-tuple-element.59.refs_2_, bf16[256,512]{1,0:T(8,128)(2,1)} %get-tuple-element.60.refs_3_, ...), custom_call_target="tpu_custom_call" | custom-call | flops 1000000000 | bytes 10000000 | tf_op jit(solution)/shard_map/pallas_call | solution.py:498
  58.6 6.4 %all-to-all-done.1.refs_1_ = bf16[128,8,128]{2,1,0:T(8,128)(2,1)S(1)} async-done(((bf16[128,8,128]{2,1,0:T(8,128)(2,1)}), bf16[128,8,128]{2,1,0:T(8,128)(2,1)S(1)}, u32[]{:S(2)}, u32[]{:S(2)}) %all-to-all-start.1) | async-done | bytes 262176 | tf_op jit(solution)/shard_map/all_to_all | solution.py:560
  65.0 0.7 copy-done.21
  65.7 9.3 %shard_map.251 = (bf16[1536,128]{1,0:T(8,128)(2,1)}, bf16[1536,128]{1,0:T(8,128)(2,1)}) custom-call(s32[1]{0:T(128)} %bitcast.refs_0_, bf16[128,8,128]{2,1,0:T(8,128)(2,1)} %copy-done.21, f32[56,432]{1,0:T(8,128)} %get-tuple-element.67.refs_2_, bf16[4,32,432]{2,1,0:T(8,128)(2,1)} %get-tuple-element.68.refs_3_, bf16[192,432]{1,0:T(8,128)(2,1)} %bitcast.16, ...), custom_call_target="tpu_custom_call" | custom-call | flops 1000000000 | bytes 10000000 | tf_op jit(solution)/shard_map/pallas_call | solution.py:498
  75.0 1.2 collective-permute-start.1
  76.2 0.1 collective-permute-start.2
  76.3 1.6 %collective-permute-done.2.refs_3_ = bf16[1024,128]{1,0:T(8,128)(2,1)S(1)} collective-permute-done((bf16[1024,128]{1,0:T(8,128)(2,1)S(1)}, bf16[1024,128]{1,0:T(8,128)(2,1)S(1)}, u32[]{:S(2)}, u32[]{:S(2)}) %collective-permute-start.2) | collective-permute-done | bytes 262176 | tf_op jit(solution)/shard_map/ppermute | solution.py:524
  78.0 0.0 collective-permute-done.1.refs_1_
  78.0 1.0 copy-done.9
  79.0 0.3 shard_map.252
  79.2 24.5 %all_to_all.20.refs_0_ = bf16[64,80,128]{2,1,0:T(8,128)(2,1)S(1)} all-to-all(bf16[64,80,128]{2,1,0:T(8,128)(2,1)S(1)} %shard_map.252), channel_id=1, replica_groups={{0,2,4,6,8,10,12,14,16,18,20,22,24,26,28,30,32,34,36,38,40,42,44,46,48,..., dimensions={0} | all-to-all | bytes 2621440 | tf_op jit(solution)/shard_map/all_to_all | solution.py:521
  103.8 1.2 shard_map.253
  105.0 2.3 %collective-permute-start.3 = (bf16[64,40,128]{2,1,0:T(8,128)(2,1)S(1)}, bf16[64,40,128]{2,1,0:T(8,128)(2,1)S(1)}, u32[]{:S(2)}, u32[]{:S(2)}) collective-permute-start(bf16[64,40,128]{2,1,0:T(8,128)(2,1)S(1)} %get-tuple-element.87.refs_2_), channel_id=1, source_target_pairs={{0,1},{1,0},{2,3},{3,2},{4,5},{5,4},{6,7},{7,6},{8,9},{9,8},{10,11... | collective-permute-start | bytes 1966088 | tf_op jit(solution)/shard_map/ppermute | solution.py:524
  107.3 4.6 %all-to-all-start.3 = ((bf16[64,40,128]{2,1,0:T(8,128)(2,1)}), bf16[64,40,128]{2,1,0:T(8,128)(2,1)S(1)}, u32[]{:S(2)}, u32[]{:S(2)}) async-start(bf16[64,40,128]{2,1,0:T(8,128)(2,1)} %get-tuple-element.84), calls=%async_computation.3 | async-start | bytes 1310720 | tf_op jit(solution)/shard_map/all_to_all | solution.py:521
  112.0 0.0 copy-start.1
  112.0 0.0 copy-start.2
  112.0 0.0 collective-permute-done.3.refs_3_
  112.0 0.9 copy-done.22
  112.9 4.7 %shard_map.254 = (f32[1024,512]{1,0:T(8,128)}, f32[192,512]{1,0:T(8,128)}) custom-call(bf16[64,32,128]{2,1,0:T(8,128)(2,1)} %get-tuple-element.85.refs_0_, bf16[64,32,128]{2,1,0:T(8,128)(2,1)} %get-tuple-element.86.refs_1_, bf16[64,40,128]{2,1,0:T(8,128)(2,1)} %copy-done.8, bf16[64,40,128]{2,1,0:T(8,128)(2,1)} %copy-done.22), custom_call_target="tpu_custom_call" | custom-call | flops 1000000000 | bytes 10000000 | tf_op jit(solution)/shard_map/pallas_call | solution.py:498
  117.6 8.4 %all-to-all-done.3.refs_1_ = bf16[64,40,128]{2,1,0:T(8,128)(2,1)S(1)} async-done(((bf16[64,40,128]{2,1,0:T(8,128)(2,1)}), bf16[64,40,128]{2,1,0:T(8,128)(2,1)S(1)}, u32[]{:S(2)}, u32[]{:S(2)}) %all-to-all-start.3) | async-done | bytes 655392 | tf_op jit(solution)/shard_map/all_to_all | solution.py:521
  126.0 1.6 %collective-permute-start.4 = (bf16[64,40,128]{2,1,0:T(8,128)(2,1)S(1)}, bf16[64,40,128]{2,1,0:T(8,128)(2,1)S(1)}, u32[]{:S(2)}, u32[]{:S(2)}) collective-permute-start(bf16[64,40,128]{2,1,0:T(8,128)(2,1)S(1)} %all-to-all-done.3.refs_1_), channel_id=1, source_target_pairs={{0,1},{1,0},{2,3},{3,2},{4,5},{5,4},{6,7},{7,6},{8,9},{9,8},{10,11... | collective-permute-start | bytes 1966088 | tf_op jit(solution)/shard_map/ppermute | solution.py:524
  127.6 1.7 %collective-permute-done.4.refs_2_ = bf16[64,40,128]{2,1,0:T(8,128)(2,1)S(1)} collective-permute-done((bf16[64,40,128]{2,1,0:T(8,128)(2,1)S(1)}, bf16[64,40,128]{2,1,0:T(8,128)(2,1)S(1)}, u32[]{:S(2)}, u32[]{:S(2)}) %collective-permute-start.4) | collective-permute-done | bytes 655392 | tf_op jit(solution)/shard_map/ppermute | solution.py:524
  129.3 1.0 copy-done.16
  130.3 4.5 %shard_map.255 = (f32[192,432]{1,0:T(8,128)}, f32[9,432]{1,0:T(8,128)}, f32[3,432]{1,0:T(4,128)}, f32[192,432]{1,0:T(8,128)}, f32[192,432]{1,0:T(8,128)}, /*inde...) custom-call(s32[1]{0:T(128)} %bitcast.refs_0_, ...), custom_call_target="tpu_custom_call" | custom-call | flops 1000000000 | bytes 10000000 | tf_op jit(solution)/shard_map/pallas_call | solution.py:498
  (27 shorter events, 0.1 us)
Async XLA Ops:
  0.6 2.1 %copy-start.7 = (s32[4]{0:T(128)S(1)}, s32[4]{0:T(128)}, u32[]{:S(2)}) copy-start(s32[4]{0:T(128)} %refs_1_.3) | copy-start | bytes 52
  0.7 2.1 %copy-start.4 = (bf16[192,432]{1,0:T(8,128)(2,1)S(1)}, bf16[192,432]{1,0:T(8,128)(2,1)}, u32[]{:S(2)}) copy-start(bf16[192,432]{1,0:T(8,128)(2,1)} %refs_10_.5) | copy-start | bytes 497668
  0.7 2.1 %copy-start.6 = (f32[4,512]{1,0:T(4,128)S(1)}, f32[4,512]{1,0:T(4,128)}, u32[]{:S(2)}) copy-start(f32[4,512]{1,0:T(4,128)} %refs_5_.6) | copy-start | bytes 24580
  0.7 2.1 %copy-start.14 = (bf16[3,432]{1,0:T(4,128)(2,1)S(1)}, bf16[3,432]{1,0:T(4,128)(2,1)}, u32[]{:S(2)}) copy-start(bf16[3,432]{1,0:T(4,128)(2,1)} %refs_10_.4) | copy-start | bytes 7780
  0.7 2.1 %copy-start.12 = (bf16[9,432]{1,0:T(8,128)(2,1)S(1)}, bf16[9,432]{1,0:T(8,128)(2,1)}, u32[]{:S(2)}) copy-start(bf16[9,432]{1,0:T(8,128)(2,1)} %refs_9_.3) | copy-start | bytes 23332
  0.7 2.1 %copy-start.13 = (bf16[3,432]{1,0:T(4,128)(2,1)S(1)}, bf16[3,432]{1,0:T(4,128)(2,1)}, u32[]{:S(2)}) copy-start(bf16[3,432]{1,0:T(4,128)(2,1)} %refs_6_.5) | copy-start | bytes 7780
  0.7 2.1 %copy-start.11 = (bf16[9,432]{1,0:T(8,128)(2,1)S(1)}, bf16[9,432]{1,0:T(8,128)(2,1)}, u32[]{:S(2)}) copy-start(bf16[9,432]{1,0:T(8,128)(2,1)} %refs_5_.5) | copy-start | bytes 23332
  0.7 2.1 %copy-start.10 = (bf16[192,432]{1,0:T(8,128)(2,1)S(1)}, bf16[192,432]{1,0:T(8,128)(2,1)}, u32[]{:S(2)}) copy-start(bf16[192,432]{1,0:T(8,128)(2,1)} %refs_4_.5) | copy-start | bytes 497668
  0.7 2.1 %copy-start.5 = (bf16[432,192]{0,1:T(8,128)(2,1)S(1)}, bf16[432,192]{0,1:T(8,128)(2,1)}, u32[]{:S(2)}) copy-start(bf16[432,192]{0,1:T(8,128)(2,1)} %param.28) | copy-start | bytes 497668
  0.8 2.1 %copy-start.3 = (bf16[432,192]{0,1:T(8,128)(2,1)S(1)}, bf16[432,192]{0,1:T(8,128)(2,1)}, u32[]{:S(2)}) copy-start(bf16[432,192]{0,1:T(8,128)(2,1)} %param.24) | copy-start | bytes 497668
  0.8 2.1 %copy-start.15 = (s32[32]{0:T(128)S(1)}, s32[32]{0:T(128)}, u32[]{:S(2)}) copy-start(s32[32]{0:T(128)} %param.17) | copy-start | bytes 388
  2.8 4.9 %copy-start = (bf16[32,4,4,4,192]{4,0,3,2,1:T(8,128)(2,1)}, bf16[32,4,4,4,192]{4,0,3,2,1:T(8,128)(2,1)S(1)}, u32[]{:S(2)}) copy-start(bf16[32,4,4,4,192]{4,0,3,2,1:T(8,128)(2,1)S(1)} %copy.28) | copy-start | bytes 2359300
  7.7 29.2 %all-to-all-start = ((bf16[64,64,128]{2,1,0:T(8,128)(2,1)}), bf16[64,64,128]{2,1,0:T(8,128)(2,1)S(1)}, u32[]{:S(2)}, u32[]{:S(2)}) async-start(bf16[64,64,128]{2,1,0:T(8,128)(2,1)} %shard_map.247), calls=%async_computation | async-start | bytes 2097152 | tf_op jit(solution)/shard_map/all_to_all | solution.py:521
  36.9 4.8 %copy-start.19 = (bf16[64,64,128]{2,1,0:T(8,128)(2,1)}, bf16[64,64,128]{2,1,0:T(8,128)(2,1)S(1)}, u32[]{:S(2)}) copy-start(bf16[64,64,128]{2,1,0:T(8,128)(2,1)S(1)} %all-to-all-done.refs_2_) | copy-start | bytes 3145732
  36.9 4.7 %collective-permute-start = (bf16[64,64,128]{2,1,0:T(8,128)(2,1)S(1)}, bf16[64,64,128]{2,1,0:T(8,128)(2,1)S(1)}, u32[]{:S(2)}, u32[]{:S(2)}) collective-permute-start(bf16[64,64,128]{2,1,0:T(8,128)(2,1)S(1)} %all-to-all-done.refs_2_), channel_id=1, source_target_pairs={{0,1},{1,0},{2,3},{3,2},{4,5},{5,4},{6,7},{7,6},{8,9},{9,8},{10,11... | collective-permute-start | bytes 3145736 | tf_op jit(solution)/shard_map/ppermute | solution.py:524
  41.6 1.0 copy-start.20
  50.2 14.8 %all-to-all-start.1 = ((bf16[128,8,128]{2,1,0:T(8,128)(2,1)}), bf16[128,8,128]{2,1,0:T(8,128)(2,1)S(1)}, u32[]{:S(2)}, u32[]{:S(2)}) async-start(bf16[128,8,128]{2,1,0:T(8,128)(2,1)} %get-tuple-element.64), calls=%async_computation.1 | async-start | bytes 524288 | tf_op jit(solution)/shard_map/all_to_all | solution.py:560
  65.0 0.7 copy-start.21
  65.7 10.5 %copy-start.23 = (bf16[1024,128]{1,0:T(8,128)(2,1)S(1)}, bf16[1024,128]{1,0:T(8,128)(2,1)}, u32[]{:S(2)}) copy-start(bf16[1024,128]{1,0:T(8,128)(2,1)} %get-tuple-element.82) | copy-start | bytes 786436
  65.7 12.3 %copy-start.17 = (bf16[1024,128]{1,0:T(8,128)(2,1)S(1)}, bf16[1024,128]{1,0:T(8,128)(2,1)}, u32[]{:S(2)}) copy-start(bf16[1024,128]{1,0:T(8,128)(2,1)} %get-tuple-element.81.refs_2_) | copy-start | bytes 786436
  65.7 12.3 %copy-start.18 = (bf16[48,128]{1,0:T(8,128)(2,1)S(1)}, bf16[48,128]{1,0:T(8,128)(2,1)}, u32[]{:S(2)}) copy-start(bf16[48,128]{1,0:T(8,128)(2,1)} %get-tuple-element.83.refs_4_) | copy-start | bytes 36868
  75.0 2.9 %collective-permute-start.1 = (bf16[1536,128]{1,0:T(8,128)(2,1)}, bf16[1536,128]{1,0:T(8,128)(2,1)S(1)}, u32[]{:S(2)}, u32[]{:S(2)}) collective-permute-start(bf16[1536,128]{1,0:T(8,128)(2,1)} %get-tuple-element.80), channel_id=1, source_target_pairs={{0,1},{1,0},{2,3},{3,2},{4,5},{5,4},{6,7},{7,6},{8,9},{9,8},{10,11... | collective-permute-start | bytes 1179656 | tf_op jit(solution)/shard_map/ppermute | solution.py:524
  76.2 1.7 %collective-permute-start.2 = (bf16[1024,128]{1,0:T(8,128)(2,1)S(1)}, bf16[1024,128]{1,0:T(8,128)(2,1)S(1)}, u32[]{:S(2)}, u32[]{:S(2)}) collective-permute-start(bf16[1024,128]{1,0:T(8,128)(2,1)S(1)} %copy-done.23), channel_id=1, source_target_pairs={{0,1},{1,0},{2,3},{3,2},{4,5},{5,4},{6,7},{7,6},{8,9},{9,8},{10,11... | collective-permute-start | bytes 786440 | tf_op jit(solution)/shard_map/ppermute | solution.py:524
  78.0 1.0 copy-start.9
  105.0 7.0 %copy-start.8 = (bf16[64,40,128]{2,1,0:T(8,128)(2,1)}, bf16[64,40,128]{2,1,0:T(8,128)(2,1)S(1)}, u32[]{:S(2)}) copy-start(bf16[64,40,128]{2,1,0:T(8,128)(2,1)S(1)} %get-tuple-element.87.refs_2_) | copy-start | bytes 1966084
  105.0 7.0 %collective-permute-start.3 = (bf16[64,40,128]{2,1,0:T(8,128)(2,1)S(1)}, bf16[64,40,128]{2,1,0:T(8,128)(2,1)S(1)}, u32[]{:S(2)}, u32[]{:S(2)}) collective-permute-start(bf16[64,40,128]{2,1,0:T(8,128)(2,1)S(1)} %get-tuple-element.87.refs_2_), channel_id=1, source_target_pairs={{0,1},{1,0},{2,3},{3,2},{4,5},{5,4},{6,7},{7,6},{8,9},{9,8},{10,11... | collective-permute-start | bytes 1966088 | tf_op jit(solution)/shard_map/ppermute | solution.py:524
  107.3 18.6 %all-to-all-start.3 = ((bf16[64,40,128]{2,1,0:T(8,128)(2,1)}), bf16[64,40,128]{2,1,0:T(8,128)(2,1)S(1)}, u32[]{:S(2)}, u32[]{:S(2)}) async-start(bf16[64,40,128]{2,1,0:T(8,128)(2,1)} %get-tuple-element.84), calls=%async_computation.3 | async-start | bytes 1310720 | tf_op jit(solution)/shard_map/all_to_all | solution.py:521
  112.0 17.3 %copy-start.1 = (bf16[512,1024]{1,0:T(8,128)(2,1)S(1)}, bf16[512,1024]{1,0:T(8,128)(2,1)}, u32[]{:S(2)}) copy-start(bf16[512,1024]{1,0:T(8,128)(2,1)} %refs_5_.7) | copy-start | bytes 3145732
  112.0 17.3 %copy-start.2 = (bf16[192,512]{1,0:T(8,128)(2,1)S(1)}, bf16[192,512]{1,0:T(8,128)(2,1)}, u32[]{:S(2)}) copy-start(bf16[192,512]{1,0:T(8,128)(2,1)} %refs_4_.7) | copy-start | bytes 589828
  112.0 0.9 copy-start.22
  126.0 3.3 %collective-permute-start.4 = (bf16[64,40,128]{2,1,0:T(8,128)(2,1)S(1)}, bf16[64,40,128]{2,1,0:T(8,128)(2,1)S(1)}, u32[]{:S(2)}, u32[]{:S(2)}) collective-permute-start(bf16[64,40,128]{2,1,0:T(8,128)(2,1)S(1)} %all-to-all-done.3.refs_1_), channel_id=1, source_target_pairs={{0,1},{1,0},{2,3},{3,2},{4,5},{5,4},{6,7},{7,6},{8,9},{9,8},{10,11... | collective-permute-start | bytes 1966088 | tf_op jit(solution)/shard_map/ppermute | solution.py:524
  129.3 1.0 copy-start.16

commit v4 on v3

--- a/solution.py
+++ b/solution.py
@@ -25,6 +25,9 @@
 LINKS_SECOND = [(0, 4), (1, 5), (2, 7), (3, 8)]
 
 
+AT_N2, AT_H2, AT_SP2, AT_G2, AT_D2, AT_N1, AT_H1, AT_SP1, INNER = 0, 4, 8, 12, 28, 44, 60, 76, 92
+
+
 def dot_nn(a, b):
     return lax.dot_general(a, b, (((1,), (0,)), ((), ())), preferred_element_type=F32)
 
@@ -65,7 +68,7 @@
     if len(kept) == 1:
         (block,) = kept
     else:
-        taps, g1, d1, sp1, n1, h1, o1, g2, d2, sp2, n2, h2 = kept
+        taps, weights, outer, inner, o1 = kept
     counts = column_of(counts_row[...])
     zero4 = jnp.zeros((HALF * HALF, ITEMS_HERE, E), F32)
     framed1[0] = zero4
@@ -94,49 +97,52 @@
         value, slope = silu_and_slope(pre)
         value = value.astype(BF).reshape(CELLS, ITEMS_HERE, E)
         if block is None:
-            g1[pl.ds(f * CELLS, CELLS)] = value
-            d1[pl.ds(f * CELLS, CELLS)] = slope.astype(BF).reshape(CELLS, ITEMS_HERE, E)
+            outer[pl.ds(f * CELLS, CELLS)] = value
+            outer[pl.ds((FRAMES + f) * CELLS, CELLS)] = slope.astype(BF).reshape(CELLS, ITEMS_HERE, E)
         outs = [jnp.zeros((ITEMS_HERE, E), F32)] * 4
         for out_cell, in_cell, tap in LINKS_FIRST:
             outs[out_cell] = outs[out_cell] + value[in_cell].astype(F32) * taps1[tap]
         for out_cell in range(4):
             framed1[f + 1, out_cell] = outs[out_cell]
             if block is None:
-                sp1[f, out_cell] = outs[out_cell].astype(BF)
+                inner[AT_SP1 + f * 4 + out_cell] = outs[out_cell].astype(BF)
         return 0
 
-    lax.fori_loop(0, FRAMES, grow, 0)
+    lax.fori_loop(0, FRAMES, grow, 0, unroll=True)
     narrow = []
     for f in range(FRAMES):
         summed = framed1[f] * frame1[0] + framed1[f + 1] * frame1[1] + framed1[f + 2] * frame1[2]
         value, slope = silu_and_slope(summed)
         narrow.append(value.astype(BF))
         if block is None:
-            h1[f * 4 : f * 4 + 4] = slope.astype(BF)
+            inner[AT_H1 + f * 4 : AT_H1 + f * 4 + 4] = slope.astype(BF)
     narrow = jnp.concatenate(narrow, axis=0)
     first = dot_nt(narrow.reshape(FRAMES * 4 * ITEMS_HERE, E), p1[...]).astype(BF)
     value, slope = silu_and_slope(dot_nn(first, e2[...]))
     value = value.astype(BF).reshape(FRAMES * 4, ITEMS_HERE, E)
     if block is None:
-        n1[...] = narrow
+        inner[AT_N1 : AT_N1 + 16] = narrow
         o1[...] = first
-        g2[...] = value
-        d2[...] = slope.astype(BF).reshape(FRAMES * 4, ITEMS_HERE, E)
+        inner[AT_G2 : AT_G2 + 16] = value
+        inner[AT_D2 : AT_D2 + 16] = slope.astype(BF).reshape(FRAMES * 4, ITEMS_HERE, E)
+        weights[0:192] = p2[...]
+        weights[192:384] = e2[...]
+        weights[384:576] = p1[...]
     for f in range(FRAMES):
         total = jnp.zeros((ITEMS_HERE, E), F32)
         for cell, tap in LINKS_SECOND:
             total = total + value[f * 4 + cell].astype(F32) * taps2[tap]
         framed2[f + 1] = total
         if block is None:
-            sp2[f] = total.astype(BF)
+            inner[AT_SP2 + f] = total.astype(BF)
     narrow = []
     for f in range(FRAMES):
         summed = framed2[f] * frame2[0] + framed2[f + 1] * frame2[1] + framed2[f + 2] * frame2[2]
         value, slope = silu_and_slope(summed)
         narrow.append(value.astype(BF))
         if block is None:
-            n2[f] = value.astype(BF)
-            h2[f] = slope.astype(BF)
+            inner[AT_N2 + f] = value.astype(BF)
+            inner[AT_H2 + f] = slope.astype(BF)
     if block is None:
         return
     second = dot_nt(jnp.concatenate(narrow, axis=0), p2[...]).astype(BF)
@@ -158,42 +164,14 @@
     block[...] = jnp.broadcast_to(rows[None], (CHIPS, 64, 128))
 
 
-def tower(
-    core, lengths, own, other, ids_ref, cot, project, up, down,
-    sent, picked_out, fetched_out, act_out, pre_grad_out, mixed_own, mixed_other,
-):
-    ids = jnp.concatenate([column_of(ids_ref[u : u + 1]) for u in range(USERS_HERE)], axis=0)
-    owner = ids // ITEMS_HERE
-    within = ids - owner * ITEMS_HERE
-    chip = owner // 2
-    place = chip * ITEMS_HERE + within
-    mine = (owner - chip * 2) == core[0]
-    lanes = lax.broadcasted_iota(jnp.int32, (ROWS, CHIPS * ITEMS_HERE), 1)
-    pick_own = (lanes == jnp.where(mine, place, -1)).astype(F32).astype(BF)
-    pick_other = (lanes == jnp.where(mine, -1, place)).astype(F32).astype(BF)
-
-    def rows_of(ref):
-        low = ref[:, 0:32, :].reshape(CHIPS * ITEMS_HERE, 128)
-        high = ref[:, 32:64, :].reshape(CHIPS * ITEMS_HERE, 128)
-        return jnp.concatenate([low, high], axis=1)
-
-    own, other = own.ready(), other.ready()
-    for late in (project, up, down):
-        late.begin()
-    mixed_own.leave(own.at[:, 32:64, :])
-    mixed_other.leave(other.at[:, 32:64, :])
-    picked = (dot_nn(pick_own, rows_of(own)) + dot_nn(pick_other, rows_of(other))).astype(BF)
+def tower_middle(picked, lengths, cot, project, up, down):
     fetched = dot_nn(picked[:, 0:C], project[...]).astype(BF)
     pre = dot_nn(fetched, up[...])
     scale = 0.7978845608028654
     square = pre * pre
     bent = jnp.tanh(scale * pre * (1.0 + 0.044715 * square))
     gate = 0.5 * (1.0 + bent)
-    picked_out[...] = picked
-    fetched_out[...] = fetched
-    act_out[...] = (pre * gate).astype(BF)
-    for out in (picked_out, fetched_out, act_out):
-        out.leave()
+    act = (pre * gate).astype(BF)
     slope = gate + 0.5 * pre * (1.0 - bent * bent) * (scale * (1.0 + 3 * 0.044715 * square))
     _, length = per_user(lengths)
     shared = cot[...] / length[0:4].astype(F32)
@@ -206,9 +184,36 @@
         pre_parts.append(alive * act_grad[u : u + 1] * slope[u * LENGTH : (u + 1) * LENGTH])
         base_parts.append(alive * shared[u : u + 1])
     pre_grad = jnp.concatenate(pre_parts, axis=0).astype(BF)
-    pre_grad_out[...] = pre_grad
-    pre_grad_out.leave()
-    rows_grad = jnp.concatenate(base_parts, axis=0) + dot_nt(pre_grad, up[...])
+    return fetched, act, pre_grad, jnp.concatenate(base_parts, axis=0)
+
+
+def tower(
+    core, lengths, own, other, ids_ref, cot, project, up, down,
+    sent, picked_out,
+):
+    ids = jnp.concatenate([column_of(ids_ref[u : u + 1]) for u in range(USERS_HERE)], axis=0)
+    owner = ids // ITEMS_HERE
+    within = ids - owner * ITEMS_HERE
+    chip = owner // 2
+    place = chip * ITEMS_HERE + within
+    mine = (owner - chip * 2) == core[0]
+    lanes = lax.broadcasted_iota(jnp.int32, (ROWS, CHIPS * ITEMS_HERE), 1)
+    pick_own = (lanes == jnp.where(mine, place, -1)).astype(F32).astype(BF)
+    pick_other = (lanes == jnp.where(mine, -1, place)).astype(F32).astype(BF)
+
+    def rows_of(ref):
+        low = ref[:, 0:32, :].reshape(CHIPS * ITEMS_HERE, 128)
+        high = ref[:, 32:64, :].reshape(CHIPS * ITEMS_HERE, 128)
+        return jnp.concatenate([low, high], axis=1)
+
+    own, other = own.ready(), other.ready()
+    for late in (project, up, down):
+        late.begin()
+    picked = (dot_nn(pick_own, rows_of(own)) + dot_nn(pick_other, rows_of(other))).astype(BF)
+    picked_out[...] = picked
+    picked_out.leave()
+    _, _, pre_grad, base = tower_middle(picked, lengths, cot, project, up, down)
+    rows_grad = base + dot_nt(pre_grad, up[...])
     rows_coarse = rows_grad.astype(BF)
     rows_fine = (rows_grad - rows_coarse.astype(F32)).astype(BF)
     low = dot_nt(rows_coarse, project[0:128]) + dot_nt(rows_fine, project[0:128])
@@ -232,23 +237,25 @@
 
 
 def tower_sums(
-    core, lengths, picked, fetched, act, pre_grad, down,
+    core, lengths, picked, cot, project, up, down,
     up_keep, up_send, factors, user_vec,
     halves,
 ):
+    picked = picked[...]
+    fetched, act, pre_grad, _ = tower_middle(picked, lengths, cot, project, up, down)
     user, length = per_user(lengths)
     at = lax.broadcasted_iota(jnp.int32, (8, ROWS), 1)
     live = ((at // LENGTH == user) & (at - user * LENGTH < length)).astype(F32).astype(BF)
-    act_sum = dot_nn(live, act[...])
-    picked_sum = dot_nn(live, picked[...])
+    act_sum = dot_nn(live, act)
+    picked_sum = dot_nn(live, picked)
     pieces = [act_sum[0:4, j * 128 : (j + 1) * 128] for j in range(8)]
     pieces += [picked_sum[0:4, j * 128 : (j + 1) * 128] for j in range(2)]
     factors[...] = jnp.concatenate(pieces + [jnp.zeros((8, 128), F32)], axis=0).astype(BF)
     coarse = act_sum.astype(BF)
     fine = (act_sum - coarse.astype(F32)).astype(BF)
-    mixed = dot_nn(live, fetched[...]) + dot_nn(coarse, down[...]) + dot_nn(fine, down[...])
+    mixed = dot_nn(live, fetched) + dot_nn(coarse, down[...]) + dot_nn(fine, down[...])
     user_vec[...] = (mixed / length.astype(F32))[0:4]
-    up_grad = dot_tn(picked[...], pre_grad[...]).astype(BF)
+    up_grad = dot_tn(picked, pre_grad).astype(BF)
     for j in range(FH // 128):
         halves[j // 4, (j % 4) * 256 : (j % 4 + 1) * 256] = up_grad[:, j * 128 : (j + 1) * 128]
     up_keep.leave(halves.at[core[0]])
@@ -256,16 +263,14 @@
 
 
 def conv_backward(
-    core, back, taps, n2, p2, h2, sp2, g2, d2, o1, e2, n1, p1, h1, sp1, x, g1, d1,
+    core, back, inner, taps, weights, o1, x, outer,
     keep, send,
     spatial_grad, wide, small, halves,
 ):
     taps1, frame1, taps2, frame2 = taps[0:9], taps[9:12], taps[12:21], taps[21:24]
     counts = taps[24:56, 0:1]
-    for late in (n2, p2, h2, sp2, g2, d2, o1, e2):
-        late.ready()
-    for late in (x, g1, d1):
-        late.begin()
+    inner.ready(), weights.ready(), o1.ready()
+    p2, e2, p1 = weights[0:192], weights[192:384], weights[384:576]
 
     def tile_sum(v):
         return jnp.sum(v.reshape(-1, 8, E), axis=0)
@@ -285,8 +290,8 @@
     out_grad = jnp.concatenate(
         [(shared * (counts > f).astype(F32)).astype(BF) for f in range(FRAMES)], axis=0
     )
-    wide[576:768, 0:E] = dot_tn(out_grad, n2[...].reshape(FRAMES * ITEMS_HERE, E))
-    summed_grad = dot_nn(out_grad, p2[...]).reshape(FRAMES, ITEMS_HERE, E) * h2[...].astype(F32)
+    wide[576:768, 0:E] = dot_tn(out_grad, inner[AT_N2 : AT_N2 + 4].reshape(FRAMES * ITEMS_HERE, E))
+    summed_grad = dot_nn(out_grad, p2).reshape(FRAMES, ITEMS_HERE, E) * inner[AT_H2 : AT_H2 + 4].astype(F32)
     spread = []
     for f in range(FRAMES):
         total = summed_grad[f] * frame2[1]
@@ -299,24 +304,24 @@
         total = jnp.zeros((8, E), F32)
         for f in range(FRAMES):
             if 0 <= f + k - 1 < FRAMES:
-                total = total + tile_sum(sp2[f + k - 1].astype(F32) * summed_grad[f])
+                total = total + tile_sum(inner[AT_SP2 + f + k - 1].astype(F32) * summed_grad[f])
         small[21 + k] = total
     parts = []
     for f in range(FRAMES):
         for cell, tap in LINKS_SECOND:
-            small[12 + tap] += tile_sum(g2[f * 4 + cell].astype(F32) * spread[f])
-            parts.append((spread[f] * taps2[tap] * d2[f * 4 + cell].astype(F32)).astype(BF))
+            small[12 + tap] += tile_sum(inner[AT_G2 + f * 4 + cell].astype(F32) * spread[f])
+            parts.append((spread[f] * taps2[tap] * inner[AT_D2 + f * 4 + cell].astype(F32)).astype(BF))
     grown_grad = jnp.concatenate(parts, axis=0)
     wide[384:576, 0:E] = dot_tn(o1[...], grown_grad)
-    first_grad = dot_nt(grown_grad, e2[...]).astype(BF)
-    wide[192:384, 0:E] = dot_tn(first_grad, n1[...].reshape(FRAMES * 4 * ITEMS_HERE, E))
-    narrow_grad = dot_nn(first_grad, p1[...]).reshape(FRAMES, 4, ITEMS_HERE, E)
-    summed_grad = [narrow_grad[f] * h1[f * 4 : f * 4 + 4].astype(F32) for f in range(FRAMES)]
+    first_grad = dot_nt(grown_grad, e2).astype(BF)
+    wide[192:384, 0:E] = dot_tn(first_grad, inner[AT_N1 : AT_N1 + 16].reshape(FRAMES * 4 * ITEMS_HERE, E))
+    narrow_grad = dot_nn(first_grad, p1).reshape(FRAMES, 4, ITEMS_HERE, E)
+    summed_grad = [narrow_grad[f] * inner[AT_H1 + f * 4 : AT_H1 + f * 4 + 4].astype(F32) for f in range(FRAMES)]
     for k in range(3):
         total = jnp.zeros((8, E), F32)
         for f in range(FRAMES):
             if 0 <= f + k - 1 < FRAMES:
-                total = total + tile_sum(sp1[f + k - 1].astype(F32) * summed_grad[f])
+                total = total + tile_sum(inner[AT_SP1 + f * 4 + 4 * k - 4 : AT_SP1 + f * 4 + 4 * k].astype(F32) * summed_grad[f])
         small[9 + k] = total
     for f in range(FRAMES):
         total = summed_grad[f] * frame1[1]
@@ -324,27 +329,30 @@
             total = total + summed_grad[f + 1] * frame1[0]
         if f > 0:
             total = total + summed_grad[f - 1] * frame1[2]
-        spatial_grad[f] = total
-
-    x.ready(), g1.ready(), d1.ready()
+        spatial_grad[f] = total.astype(BF)
+
+    x.ready(), outer.ready()
+    half_taps = taps1.astype(BF)
 
     def grow_back(f, _):
         live = counts > lax.convert_element_type(f, F32)
         x_f = x[pl.ds(f * CELLS, CELLS)]
         x_f = jnp.where(live[None], x_f, jnp.zeros_like(x_f)).reshape(CELLS * ITEMS_HERE, C)
-        sums = [jnp.zeros((8, E), F32)] * 9
-        grads = [jnp.zeros((ITEMS_HERE, E), F32)] * CELLS
+        outs = [spatial_grad[f, cell] for cell in range(4)]
+        sums = [None] * 9
+        grads = [None] * CELLS
         for out_cell, in_cell, tap in LINKS_FIRST:
-            from_out = spatial_grad[f, out_cell]
-            grads[in_cell] = grads[in_cell] + from_out * taps1[tap]
-            sums[tap] = sums[tap] + tile_sum(g1[f * CELLS + in_cell].astype(F32) * from_out)
+            term = outs[out_cell] * half_taps[tap]
+            grads[in_cell] = term if grads[in_cell] is None else grads[in_cell] + term
+            term = outer[f * CELLS + in_cell] * outs[out_cell]
+            sums[tap] = term if sums[tap] is None else sums[tap] + term
         for tap in range(9):
-            small[tap] += sums[tap]
-        grads = [(grads[cell] * d1[f * CELLS + cell].astype(F32)).astype(BF) for cell in range(CELLS)]
+            small[tap] += tile_sum(sums[tap].astype(F32))
+        grads = [grads[cell] * outer[(FRAMES + f) * CELLS + cell] for cell in range(CELLS)]
         wide[0:192, 0:E] += dot_tn(x_f, jnp.concatenate(grads, axis=0))
         return 0
 
-    lax.fori_loop(0, FRAMES, grow_back, 0)
+    lax.fori_loop(0, FRAMES, grow_back, 0, unroll=True)
     sums = jnp.sum(small[...], axis=1).astype(BF)
     put = lax.broadcasted_iota(jnp.int32, (32, 128), 1) == lax.broadcasted_iota(jnp.int32, (32, 128), 0) + 64
     wide[0:E, 384:512] += dot_tn(sums, put.astype(F32).astype(BF))
@@ -376,7 +384,7 @@
     for src in (own, other):
         parts = []
         for k in range(4):
-            got = src[:, 8 * k : 8 * k + 8, :].reshape(CHIPS * 8, 128).astype(F32)
+            got = src[:, 32 + 8 * k : 40 + 8 * k, :].reshape(CHIPS * 8, 128).astype(F32)
             left = pltpu.roll(got, 64, 1)
             right = pltpu.roll(got, CHIPS * 8 - 4, 0)
             parts.append(jnp.where(row < 4, jnp.where(lane < 64, left, right), 0.0))
@@ -534,54 +542,43 @@
     (block,) = call(conv_forward, [shape((CHIPS, 64, 128))], "svvvvvvvvvvv", "v", framed, megabytes=24)(
         lengths, x, counts, user_cotangent, expand_first, *weights
     )
-    taps, g1, d1, sp1, n1, h1, o1, g2, d2, sp2, n2, h2 = call(
+    kept = call(
         conv_forward,
-        [
-            shape((56, E), F32),
-            shape((64, n, E)), shape((64, n, E)), shape((4, 4, n, E)), shape((16, n, E)), shape((16, n, E)),
-            shape((512, C)), shape((16, n, E)), shape((16, n, E)), shape((4, n, E)), shape((4, n, E)), shape((4, n, E)),
-        ],
+        [shape((56, E), F32), shape((576, E)), shape((2 * 64, n, E)), shape((INNER, n, E)), shape((512, C))],
         "shvvhvvhhvvh",
-        "h" * 12,
+        "h" * 5,
         framed,
     )(lengths, x, counts, user_cotangent, expand_first, *weights)
     own = across_chips(block)
-    own, taps = lax.optimization_barrier((own, taps))
-    sent, *seen, mixed_own, mixed_other = call(
-        tower,
-        [
-            shape((DEVICES, 8, 128)), shape((ROWS, 256)), shape((ROWS, D)), shape((ROWS, FH)), shape((ROWS, FH)),
-            shape((CHIPS, 32, 128)), shape((CHIPS, 32, 128)),
-        ],
-        "sshhvvwww",
-        "hhhhhhh",
-        unstaged=(5, 6),
-    )(core, lengths, own, swap(own), histories, user_cotangent, item_project, tower_up, tower_down)
+    own, (taps, kept_weights, outer, inner, o1) = lax.optimization_barrier((own, kept))
+    other = swap(own)
+    sent, picked = call(tower, [shape((DEVICES, 8, 128)), shape((ROWS, 256))], "sshhvvwww", "hh")(
+        core, lengths, own, other, histories, user_cotangent, item_project, tower_up, tower_down
+    )
     back = lax.all_to_all(sent, AXES, 0, 0, tiled=True)
     up_keep, up_send, factors, user_vec = call(
         tower_sums,
         [shape((1024, 128)), shape((1024, 128)), shape((48, 128)), shape((USERS_HERE, D), F32)],
-        "sshhhhh",
+        "sshvhhh",
         "hhhv",
         [pltpu.VMEM((2, 1024, 128), BF)],
         unstaged=(0, 1),
-    )(core, lengths, *seen, tower_down)
+    )(core, lengths, picked, user_cotangent, item_project, tower_up, tower_down)
     back, up_send = lax.optimization_barrier((back, up_send))
     up_other = swap(up_send)
     conv_keep, conv_send = call(
         conv_backward,
         [shape((1536, 128)), shape((1536, 128))],
-        "sv" + "h" * 13 + "www",
+        "sv" + "h" * 6,
         "vv",
         [
-            pltpu.VMEM((4, 4, n, E), F32),
+            pltpu.VMEM((4, 4, n, E), BF),
             pltpu.VMEM((768, 512), F32),
             pltpu.VMEM((32, 8, E), F32),
             pltpu.VMEM((2, 1536, 128), BF),
         ],
-    )(
-        core, back, taps, n2, weights[6], h2, sp2, g2, d2, o1, weights[3], n1, weights[2], h1, sp1, x, g1, d1,
-    )
+        megabytes=50,
+    )(core, back, inner, taps, kept_weights, o1, x, outer)
     (third,) = call(merge, [shape((CHIPS, 80, 128))], "vvvvv", "v", megabytes=16)(
         conv_keep, swap(conv_send), up_keep, up_other, factors
     )
@@ -591,7 +588,7 @@
     )(third)
     fourth = across_chips(fourth)
     grad_down, item_base = call(finish_low_rank, [shape((FH, D), F32), shape((C, D), F32)], "hhhh", "hh")(
-        mixed_own, mixed_other, factors, swap(factors)
+        own, other, factors, swap(factors)
     )
     fourth, item_base = lax.optimization_barrier((fourth, item_base))
     *conv_grads, grad_item, grad_up = call(

time: 136 us -> 130 us (0.956)
  Pallas kernels: 46.5 us -> 43.1 us
  local copies, waits for them, and re-layouts: 6.61 us -> 4.99 us
    pallas_call x9, Pallas kernels: 46.5 us -> 43.1 us  [run(): pl.pallas_call(body, out_shape=outs, in_specs=[pl.BlockSpec(memory_space=...]
    unnamed x49 -> x53, local copies, waits for them, and re-layouts: 6.61 us -> 4.99 us
  transfers between devices with their start and end apart: 8 -> 8, of which waited for: 6 -> 6; matrix products, arithmetic and copies ran while one was open for 0% -> 0% of each run, Pallas kernels for 14% -> 15%
where the time goes in v4:
time: 130 us
  Pallas kernels  43.1 us (33%)
  starting transfers between devices  28.4 us (22%)
  waiting for transfers between devices  27.3 us (21%)
  blocking collectives  24.5 us (19%)
  local copies, waits for them, and re-layouts  4.99 us (4%)
    pallas_call x9, Pallas kernels, run(): pl.pallas_call(body, out_shape=outs, in_specs=[pl.BlockSpec(memory_space=...  43.1 us
    all_to_all x1, blocking collectives, across_chips(): lax.all_to_all(v, AXES, 0, 0, axis_index_groups=same_core, tiled=True)  24.5 us
    all_to_all x2, starting transfers between devices, across_chips(): lax.all_to_all(v, AXES, 0, 0, axis_index_groups=same_core, tiled=True)  16.6 us
    all_to_all x2, waiting for transfers between devices, across_chips(): lax.all_to_all(v, AXES, 0, 0, axis_index_groups=same_core, tiled=True)  16.1 us
    ppermute x5, starting transfers between devices, swap(): return lax.ppermute(v, 'seq', [(i, i ^ 1) for i in range(8)])  7.88 us
    ppermute x5, waiting for transfers between devices, swap(): return lax.ppermute(v, 'seq', [(i, i ^ 1) for i in range(8)])  5.64 us
    all_to_all x1, waiting for transfers between devices, local(): back = lax.all_to_all(sent, AXES, 0, 0, tiled=True)  5.55 us
    unnamed x53, local copies, waits for them, and re-layouts  4.99 us
  transfers between devices with their start and end apart: 8, of which 6 were waited for; matrix products, arithmetic and copies ran while one was open for 0% of the time, Pallas kernels for 15%

profile of v4, /device:TPU:1, one launch (start us, length us, event | category | flops | bytes accessed | tf_op | source)
XLA Modules:
  0.0 129.6 jit_solution(8428938668550972446)
XLA Ops:
  0.6 0.0 copy-start.7
  0.7 0.0 copy-start.8
  0.7 0.0 copy-start.17
  0.7 0.0 copy-start.15
  0.7 0.0 copy-start.12
  0.7 0.0 copy-start.16
  0.7 0.0 copy-start.14
  0.7 0.0 copy-start.10
  0.7 0.0 copy-start.13
  0.8 0.0 copy-start.11
  0.8 0.0 copy-start.18
  0.8 2.0 %copy.28 = bf16[32,4,4,4,192]{4,0,3,2,1:T(8,128)(2,1)S(1)} copy(bf16[32,4,4,4,192]{4,3,2,1,0:T(4,128)(2,1)} %param.16) | data formatting | bytes 1572864 | tf_op args[0]
  2.7 0.0 copy-start
  2.9 4.4 %shard_map.247 = bf16[64,64,128]{2,1,0:T(8,128)(2,1)} custom-call(s32[4]{0:T(128)S(1)} %copy-done.8, bf16[64,32,192]{2,1,0:T(8,128)(2,1)S(1)} %bitcast.9, s32[1,32]{1,0:T(1,128)S(1)} %bitcast.17, f32[4,512]{1,0:T(4,128)S(1)} %copy-done.7, bf16[192,432]{1,0:T(8,128)(2,1)S(1)} %copy-done.10, bf16[9,432]{1,0:T(8,128)(2,1)S(1)} %copy-done.14, ...), custom_call_target="tpu_custom_call" | custom-call | flops 1000000000 | bytes 10000000 | tf_op jit(solution)/shard_map/pallas_call | solution.py:506
  7.3 12.0 %all-to-all-start = ((bf16[64,64,128]{2,1,0:T(8,128)(2,1)}), bf16[64,64,128]{2,1,0:T(8,128)(2,1)S(1)}, u32[]{:S(2)}, u32[]{:S(2)}) async-start(bf16[64,64,128]{2,1,0:T(8,128)(2,1)} %shard_map.247), calls=%async_computation | async-start | bytes 2097152 | tf_op jit(solution)/shard_map/all_to_all | solution.py:529
  19.3 9.3 %shard_map.248 = (f32[56,432]{1,0:T(8,128)}, bf16[576,432]{1,0:T(8,128)(2,1)}, bf16[128,32,432]{2,1,0:T(8,128)(2,1)}, bf16[92,32,432]{2,1,0:T(8,128)(2,1)}, bf16[512,192]{1,0:T(8,128)(2,1)}) custom-call(s32[4]{0:T(128)} %refs_1_.3, bf16[64,32,192]{2,1,0:T(8,128)(2,1)} %bitcast.10, s32[1,32]{1,0:T(1,128)} %bitcast.16, f32[4,512]{1,0:T(4,128)} %refs_3_.5, ...), custom_call_target="tpu_custom_call" | custom-call | flops 1000000000 | bytes 10000000 | tf_op jit(solution)/shard_map/pallas_call | solution.py:506
  28.6 7.9 %all-to-all-done.refs_2_.refs_0_ = bf16[64,64,128]{2,1,0:T(8,128)(2,1)S(1)} async-done(((bf16[64,64,128]{2,1,0:T(8,128)(2,1)}), bf16[64,64,128]{2,1,0:T(8,128)(2,1)S(1)}, u32[]{:S(2)}, u32[]{:S(2)}) %all-to-all-start) | async-done | bytes 1048608 | tf_op jit(solution)/shard_map/all_to_all | solution.py:529
  36.5 2.5 %collective-permute-start = (bf16[64,64,128]{2,1,0:T(8,128)(2,1)S(1)}, bf16[64,64,128]{2,1,0:T(8,128)(2,1)S(1)}, u32[]{:S(2)}, u32[]{:S(2)}) collective-permute-start(bf16[64,64,128]{2,1,0:T(8,128)(2,1)S(1)} %all-to-all-done.refs_2_.refs_0_), channel_id=1, source_target_pairs={{0,1},{1,0},{2,3},{3,2},{4,5},{5,4},{6,7},{7,6},{8,9},{9,8},{10,11... | collective-permute-start | bytes 3145736 | tf_op jit(solution)/shard_map/ppermute | solution.py:532
  39.0 2.3 %collective-permute-done.refs_3_.refs_1_ = bf16[64,64,128]{2,1,0:T(8,128)(2,1)S(1)} collective-permute-done((bf16[64,64,128]{2,1,0:T(8,128)(2,1)S(1)}, bf16[64,64,128]{2,1,0:T(8,128)(2,1)S(1)}, u32[]{:S(2)}, u32[]{:S(2)}) %collective-permute-start) | collective-permute-done | bytes 1048608 | tf_op jit(solution)/shard_map/ppermute | solution.py:532
  41.3 1.1 copy-done.23
  42.3 7.2 %shard_map.249 = (bf16[128,8,128]{2,1,0:T(8,128)(2,1)}, bf16[256,256]{1,0:T(8,128)(2,1)}) custom-call(s32[1]{0:T(128)} %bitcast.refs_0_, s32[4]{0:T(128)} %refs_1_.3, bf16[64,64,128]{2,1,0:T(8,128)(2,1)} %copy-done.22, bf16[64,64,128]{2,1,0:T(8,128)(2,1)} %copy-done.23, s32[4,64]{1,0:T(4,128)} %refs_4_.7, f32[4,512]{1,0:T(4,128)} %refs_3_.5, ...), custom_call_target="tpu_custom_call" | custom-call | flops 1000000000 | bytes 10000000 | tf_op jit(solution)/shard_map/pallas_call | solution.py:506
  49.6 0.0 copy-start.1
  49.6 0.0 copy-start.4
  49.6 3.9 %all-to-all-start.1 = ((bf16[128,8,128]{2,1,0:T(8,128)(2,1)}), bf16[128,8,128]{2,1,0:T(8,128)(2,1)S(1)}, u32[]{:S(2)}, u32[]{:S(2)}) async-start(bf16[128,8,128]{2,1,0:T(8,128)(2,1)} %get-tuple-element.57), calls=%async_computation.1 | async-start | bytes 524288 | tf_op jit(solution)/shard_map/all_to_all | solution.py:558
  53.5 5.5 %shard_map.250 = (bf16[1024,128]{1,0:T(8,128)(2,1)}, bf16[1024,128]{1,0:T(8,128)(2,1)}, bf16[48,128]{1,0:T(8,128)(2,1)}, f32[4,512]{1,0:T(4,128)}) custom-call(s32[1]{0:T(128)} %bitcast.refs_0_, s32[4]{0:T(128)} %refs_1_.3, bf16[256,256]{1,0:T(8,128)(2,1)} %get-tuple-element.55.refs_2_, f32[4,512]{1,0:T(4,128)} %refs_3_.5, bf16[192,512]{1,0:T(8,128)(2,1)} %refs_4_.9, ...), custom_call_target="tpu_custom_call" | custom-call | flops 1000000000 | bytes 10000000 | tf_op jit(solution)/shard_map/pallas_call | solution.py:506
  59.0 5.5 %all-to-all-done.1.refs_1_ = bf16[128,8,128]{2,1,0:T(8,128)(2,1)S(1)} async-done(((bf16[128,8,128]{2,1,0:T(8,128)(2,1)}), bf16[128,8,128]{2,1,0:T(8,128)(2,1)S(1)}, u32[]{:S(2)}, u32[]{:S(2)}) %all-to-all-start.1) | async-done | bytes 262176 | tf_op jit(solution)/shard_map/all_to_all | solution.py:558
  64.6 0.0 copy-start.25
  64.6 0.0 copy-start.20
  64.6 0.0 copy-start.21
  64.6 5.8 %shard_map.251 = (bf16[1536,128]{1,0:T(8,128)(2,1)S(1)}, bf16[1536,128]{1,0:T(8,128)(2,1)S(1)}) custom-call(s32[1]{0:T(128)} %bitcast.refs_0_, bf16[128,8,128]{2,1,0:T(8,128)(2,1)S(1)} %all-to-all-done.1.refs_1_, bf16[92,32,432]{2,1,0:T(8,128)(2,1)} %get-tuple-element.60.refs_2_, f32[56,432]{1,0:T(8,128)S(1)} %copy-done.6, bf16[576,432]{1,0:T(8,128)(2,1)S(1)} %copy-done.3, ...), custom_call_target="tpu_custom_call" | custom-call | flops 1000000000 | bytes 10000000 | tf_op jit(solution)/shard_map/pallas_call | solution.py:506
  70.4 1.2 collective-permute-start.1
  71.6 0.1 collective-permute-start.2
  71.7 1.6 %collective-permute-done.2.refs_3_ = bf16[1024,128]{1,0:T(8,128)(2,1)S(1)} collective-permute-done((bf16[1024,128]{1,0:T(8,128)(2,1)S(1)}, bf16[1024,128]{1,0:T(8,128)(2,1)S(1)}, u32[]{:S(2)}, u32[]{:S(2)}) %collective-permute-start.2) | collective-permute-done | bytes 262176 | tf_op jit(solution)/shard_map/ppermute | solution.py:532
  73.3 0.0 collective-permute-done.1.refs_1_
  73.3 0.3 shard_map.252
  73.6 24.5 %all_to_all.20.refs_0_ = bf16[64,80,128]{2,1,0:T(8,128)(2,1)S(1)} all-to-all(bf16[64,80,128]{2,1,0:T(8,128)(2,1)S(1)} %shard_map.252), channel_id=1, replica_groups={{0,2,4,6,8,10,12,14,16,18,20,22,24,26,28,30,32,34,36,38,40,42,44,46,48,..., dimensions={0} | all-to-all | bytes 2621440 | tf_op jit(solution)/shard_map/all_to_all | solution.py:529
  98.1 1.2 shard_map.253
  99.4 2.5 %collective-permute-start.3 = (bf16[64,40,128]{2,1,0:T(8,128)(2,1)S(1)}, bf16[64,40,128]{2,1,0:T(8,128)(2,1)S(1)}, u32[]{:S(2)}, u32[]{:S(2)}) collective-permute-start(bf16[64,40,128]{2,1,0:T(8,128)(2,1)S(1)} %get-tuple-element.71.refs_2_), channel_id=1, source_target_pairs={{0,1},{1,0},{2,3},{3,2},{4,5},{5,4},{6,7},{7,6},{8,9},{9,8},{10,11... | collective-permute-start | bytes 1966088 | tf_op jit(solution)/shard_map/ppermute | solution.py:532
  101.9 4.6 %all-to-all-start.3 = ((bf16[64,40,128]{2,1,0:T(8,128)(2,1)}), bf16[64,40,128]{2,1,0:T(8,128)(2,1)S(1)}, u32[]{:S(2)}, u32[]{:S(2)}) async-start(bf16[64,40,128]{2,1,0:T(8,128)(2,1)} %get-tuple-element.70), calls=%async_computation.3 | async-start | bytes 1310720 | tf_op jit(solution)/shard_map/all_to_all | solution.py:529
  106.6 0.0 copy-start.2
  106.6 0.0 copy-start.5
  106.6 0.8 copy-done.24
  107.5 4.9 %shard_map.254 = (f32[1024,512]{1,0:T(8,128)}, f32[192,512]{1,0:T(8,128)}) custom-call(bf16[64,64,128]{2,1,0:T(8,128)(2,1)} %copy-done.22, bf16[64,64,128]{2,1,0:T(8,128)(2,1)} %copy-done.23, bf16[64,40,128]{2,1,0:T(8,128)(2,1)} %copy-done.9, bf16[64,40,128]{2,1,0:T(8,128)(2,1)} %copy-done.24), custom_call_target="tpu_custom_call" | custom-call | flops 1000000000 | bytes 10000000 | tf_op jit(solution)/shard_map/pallas_call | solution.py:506
  112.4 8.2 %all-to-all-done.3.refs_1_ = bf16[64,40,128]{2,1,0:T(8,128)(2,1)S(1)} async-done(((bf16[64,40,128]{2,1,0:T(8,128)(2,1)}), bf16[64,40,128]{2,1,0:T(8,128)(2,1)S(1)}, u32[]{:S(2)}, u32[]{:S(2)}) %all-to-all-start.3) | async-done | bytes 655392 | tf_op jit(solution)/shard_map/all_to_all | solution.py:529
  120.6 1.6 %collective-permute-start.4 = (bf16[64,40,128]{2,1,0:T(8,128)(2,1)S(1)}, bf16[64,40,128]{2,1,0:T(8,128)(2,1)S(1)}, u32[]{:S(2)}, u32[]{:S(2)}) collective-permute-start(bf16[64,40,128]{2,1,0:T(8,128)(2,1)S(1)} %all-to-all-done.3.refs_1_), channel_id=1, source_target_pairs={{0,1},{1,0},{2,3},{3,2},{4,5},{5,4},{6,7},{7,6},{8,9},{9,8},{10,11... | collective-permute-start | bytes 1966088 | tf_op jit(solution)/shard_map/ppermute | solution.py:532
  122.2 1.7 %collective-permute-done.4.refs_2_ = bf16[64,40,128]{2,1,0:T(8,128)(2,1)S(1)} collective-permute-done((bf16[64,40,128]{2,1,0:T(8,128)(2,1)S(1)}, bf16[64,40,128]{2,1,0:T(8,128)(2,1)S(1)}, u32[]{:S(2)}, u32[]{:S(2)}) %collective-permute-start.4) | collective-permute-done | bytes 655392 | tf_op jit(solution)/shard_map/ppermute | solution.py:532
  123.9 1.0 copy-done.19
  124.9 4.5 %shard_map.255 = (f32[192,432]{1,0:T(8,128)}, f32[9,432]{1,0:T(8,128)}, f32[3,432]{1,0:T(4,128)}, f32[192,432]{1,0:T(8,128)}, f32[192,432]{1,0:T(8,128)}, /*inde...) custom-call(s32[1]{0:T(128)} %bitcast.refs_0_, ...), custom_call_target="tpu_custom_call" | custom-call | flops 1000000000 | bytes 10000000 | tf_op jit(solution)/shard_map/pallas_call | solution.py:506
  (31 shorter events, 0.1 us)
Async XLA Ops:
  0.6 2.1 %copy-start.7 = (f32[4,512]{1,0:T(4,128)S(1)}, f32[4,512]{1,0:T(4,128)}, u32[]{:S(2)}) copy-start(f32[4,512]{1,0:T(4,128)} %refs_3_.5) | copy-start | bytes 24580
  0.7 2.1 %copy-start.8 = (s32[4]{0:T(128)S(1)}, s32[4]{0:T(128)}, u32[]{:S(2)}) copy-start(s32[4]{0:T(128)} %refs_1_.3) | copy-start | bytes 52
  0.7 2.1 %copy-start.17 = (bf16[3,432]{1,0:T(4,128)(2,1)S(1)}, bf16[3,432]{1,0:T(4,128)(2,1)}, u32[]{:S(2)}) copy-start(bf16[3,432]{1,0:T(4,128)(2,1)} %refs_10_.3) | copy-start | bytes 7780
  0.7 2.1 %copy-start.15 = (bf16[9,432]{1,0:T(8,128)(2,1)S(1)}, bf16[9,432]{1,0:T(8,128)(2,1)}, u32[]{:S(2)}) copy-start(bf16[9,432]{1,0:T(8,128)(2,1)} %refs_9_.3) | copy-start | bytes 23332
  0.7 2.1 %copy-start.12 = (bf16[192,432]{1,0:T(8,128)(2,1)S(1)}, bf16[192,432]{1,0:T(8,128)(2,1)}, u32[]{:S(2)}) copy-start(bf16[192,432]{1,0:T(8,128)(2,1)} %refs_8_.4) | copy-start | bytes 497668
  0.7 2.1 %copy-start.16 = (bf16[3,432]{1,0:T(4,128)(2,1)S(1)}, bf16[3,432]{1,0:T(4,128)(2,1)}, u32[]{:S(2)}) copy-start(bf16[3,432]{1,0:T(4,128)(2,1)} %refs_6_.5) | copy-start | bytes 7780
  0.7 2.1 %copy-start.14 = (bf16[9,432]{1,0:T(8,128)(2,1)S(1)}, bf16[9,432]{1,0:T(8,128)(2,1)}, u32[]{:S(2)}) copy-start(bf16[9,432]{1,0:T(8,128)(2,1)} %refs_5_.6) | copy-start | bytes 23332
  0.7 2.1 %copy-start.10 = (bf16[192,432]{1,0:T(8,128)(2,1)S(1)}, bf16[192,432]{1,0:T(8,128)(2,1)}, u32[]{:S(2)}) copy-start(bf16[192,432]{1,0:T(8,128)(2,1)} %refs_4_.6) | copy-start | bytes 497668
  0.7 2.1 %copy-start.13 = (bf16[432,192]{0,1:T(8,128)(2,1)S(1)}, bf16[432,192]{0,1:T(8,128)(2,1)}, u32[]{:S(2)}) copy-start(bf16[432,192]{0,1:T(8,128)(2,1)} %param.28) | copy-start | bytes 497668
  0.8 2.1 %copy-start.11 = (bf16[432,192]{0,1:T(8,128)(2,1)S(1)}, bf16[432,192]{0,1:T(8,128)(2,1)}, u32[]{:S(2)}) copy-start(bf16[432,192]{0,1:T(8,128)(2,1)} %param.24) | copy-start | bytes 497668
  0.8 2.1 %copy-start.18 = (s32[32]{0:T(128)S(1)}, s32[32]{0:T(128)}, u32[]{:S(2)}) copy-start(s32[32]{0:T(128)} %param.17) | copy-start | bytes 388
  2.7 4.6 %copy-start = (bf16[32,4,4,4,192]{4,0,3,2,1:T(8,128)(2,1)}, bf16[32,4,4,4,192]{4,0,3,2,1:T(8,128)(2,1)S(1)}, u32[]{:S(2)}) copy-start(bf16[32,4,4,4,192]{4,0,3,2,1:T(8,128)(2,1)S(1)} %copy.28) | copy-start | bytes 2359300
  7.3 29.2 %all-to-all-start = ((bf16[64,64,128]{2,1,0:T(8,128)(2,1)}), bf16[64,64,128]{2,1,0:T(8,128)(2,1)S(1)}, u32[]{:S(2)}, u32[]{:S(2)}) async-start(bf16[64,64,128]{2,1,0:T(8,128)(2,1)} %shard_map.247), calls=%async_computation | async-start | bytes 2097152 | tf_op jit(solution)/shard_map/all_to_all | solution.py:529
  36.5 4.8 %copy-start.22 = (bf16[64,64,128]{2,1,0:T(8,128)(2,1)}, bf16[64,64,128]{2,1,0:T(8,128)(2,1)S(1)}, u32[]{:S(2)}) copy-start(bf16[64,64,128]{2,1,0:T(8,128)(2,1)S(1)} %all-to-all-done.refs_2_.refs_0_) | copy-start | bytes 3145732
  36.5 4.7 %collective-permute-start = (bf16[64,64,128]{2,1,0:T(8,128)(2,1)S(1)}, bf16[64,64,128]{2,1,0:T(8,128)(2,1)S(1)}, u32[]{:S(2)}, u32[]{:S(2)}) collective-permute-start(bf16[64,64,128]{2,1,0:T(8,128)(2,1)S(1)} %all-to-all-done.refs_2_.refs_0_), channel_id=1, source_target_pairs={{0,1},{1,0},{2,3},{3,2},{4,5},{5,4},{6,7},{7,6},{8,9},{9,8},{10,11... | collective-permute-start | bytes 3145736 | tf_op jit(solution)/shard_map/ppermute | solution.py:532
  41.3 1.1 copy-start.23
  49.6 15.0 %copy-start.1 = (bf16[32,4,4,4,192]{4,0,3,2,1:T(8,128)(2,1)S(1)}, bf16[32,4,4,4,192]{4,0,3,2,1:T(8,128)(2,1)}, u32[]{:S(2)}) copy-start(bf16[32,4,4,4,192]{4,0,3,2,1:T(8,128)(2,1)} %copy-done) | copy-start | bytes 2359300
  49.6 15.0 %copy-start.3 = (bf16[576,432]{1,0:T(8,128)(2,1)S(1)}, bf16[576,432]{1,0:T(8,128)(2,1)}, u32[]{:S(2)}) copy-start(bf16[576,432]{1,0:T(8,128)(2,1)} %get-tuple-element.62.refs_4_) | copy-start | bytes 1492996
  49.6 15.0 %copy-start.4 = (bf16[512,192]{1,0:T(8,128)(2,1)S(1)}, bf16[512,192]{1,0:T(8,128)(2,1)}, u32[]{:S(2)}) copy-start(bf16[512,192]{1,0:T(8,128)(2,1)} %get-tuple-element.63.refs_5_) | copy-start | bytes 589828
  49.6 15.0 %copy-start.6 = (f32[56,432]{1,0:T(8,128)S(1)}, f32[56,432]{1,0:T(8,128)}, u32[]{:S(2)}) copy-start(f32[56,432]{1,0:T(8,128)} %get-tuple-element.61.refs_3_) | copy-start | bytes 290308
  49.6 15.0 %all-to-all-start.1 = ((bf16[128,8,128]{2,1,0:T(8,128)(2,1)}), bf16[128,8,128]{2,1,0:T(8,128)(2,1)S(1)}, u32[]{:S(2)}, u32[]{:S(2)}) async-start(bf16[128,8,128]{2,1,0:T(8,128)(2,1)} %get-tuple-element.57), calls=%async_computation.1 | async-start | bytes 524288 | tf_op jit(solution)/shard_map/all_to_all | solution.py:558
  64.6 7.0 %copy-start.25 = (bf16[1024,128]{1,0:T(8,128)(2,1)S(1)}, bf16[1024,128]{1,0:T(8,128)(2,1)}, u32[]{:S(2)}) copy-start(bf16[1024,128]{1,0:T(8,128)(2,1)} %get-tuple-element.68) | copy-start | bytes 786436
  64.6 8.7 %copy-start.20 = (bf16[1024,128]{1,0:T(8,128)(2,1)S(1)}, bf16[1024,128]{1,0:T(8,128)(2,1)}, u32[]{:S(2)}) copy-start(bf16[1024,128]{1,0:T(8,128)(2,1)} %get-tuple-element.67.refs_2_) | copy-start | bytes 786436
  64.6 8.7 %copy-start.21 = (bf16[48,128]{1,0:T(8,128)(2,1)S(1)}, bf16[48,128]{1,0:T(8,128)(2,1)}, u32[]{:S(2)}) copy-start(bf16[48,128]{1,0:T(8,128)(2,1)} %get-tuple-element.69.refs_4_) | copy-start | bytes 36868
  70.4 2.9 %collective-permute-start.1 = (bf16[1536,128]{1,0:T(8,128)(2,1)S(1)}, bf16[1536,128]{1,0:T(8,128)(2,1)S(1)}, u32[]{:S(2)}, u32[]{:S(2)}) collective-permute-start(bf16[1536,128]{1,0:T(8,128)(2,1)S(1)} %get-tuple-element.66), channel_id=1, source_target_pairs={{0,1},{1,0},{2,3},{3,2},{4,5},{5,4},{6,7},{7,6},{8,9},{9,8},{10,11... | collective-permute-start | bytes 1179656 | tf_op jit(solution)/shard_map/ppermute | solution.py:532
  71.6 1.7 %collective-permute-start.2 = (bf16[1024,128]{1,0:T(8,128)(2,1)S(1)}, bf16[1024,128]{1,0:T(8,128)(2,1)S(1)}, u32[]{:S(2)}, u32[]{:S(2)}) collective-permute-start(bf16[1024,128]{1,0:T(8,128)(2,1)S(1)} %copy-done.25), channel_id=1, source_target_pairs={{0,1},{1,0},{2,3},{3,2},{4,5},{5,4},{6,7},{7,6},{8,9},{9,8},{10,11... | collective-permute-start | bytes 786440 | tf_op jit(solution)/shard_map/ppermute | solution.py:532
  99.4 7.2 %copy-start.9 = (bf16[64,40,128]{2,1,0:T(8,128)(2,1)}, bf16[64,40,128]{2,1,0:T(8,128)(2,1)S(1)}, u32[]{:S(2)}) copy-start(bf16[64,40,128]{2,1,0:T(8,128)(2,1)S(1)} %get-tuple-element.71.refs_2_) | copy-start | bytes 1966084
  99.4 7.2 %collective-permute-start.3 = (bf16[64,40,128]{2,1,0:T(8,128)(2,1)S(1)}, bf16[64,40,128]{2,1,0:T(8,128)(2,1)S(1)}, u32[]{:S(2)}, u32[]{:S(2)}) collective-permute-start(bf16[64,40,128]{2,1,0:T(8,128)(2,1)S(1)} %get-tuple-element.71.refs_2_), channel_id=1, source_target_pairs={{0,1},{1,0},{2,3},{3,2},{4,5},{5,4},{6,7},{7,6},{8,9},{9,8},{10,11... | collective-permute-start | bytes 1966088 | tf_op jit(solution)/shard_map/ppermute | solution.py:532
  101.9 18.6 %all-to-all-start.3 = ((bf16[64,40,128]{2,1,0:T(8,128)(2,1)}), bf16[64,40,128]{2,1,0:T(8,128)(2,1)S(1)}, u32[]{:S(2)}, u32[]{:S(2)}) async-start(bf16[64,40,128]{2,1,0:T(8,128)(2,1)} %get-tuple-element.70), calls=%async_computation.3 | async-start | bytes 1310720 | tf_op jit(solution)/shard_map/all_to_all | solution.py:529
  106.6 17.3 %copy-start.2 = (bf16[512,1024]{1,0:T(8,128)(2,1)S(1)}, bf16[512,1024]{1,0:T(8,128)(2,1)}, u32[]{:S(2)}) copy-start(bf16[512,1024]{1,0:T(8,128)(2,1)} %refs_5_.9) | copy-start | bytes 3145732
  106.6 17.3 %copy-start.5 = (bf16[192,512]{1,0:T(8,128)(2,1)S(1)}, bf16[192,512]{1,0:T(8,128)(2,1)}, u32[]{:S(2)}) copy-start(bf16[192,512]{1,0:T(8,128)(2,1)} %refs_4_.9) | copy-start | bytes 589828
  106.6 0.8 copy-start.24
  120.6 3.3 %collective-permute-start.4 = (bf16[64,40,128]{2,1,0:T(8,128)(2,1)S(1)}, bf16[64,40,128]{2,1,0:T(8,128)(2,1)S(1)}, u32[]{:S(2)}, u32[]{:S(2)}) collective-permute-start(bf16[64,40,128]{2,1,0:T(8,128)(2,1)S(1)} %all-to-all-done.3.refs_1_), channel_id=1, source_target_pairs={{0,1},{1,0},{2,3},{3,2},{4,5},{5,4},{6,7},{7,6},{8,9},{9,8},{10,11... | collective-permute-start | bytes 1966088 | tf_op jit(solution)/shard_map/ppermute | solution.py:532
  123.9 1.0 copy-start.19

commit v5 on v4

--- a/solution.py
+++ b/solution.py
@@ -206,9 +206,16 @@
         high = ref[:, 32:64, :].reshape(CHIPS * ITEMS_HERE, 128)
         return jnp.concatenate([low, high], axis=1)
 
+    across = lax.broadcasted_iota(jnp.int32, (ROWS, ROWS), 1)
+    down_rows = lax.broadcasted_iota(jnp.int32, (ROWS, ROWS), 0)
+    owner_row = jnp.sum(jnp.where(across == down_rows, owner.astype(F32), 0.0), axis=0, keepdims=True).astype(jnp.int32)
+    earlier = down_rows < across
+    rank = jnp.sum(((owner == owner_row) & earlier).astype(F32), axis=0, keepdims=True).astype(jnp.int32)
+    slot = owner_row * 8 + rank
+    sent_at = lax.broadcasted_iota(jnp.int32, (DEVICES * 8, ROWS), 0)
+    put_low = (sent_at == slot).astype(F32).astype(BF)
+    put_high = (sent_at == slot + CAPACITY).astype(F32).astype(BF)
     own, other = own.ready(), other.ready()
-    for late in (project, up, down):
-        late.begin()
     picked = (dot_nn(pick_own, rows_of(own)) + dot_nn(pick_other, rows_of(other))).astype(BF)
     picked_out[...] = picked
     picked_out.leave()
@@ -223,15 +230,6 @@
     low = jnp.where(lane < 96, low, jnp.where(lane == 96, tag, 0.0)).astype(BF)
     high = jnp.where(lane >= 32, high, jnp.where(lane == 0, tag, 0.0)).astype(BF)
 
-    across = lax.broadcasted_iota(jnp.int32, (ROWS, ROWS), 1)
-    down_rows = lax.broadcasted_iota(jnp.int32, (ROWS, ROWS), 0)
-    owner_row = jnp.sum(jnp.where(across == down_rows, owner.astype(F32), 0.0), axis=0, keepdims=True).astype(jnp.int32)
-    earlier = down_rows < across
-    rank = jnp.sum(((owner == owner_row) & earlier).astype(F32), axis=0, keepdims=True).astype(jnp.int32)
-    slot = owner_row * 8 + rank
-    sent_at = lax.broadcasted_iota(jnp.int32, (DEVICES * 8, ROWS), 0)
-    put_low = (sent_at == slot).astype(F32).astype(BF)
-    put_high = (sent_at == slot + CAPACITY).astype(F32).astype(BF)
     back = (dot_nn(put_low, low) + dot_nn(put_high, high)).astype(BF)
     sent[...] = back.reshape(DEVICES, 8, 128)
 
@@ -269,8 +267,6 @@
 ):
     taps1, frame1, taps2, frame2 = taps[0:9], taps[9:12], taps[12:21], taps[21:24]
     counts = taps[24:56, 0:1]
-    inner.ready(), weights.ready(), o1.ready()
-    p2, e2, p1 = weights[0:192], weights[192:384], weights[384:576]
 
     def tile_sum(v):
         return jnp.sum(v.reshape(-1, 8, E), axis=0)
@@ -290,6 +286,8 @@
     out_grad = jnp.concatenate(
         [(shared * (counts > f).astype(F32)).astype(BF) for f in range(FRAMES)], axis=0
     )
+    inner.ready(), weights.ready(), o1.ready()
+    p2, e2, p1 = weights[0:192], weights[192:384], weights[384:576]
     wide[576:768, 0:E] = dot_tn(out_grad, inner[AT_N2 : AT_N2 + 4].reshape(FRAMES * ITEMS_HERE, E))
     summed_grad = dot_nn(out_grad, p2).reshape(FRAMES, ITEMS_HERE, E) * inner[AT_H2 : AT_H2 + 4].astype(F32)
     spread = []
@@ -408,7 +406,7 @@
 def finish(
     core, mine, theirs, item_base, project, up,
     ge1, gs1, gt1, gp1, ge2, gs2, gt2, gp2, grad_item, grad_up,
-    halves,
+    halves, part_sems,
 ):
     halves[core[0]] = mine[...]
     halves[1 - core[0]] = theirs[...]
@@ -427,12 +425,18 @@
     gs2[...] = small[76:85]
     gt2[...] = small[85:88]
     item = item_base[...]
+    parts = []
     for j in range(FH // 128):
         part = halves[j // 4, :, 24:40, :].reshape(1024, 128)[(j % 4) * 256 : (j % 4) * 256 + C]
         cut = slice(j * 128, (j + 1) * 128)
         grad_up[:, cut] = dot_tn(project[...], part)
         item = item + dot_nt(part, up[:, cut])
+        if j % 2:
+            parts.append(grad_up.leave_part((slice(None), pl.ds((j - 1) * 128, 256)), part_sems.at[j // 2]))
     grad_item[...] = item
+    grad_item.leave()
+    for part in parts:
+        part.wait()
 
 
 def shape(dims, dtype=BF):
@@ -466,6 +470,11 @@
     def __setitem__(self, index, value):
         self.ref[index] = value
 
+    def leave_part(self, index, semaphore):
+        part = pltpu.make_async_copy(self.ref.at[index], self.target.at[index], semaphore)
+        part.start()
+        return part
+
     def leave(self, source=None):
         source = self.ref if source is None else source
         self.copy = pltpu.make_async_copy(source, self.target, self.semaphore)
@@ -474,7 +483,7 @@
 
 def call(kernel, outs, places, out_places, scratch=(), unstaged=(), megabytes=58):
     staged_in = [i for i, p in enumerate(places) if p in "hw"]
-    staged_out = [i for i, p in enumerate(out_places) if p == "h"]
+    staged_out = [i for i, p in enumerate(out_places) if p in "hw"]
     spaces = {"s": pltpu.SMEM, "v": pltpu.VMEM, "h": pl.ANY, "w": pl.ANY}
 
     def run(*args):
@@ -498,10 +507,11 @@
             for i in staged_in:
                 ins[i].ready()
             for i in staged_out:
-                if results[i].copy is None:
+                if results[i].copy is None and out_places[i] == "h":
                     results[i].leave()
             for i in staged_out:
-                results[i].copy.wait()
+                if results[i].copy is not None:
+                    results[i].copy.wait()
 
         return pl.pallas_call(
             body,
@@ -552,7 +562,7 @@
     own = across_chips(block)
     own, (taps, kept_weights, outer, inner, o1) = lax.optimization_barrier((own, kept))
     other = swap(own)
-    sent, picked = call(tower, [shape((DEVICES, 8, 128)), shape((ROWS, 256))], "sshhvvwww", "hh")(
+    sent, picked = call(tower, [shape((DEVICES, 8, 128)), shape((ROWS, 256))], "sshhvvhhh", "hh")(
         core, lengths, own, other, histories, user_cotangent, item_project, tower_up, tower_down
     )
     back = lax.all_to_all(sent, AXES, 0, 0, tiled=True)
@@ -590,14 +600,14 @@
     grad_down, item_base = call(finish_low_rank, [shape((FH, D), F32), shape((C, D), F32)], "hhhh", "hh")(
         own, other, factors, swap(factors)
     )
-    fourth, item_base = lax.optimization_barrier((fourth, item_base))
+    fourth, _ = lax.optimization_barrier((fourth, item_base))
     *conv_grads, grad_item, grad_up = call(
         finish,
         [shape((C, E), F32), shape((9, E), F32), shape((3, E), F32), shape((C, E), F32)] * 2
         + [shape((C, D), F32), shape((D, FH), F32)],
         "svvhhh",
-        "hvvhhvvhhh",
-        [pltpu.VMEM((2, CHIPS, 40, 128), BF)],
+        "hvvhhvvhhw",
+        [pltpu.VMEM((2, CHIPS, 40, 128), BF), pltpu.SemaphoreType.DMA((4,))],
         megabytes=32,
     )(core, fourth, swap(fourth), item_base, item_project, tower_up)
     conv_grads[3] = conv_grads[3].T

time: 130 us -> 129 us (level)
  Pallas kernels: 43.1 us -> 41.8 us
    pallas_call x9, Pallas kernels: 43.1 us -> 41.8 us  [run(): pl.pallas_call(body, out_shape=outs, in_specs=[pl.BlockSpec(memory_space=...]
where the time goes in v5:
time: 129 us; the launch traced here: 128 us
  Pallas kernels  41.8 us (32%)
  starting transfers between devices  28.2 us (22%)
  waiting for transfers between devices  27.3 us (21%)
  blocking collectives  24.5 us (19%)
  local copies, waits for them, and re-layouts  4.99 us (4%)
    pallas_call x9, Pallas kernels, run(): pl.pallas_call(body, out_shape=outs, in_specs=[pl.BlockSpec(memory_space=...  41.8 us
    all_to_all x1, blocking collectives, across_chips(): lax.all_to_all(v, AXES, 0, 0, axis_index_groups=same_core, tiled=True)  24.5 us
    all_to_all x2, starting transfers between devices, across_chips(): lax.all_to_all(v, AXES, 0, 0, axis_index_groups=same_core, tiled=True)  16.6 us
    all_to_all x2, waiting for transfers between devices, across_chips(): lax.all_to_all(v, AXES, 0, 0, axis_index_groups=same_core, tiled=True)  16.1 us
    ppermute x5, starting transfers between devices, swap(): return lax.ppermute(v, 'seq', [(i, i ^ 1) for i in range(8)])  7.68 us
    ppermute x5, waiting for transfers between devices, swap(): return lax.ppermute(v, 'seq', [(i, i ^ 1) for i in range(8)])  5.64 us
    all_to_all x1, waiting for transfers between devices, local(): back = lax.all_to_all(sent, AXES, 0, 0, tiled=True)  5.55 us
    unnamed x53, local copies, waits for them, and re-layouts  4.99 us
  transfers between devices with their start and end apart: 8, of which 6 were waited for; matrix products, arithmetic and copies ran while one was open for 0% of the time, Pallas kernels for 15%

profile of v5, /device:TPU:1, one launch (start us, length us, event | category | flops | bytes accessed | tf_op | source)
XLA Modules:
  0.0 128.0 jit_solution(1066671697620170659)
XLA Ops:
  0.6 0.0 copy-start.7
  0.7 0.0 copy-start.8
  0.7 0.0 copy-start.17
  0.7 0.0 copy-start.15
  0.7 0.0 copy-start.12
  0.7 0.0 copy-start.16
  0.7 0.0 copy-start.14
  0.7 0.0 copy-start.10
  0.7 0.0 copy-start.13
  0.8 0.0 copy-start.11
  0.8 0.0 copy-start.18
  0.8 2.0 %copy.28 = bf16[32,4,4,4,192]{4,0,3,2,1:T(8,128)(2,1)S(1)} copy(bf16[32,4,4,4,192]{4,3,2,1,0:T(4,128)(2,1)} %param.16) | data formatting | bytes 1572864 | tf_op args[0]
  2.7 0.0 copy-start
  2.9 4.4 %shard_map.247 = bf16[64,64,128]{2,1,0:T(8,128)(2,1)} custom-call(s32[4]{0:T(128)S(1)} %copy-done.8, bf16[64,32,192]{2,1,0:T(8,128)(2,1)S(1)} %bitcast.9, s32[1,32]{1,0:T(1,128)S(1)} %bitcast.17, f32[4,512]{1,0:T(4,128)S(1)} %copy-done.7, bf16[192,432]{1,0:T(8,128)(2,1)S(1)} %copy-done.10, bf16[9,432]{1,0:T(8,128)(2,1)S(1)} %copy-done.14, ...), custom_call_target="tpu_custom_call" | custom-call | flops 1000000000 | bytes 10000000 | tf_op jit(solution)/shard_map/pallas_call | solution.py:516
  7.3 12.0 %all-to-all-start = ((bf16[64,64,128]{2,1,0:T(8,128)(2,1)}), bf16[64,64,128]{2,1,0:T(8,128)(2,1)S(1)}, u32[]{:S(2)}, u32[]{:S(2)}) async-start(bf16[64,64,128]{2,1,0:T(8,128)(2,1)} %shard_map.247), calls=%async_computation | async-start | bytes 2097152 | tf_op jit(solution)/shard_map/all_to_all | solution.py:539
  19.3 9.3 %shard_map.248 = (f32[56,432]{1,0:T(8,128)}, bf16[576,432]{1,0:T(8,128)(2,1)}, bf16[128,32,432]{2,1,0:T(8,128)(2,1)}, bf16[92,32,432]{2,1,0:T(8,128)(2,1)}, bf16[512,192]{1,0:T(8,128)(2,1)}) custom-call(s32[4]{0:T(128)} %refs_1_.3, bf16[64,32,192]{2,1,0:T(8,128)(2,1)} %bitcast.10, s32[1,32]{1,0:T(1,128)} %bitcast.16, f32[4,512]{1,0:T(4,128)} %refs_3_.5, ...), custom_call_target="tpu_custom_call" | custom-call | flops 1000000000 | bytes 10000000 | tf_op jit(solution)/shard_map/pallas_call | solution.py:516
  28.6 7.9 %all-to-all-done.refs_2_.refs_0_ = bf16[64,64,128]{2,1,0:T(8,128)(2,1)S(1)} async-done(((bf16[64,64,128]{2,1,0:T(8,128)(2,1)}), bf16[64,64,128]{2,1,0:T(8,128)(2,1)S(1)}, u32[]{:S(2)}, u32[]{:S(2)}) %all-to-all-start) | async-done | bytes 1048608 | tf_op jit(solution)/shard_map/all_to_all | solution.py:539
  36.5 2.5 %collective-permute-start = (bf16[64,64,128]{2,1,0:T(8,128)(2,1)S(1)}, bf16[64,64,128]{2,1,0:T(8,128)(2,1)S(1)}, u32[]{:S(2)}, u32[]{:S(2)}) collective-permute-start(bf16[64,64,128]{2,1,0:T(8,128)(2,1)S(1)} %all-to-all-done.refs_2_.refs_0_), channel_id=1, source_target_pairs={{0,1},{1,0},{2,3},{3,2},{4,5},{5,4},{6,7},{7,6},{8,9},{9,8},{10,11... | collective-permute-start | bytes 3145736 | tf_op jit(solution)/shard_map/ppermute | solution.py:542
  39.0 2.3 %collective-permute-done.refs_3_.refs_1_ = bf16[64,64,128]{2,1,0:T(8,128)(2,1)S(1)} collective-permute-done((bf16[64,64,128]{2,1,0:T(8,128)(2,1)S(1)}, bf16[64,64,128]{2,1,0:T(8,128)(2,1)S(1)}, u32[]{:S(2)}, u32[]{:S(2)}) %collective-permute-start) | collective-permute-done | bytes 1048608 | tf_op jit(solution)/shard_map/ppermute | solution.py:542
  41.3 1.1 copy-done.23
  42.3 7.2 %shard_map.249 = (bf16[128,8,128]{2,1,0:T(8,128)(2,1)}, bf16[256,256]{1,0:T(8,128)(2,1)}) custom-call(s32[1]{0:T(128)} %bitcast.refs_0_, s32[4]{0:T(128)} %refs_1_.3, bf16[64,64,128]{2,1,0:T(8,128)(2,1)} %copy-done.22, bf16[64,64,128]{2,1,0:T(8,128)(2,1)} %copy-done.23, s32[4,64]{1,0:T(4,128)} %refs_4_.7, f32[4,512]{1,0:T(4,128)} %refs_3_.5, ...), custom_call_target="tpu_custom_call" | custom-call | flops 1000000000 | bytes 10000000 | tf_op jit(solution)/shard_map/pallas_call | solution.py:516
  49.5 0.0 copy-start.1
  49.5 0.0 copy-start.4
  49.6 3.9 %all-to-all-start.1 = ((bf16[128,8,128]{2,1,0:T(8,128)(2,1)}), bf16[128,8,128]{2,1,0:T(8,128)(2,1)S(1)}, u32[]{:S(2)}, u32[]{:S(2)}) async-start(bf16[128,8,128]{2,1,0:T(8,128)(2,1)} %get-tuple-element.56), calls=%async_computation.1 | async-start | bytes 524288 | tf_op jit(solution)/shard_map/all_to_all | solution.py:568
  53.5 5.5 %shard_map.250 = (bf16[1024,128]{1,0:T(8,128)(2,1)}, bf16[1024,128]{1,0:T(8,128)(2,1)}, bf16[48,128]{1,0:T(8,128)(2,1)}, f32[4,512]{1,0:T(4,128)}) custom-call(s32[1]{0:T(128)} %bitcast.refs_0_, s32[4]{0:T(128)} %refs_1_.3, bf16[256,256]{1,0:T(8,128)(2,1)} %get-tuple-element.54.refs_2_, f32[4,512]{1,0:T(4,128)} %refs_3_.5, bf16[192,512]{1,0:T(8,128)(2,1)} %refs_4_.9, ...), custom_call_target="tpu_custom_call" | custom-call | flops 1000000000 | bytes 10000000 | tf_op jit(solution)/shard_map/pallas_call | solution.py:516
  59.0 5.5 %all-to-all-done.1.refs_1_ = bf16[128,8,128]{2,1,0:T(8,128)(2,1)S(1)} async-done(((bf16[128,8,128]{2,1,0:T(8,128)(2,1)}), bf16[128,8,128]{2,1,0:T(8,128)(2,1)S(1)}, u32[]{:S(2)}, u32[]{:S(2)}) %all-to-all-start.1) | async-done | bytes 262176 | tf_op jit(solution)/shard_map/all_to_all | solution.py:568
  64.5 0.0 copy-start.25
  64.6 0.0 copy-start.20
  64.6 0.0 copy-start.21
  64.6 5.0 %shard_map.251 = (bf16[1536,128]{1,0:T(8,128)(2,1)S(1)}, bf16[1536,128]{1,0:T(8,128)(2,1)S(1)}) custom-call(s32[1]{0:T(128)} %bitcast.refs_0_, bf16[128,8,128]{2,1,0:T(8,128)(2,1)S(1)} %all-to-all-done.1.refs_1_, bf16[92,32,432]{2,1,0:T(8,128)(2,1)} %get-tuple-element.59.refs_2_, f32[56,432]{1,0:T(8,128)S(1)} %copy-done.6, bf16[576,432]{1,0:T(8,128)(2,1)S(1)} %copy-done.3, ...), custom_call_target="tpu_custom_call" | custom-call | flops 1000000000 | bytes 10000000 | tf_op jit(solution)/shard_map/pallas_call | solution.py:516
  69.6 1.2 collective-permute-start.1
  70.8 0.1 collective-permute-start.2
  70.9 1.6 %collective-permute-done.2.refs_3_ = bf16[1024,128]{1,0:T(8,128)(2,1)S(1)} collective-permute-done((bf16[1024,128]{1,0:T(8,128)(2,1)S(1)}, bf16[1024,128]{1,0:T(8,128)(2,1)S(1)}, u32[]{:S(2)}, u32[]{:S(2)}) %collective-permute-start.2) | collective-permute-done | bytes 262176 | tf_op jit(solution)/shard_map/ppermute | solution.py:542
  72.5 0.0 collective-permute-done.1.refs_1_
  72.5 0.3 shard_map.252
  72.8 24.5 %all_to_all.20.refs_0_ = bf16[64,80,128]{2,1,0:T(8,128)(2,1)S(1)} all-to-all(bf16[64,80,128]{2,1,0:T(8,128)(2,1)S(1)} %shard_map.252), channel_id=1, replica_groups={{0,2,4,6,8,10,12,14,16,18,20,22,24,26,28,30,32,34,36,38,40,42,44,46,48,..., dimensions={0} | all-to-all | bytes 2621440 | tf_op jit(solution)/shard_map/all_to_all | solution.py:539
  97.3 1.2 shard_map.253
  98.6 2.3 %collective-permute-start.3 = (bf16[64,40,128]{2,1,0:T(8,128)(2,1)S(1)}, bf16[64,40,128]{2,1,0:T(8,128)(2,1)S(1)}, u32[]{:S(2)}, u32[]{:S(2)}) collective-permute-start(bf16[64,40,128]{2,1,0:T(8,128)(2,1)S(1)} %get-tuple-element.70.refs_2_), channel_id=1, source_target_pairs={{0,1},{1,0},{2,3},{3,2},{4,5},{5,4},{6,7},{7,6},{8,9},{9,8},{10,11... | collective-permute-start | bytes 1966088 | tf_op jit(solution)/shard_map/ppermute | solution.py:542
  100.9 4.6 %all-to-all-start.3 = ((bf16[64,40,128]{2,1,0:T(8,128)(2,1)}), bf16[64,40,128]{2,1,0:T(8,128)(2,1)S(1)}, u32[]{:S(2)}, u32[]{:S(2)}) async-start(bf16[64,40,128]{2,1,0:T(8,128)(2,1)} %get-tuple-element.69), calls=%async_computation.3 | async-start | bytes 1310720 | tf_op jit(solution)/shard_map/all_to_all | solution.py:539
  105.5 0.0 copy-start.2
  105.6 0.0 copy-start.5
  105.6 0.8 copy-done.24
  106.4 4.9 %shard_map.254 = (f32[1024,512]{1,0:T(8,128)}, f32[192,512]{1,0:T(8,128)}) custom-call(bf16[64,64,128]{2,1,0:T(8,128)(2,1)} %copy-done.22, bf16[64,64,128]{2,1,0:T(8,128)(2,1)} %copy-done.23, bf16[64,40,128]{2,1,0:T(8,128)(2,1)} %copy-done.9, bf16[64,40,128]{2,1,0:T(8,128)(2,1)} %copy-done.24), custom_call_target="tpu_custom_call" | custom-call | flops 1000000000 | bytes 10000000 | tf_op jit(solution)/shard_map/pallas_call | solution.py:516
  111.4 8.2 %all-to-all-done.3.refs_1_ = bf16[64,40,128]{2,1,0:T(8,128)(2,1)S(1)} async-done(((bf16[64,40,128]{2,1,0:T(8,128)(2,1)}), bf16[64,40,128]{2,1,0:T(8,128)(2,1)S(1)}, u32[]{:S(2)}, u32[]{:S(2)}) %all-to-all-start.3) | async-done | bytes 655392 | tf_op jit(solution)/shard_map/all_to_all | solution.py:539
  119.5 1.6 %collective-permute-start.4 = (bf16[64,40,128]{2,1,0:T(8,128)(2,1)S(1)}, bf16[64,40,128]{2,1,0:T(8,128)(2,1)S(1)}, u32[]{:S(2)}, u32[]{:S(2)}) collective-permute-start(bf16[64,40,128]{2,1,0:T(8,128)(2,1)S(1)} %all-to-all-done.3.refs_1_), channel_id=1, source_target_pairs={{0,1},{1,0},{2,3},{3,2},{4,5},{5,4},{6,7},{7,6},{8,9},{9,8},{10,11... | collective-permute-start | bytes 1966088 | tf_op jit(solution)/shard_map/ppermute | solution.py:542
  121.1 1.7 %collective-permute-done.4.refs_2_ = bf16[64,40,128]{2,1,0:T(8,128)(2,1)S(1)} collective-permute-done((bf16[64,40,128]{2,1,0:T(8,128)(2,1)S(1)}, bf16[64,40,128]{2,1,0:T(8,128)(2,1)S(1)}, u32[]{:S(2)}, u32[]{:S(2)}) %collective-permute-start.4) | collective-permute-done | bytes 655392 | tf_op jit(solution)/shard_map/ppermute | solution.py:542
  122.9 1.0 copy-done.19
  123.9 4.0 %shard_map.255 = (f32[192,432]{1,0:T(8,128)}, f32[9,432]{1,0:T(8,128)}, f32[3,432]{1,0:T(4,128)}, f32[192,432]{1,0:T(8,128)}, f32[192,432]{1,0:T(8,128)}, /*inde...) custom-call(s32[1]{0:T(128)} %bitcast.refs_0_, ...), custom_call_target="tpu_custom_call" | custom-call | flops 1000000000 | bytes 10000000 | tf_op jit(solution)/shard_map/pallas_call | solution.py:516
  (31 shorter events, 0.1 us)
Async XLA Ops:
  0.6 2.1 %copy-start.7 = (f32[4,512]{1,0:T(4,128)S(1)}, f32[4,512]{1,0:T(4,128)}, u32[]{:S(2)}) copy-start(f32[4,512]{1,0:T(4,128)} %refs_3_.5) | copy-start | bytes 24580
  0.7 2.1 %copy-start.8 = (s32[4]{0:T(128)S(1)}, s32[4]{0:T(128)}, u32[]{:S(2)}) copy-start(s32[4]{0:T(128)} %refs_1_.3) | copy-start | bytes 52
  0.7 2.1 %copy-start.17 = (bf16[3,432]{1,0:T(4,128)(2,1)S(1)}, bf16[3,432]{1,0:T(4,128)(2,1)}, u32[]{:S(2)}) copy-start(bf16[3,432]{1,0:T(4,128)(2,1)} %refs_10_.3) | copy-start | bytes 7780
  0.7 2.1 %copy-start.15 = (bf16[9,432]{1,0:T(8,128)(2,1)S(1)}, bf16[9,432]{1,0:T(8,128)(2,1)}, u32[]{:S(2)}) copy-start(bf16[9,432]{1,0:T(8,128)(2,1)} %refs_9_.3) | copy-start | bytes 23332
  0.7 2.1 %copy-start.12 = (bf16[192,432]{1,0:T(8,128)(2,1)S(1)}, bf16[192,432]{1,0:T(8,128)(2,1)}, u32[]{:S(2)}) copy-start(bf16[192,432]{1,0:T(8,128)(2,1)} %refs_8_.4) | copy-start | bytes 497668
  0.7 2.1 %copy-start.16 = (bf16[3,432]{1,0:T(4,128)(2,1)S(1)}, bf16[3,432]{1,0:T(4,128)(2,1)}, u32[]{:S(2)}) copy-start(bf16[3,432]{1,0:T(4,128)(2,1)} %refs_6_.5) | copy-start | bytes 7780
  0.7 2.1 %copy-start.14 = (bf16[9,432]{1,0:T(8,128)(2,1)S(1)}, bf16[9,432]{1,0:T(8,128)(2,1)}, u32[]{:S(2)}) copy-start(bf16[9,432]{1,0:T(8,128)(2,1)} %refs_5_.6) | copy-start | bytes 23332
  0.7 2.1 %copy-start.10 = (bf16[192,432]{1,0:T(8,128)(2,1)S(1)}, bf16[192,432]{1,0:T(8,128)(2,1)}, u32[]{:S(2)}) copy-start(bf16[192,432]{1,0:T(8,128)(2,1)} %refs_4_.6) | copy-start | bytes 497668
  0.7 2.1 %copy-start.13 = (bf16[432,192]{0,1:T(8,128)(2,1)S(1)}, bf16[432,192]{0,1:T(8,128)(2,1)}, u32[]{:S(2)}) copy-start(bf16[432,192]{0,1:T(8,128)(2,1)} %param.28) | copy-start | bytes 497668
  0.8 2.1 %copy-start.11 = (bf16[432,192]{0,1:T(8,128)(2,1)S(1)}, bf16[432,192]{0,1:T(8,128)(2,1)}, u32[]{:S(2)}) copy-start(bf16[432,192]{0,1:T(8,128)(2,1)} %param.24) | copy-start | bytes 497668
  0.8 2.1 %copy-start.18 = (s32[32]{0:T(128)S(1)}, s32[32]{0:T(128)}, u32[]{:S(2)}) copy-start(s32[32]{0:T(128)} %param.17) | copy-start | bytes 388
  2.7 4.6 %copy-start = (bf16[32,4,4,4,192]{4,0,3,2,1:T(8,128)(2,1)}, bf16[32,4,4,4,192]{4,0,3,2,1:T(8,128)(2,1)S(1)}, u32[]{:S(2)}) copy-start(bf16[32,4,4,4,192]{4,0,3,2,1:T(8,128)(2,1)S(1)} %copy.28) | copy-start | bytes 2359300
  7.3 29.2 %all-to-all-start = ((bf16[64,64,128]{2,1,0:T(8,128)(2,1)}), bf16[64,64,128]{2,1,0:T(8,128)(2,1)S(1)}, u32[]{:S(2)}, u32[]{:S(2)}) async-start(bf16[64,64,128]{2,1,0:T(8,128)(2,1)} %shard_map.247), calls=%async_computation | async-start | bytes 2097152 | tf_op jit(solution)/shard_map/all_to_all | solution.py:539
  36.5 4.8 %copy-start.22 = (bf16[64,64,128]{2,1,0:T(8,128)(2,1)}, bf16[64,64,128]{2,1,0:T(8,128)(2,1)S(1)}, u32[]{:S(2)}) copy-start(bf16[64,64,128]{2,1,0:T(8,128)(2,1)S(1)} %all-to-all-done.refs_2_.refs_0_) | copy-start | bytes 3145732
  36.5 4.7 %collective-permute-start = (bf16[64,64,128]{2,1,0:T(8,128)(2,1)S(1)}, bf16[64,64,128]{2,1,0:T(8,128)(2,1)S(1)}, u32[]{:S(2)}, u32[]{:S(2)}) collective-permute-start(bf16[64,64,128]{2,1,0:T(8,128)(2,1)S(1)} %all-to-all-done.refs_2_.refs_0_), channel_id=1, source_target_pairs={{0,1},{1,0},{2,3},{3,2},{4,5},{5,4},{6,7},{7,6},{8,9},{9,8},{10,11... | collective-permute-start | bytes 3145736 | tf_op jit(solution)/shard_map/ppermute | solution.py:542
  41.3 1.1 copy-start.23
  49.5 15.0 %copy-start.1 = (bf16[32,4,4,4,192]{4,0,3,2,1:T(8,128)(2,1)S(1)}, bf16[32,4,4,4,192]{4,0,3,2,1:T(8,128)(2,1)}, u32[]{:S(2)}) copy-start(bf16[32,4,4,4,192]{4,0,3,2,1:T(8,128)(2,1)} %copy-done) | copy-start | bytes 2359300
  49.5 15.0 %copy-start.3 = (bf16[576,432]{1,0:T(8,128)(2,1)S(1)}, bf16[576,432]{1,0:T(8,128)(2,1)}, u32[]{:S(2)}) copy-start(bf16[576,432]{1,0:T(8,128)(2,1)} %get-tuple-element.61.refs_4_) | copy-start | bytes 1492996
  49.5 15.0 %copy-start.4 = (bf16[512,192]{1,0:T(8,128)(2,1)S(1)}, bf16[512,192]{1,0:T(8,128)(2,1)}, u32[]{:S(2)}) copy-start(bf16[512,192]{1,0:T(8,128)(2,1)} %get-tuple-element.62.refs_5_) | copy-start | bytes 589828
  49.6 15.0 %copy-start.6 = (f32[56,432]{1,0:T(8,128)S(1)}, f32[56,432]{1,0:T(8,128)}, u32[]{:S(2)}) copy-start(f32[56,432]{1,0:T(8,128)} %get-tuple-element.60.refs_3_) | copy-start | bytes 290308
  49.6 15.0 %all-to-all-start.1 = ((bf16[128,8,128]{2,1,0:T(8,128)(2,1)}), bf16[128,8,128]{2,1,0:T(8,128)(2,1)S(1)}, u32[]{:S(2)}, u32[]{:S(2)}) async-start(bf16[128,8,128]{2,1,0:T(8,128)(2,1)} %get-tuple-element.56), calls=%async_computation.1 | async-start | bytes 524288 | tf_op jit(solution)/shard_map/all_to_all | solution.py:568
  64.5 6.3 %copy-start.25 = (bf16[1024,128]{1,0:T(8,128)(2,1)S(1)}, bf16[1024,128]{1,0:T(8,128)(2,1)}, u32[]{:S(2)}) copy-start(bf16[1024,128]{1,0:T(8,128)(2,1)} %get-tuple-element.67) | copy-start | bytes 786436
  64.6 8.0 %copy-start.20 = (bf16[1024,128]{1,0:T(8,128)(2,1)S(1)}, bf16[1024,128]{1,0:T(8,128)(2,1)}, u32[]{:S(2)}) copy-start(bf16[1024,128]{1,0:T(8,128)(2,1)} %get-tuple-element.66.refs_2_) | copy-start | bytes 786436
  64.6 8.0 %copy-start.21 = (bf16[48,128]{1,0:T(8,128)(2,1)S(1)}, bf16[48,128]{1,0:T(8,128)(2,1)}, u32[]{:S(2)}) copy-start(bf16[48,128]{1,0:T(8,128)(2,1)} %get-tuple-element.68.refs_4_) | copy-start | bytes 36868
  69.6 2.9 %collective-permute-start.1 = (bf16[1536,128]{1,0:T(8,128)(2,1)S(1)}, bf16[1536,128]{1,0:T(8,128)(2,1)S(1)}, u32[]{:S(2)}, u32[]{:S(2)}) collective-permute-start(bf16[1536,128]{1,0:T(8,128)(2,1)S(1)} %get-tuple-element.65), channel_id=1, source_target_pairs={{0,1},{1,0},{2,3},{3,2},{4,5},{5,4},{6,7},{7,6},{8,9},{9,8},{10,11... | collective-permute-start | bytes 1179656 | tf_op jit(solution)/shard_map/ppermute | solution.py:542
  70.8 1.7 %collective-permute-start.2 = (bf16[1024,128]{1,0:T(8,128)(2,1)S(1)}, bf16[1024,128]{1,0:T(8,128)(2,1)S(1)}, u32[]{:S(2)}, u32[]{:S(2)}) collective-permute-start(bf16[1024,128]{1,0:T(8,128)(2,1)S(1)} %copy-done.25), channel_id=1, source_target_pairs={{0,1},{1,0},{2,3},{3,2},{4,5},{5,4},{6,7},{7,6},{8,9},{9,8},{10,11... | collective-permute-start | bytes 786440 | tf_op jit(solution)/shard_map/ppermute | solution.py:542
  98.6 7.0 %copy-start.9 = (bf16[64,40,128]{2,1,0:T(8,128)(2,1)}, bf16[64,40,128]{2,1,0:T(8,128)(2,1)S(1)}, u32[]{:S(2)}) copy-start(bf16[64,40,128]{2,1,0:T(8,128)(2,1)S(1)} %get-tuple-element.70.refs_2_) | copy-start | bytes 1966084
  98.6 7.0 %collective-permute-start.3 = (bf16[64,40,128]{2,1,0:T(8,128)(2,1)S(1)}, bf16[64,40,128]{2,1,0:T(8,128)(2,1)S(1)}, u32[]{:S(2)}, u32[]{:S(2)}) collective-permute-start(bf16[64,40,128]{2,1,0:T(8,128)(2,1)S(1)} %get-tuple-element.70.refs_2_), channel_id=1, source_target_pairs={{0,1},{1,0},{2,3},{3,2},{4,5},{5,4},{6,7},{7,6},{8,9},{9,8},{10,11... | collective-permute-start | bytes 1966088 | tf_op jit(solution)/shard_map/ppermute | solution.py:542
  100.9 18.6 %all-to-all-start.3 = ((bf16[64,40,128]{2,1,0:T(8,128)(2,1)}), bf16[64,40,128]{2,1,0:T(8,128)(2,1)S(1)}, u32[]{:S(2)}, u32[]{:S(2)}) async-start(bf16[64,40,128]{2,1,0:T(8,128)(2,1)} %get-tuple-element.69), calls=%async_computation.3 | async-start | bytes 1310720 | tf_op jit(solution)/shard_map/all_to_all | solution.py:539
  105.5 17.3 %copy-start.2 = (bf16[512,1024]{1,0:T(8,128)(2,1)S(1)}, bf16[512,1024]{1,0:T(8,128)(2,1)}, u32[]{:S(2)}) copy-start(bf16[512,1024]{1,0:T(8,128)(2,1)} %refs_5_.9) | copy-start | bytes 3145732
  105.6 17.3 %copy-start.5 = (bf16[192,512]{1,0:T(8,128)(2,1)S(1)}, bf16[192,512]{1,0:T(8,128)(2,1)}, u32[]{:S(2)}) copy-start(bf16[192,512]{1,0:T(8,128)(2,1)} %refs_4_.9) | copy-start | bytes 589828
  105.6 0.8 copy-start.24
  119.5 3.3 %collective-permute-start.4 = (bf16[64,40,128]{2,1,0:T(8,128)(2,1)S(1)}, bf16[64,40,128]{2,1,0:T(8,128)(2,1)S(1)}, u32[]{:S(2)}, u32[]{:S(2)}) collective-permute-start(bf16[64,40,128]{2,1,0:T(8,128)(2,1)S(1)} %all-to-all-done.3.refs_1_), channel_id=1, source_target_pairs={{0,1},{1,0},{2,3},{3,2},{4,5},{5,4},{6,7},{7,6},{8,9},{9,8},{10,11... | collective-permute-start | bytes 1966088 | tf_op jit(solution)/shard_map/ppermute | solution.py:542
  122.9 1.0 copy-start.19

commit v6 on v5

--- a/solution.py
+++ b/solution.py
@@ -481,7 +481,7 @@
         self.copy.start()
 
 
-def call(kernel, outs, places, out_places, scratch=(), unstaged=(), megabytes=58):
+def call(kernel, outs, places, out_places, scratch=(), unstaged=(), megabytes=58, aliases=None):
     staged_in = [i for i, p in enumerate(places) if p in "hw"]
     staged_out = [i for i, p in enumerate(out_places) if p in "hw"]
     spaces = {"s": pltpu.SMEM, "v": pltpu.VMEM, "h": pl.ANY, "w": pl.ANY}
@@ -519,6 +519,7 @@
             in_specs=[pl.BlockSpec(memory_space=spaces[p]) for p in places],
             out_specs=[pl.BlockSpec(memory_space=spaces[p]) for p in out_places],
             scratch_shapes=list(scratch) + stages + sems,
+            input_output_aliases=aliases or {},
             cost_estimate=pl.CostEstimate(flops=10**9, bytes_accessed=10**7, transcendentals=10**6),
             compiler_params=pltpu.CompilerParams(vmem_limit_bytes=megabytes * 1024 * 1024),
         )(*args)
@@ -600,7 +601,7 @@
     grad_down, item_base = call(finish_low_rank, [shape((FH, D), F32), shape((C, D), F32)], "hhhh", "hh")(
         own, other, factors, swap(factors)
     )
-    fourth, _ = lax.optimization_barrier((fourth, item_base))
+    fourth, item_base = lax.optimization_barrier((fourth, item_base))
     *conv_grads, grad_item, grad_up = call(
         finish,
         [shape((C, E), F32), shape((9, E), F32), shape((3, E), F32), shape((C, E), F32)] * 2
@@ -609,6 +610,7 @@
         "hvvhhvvhhw",
         [pltpu.VMEM((2, CHIPS, 40, 128), BF), pltpu.SemaphoreType.DMA((4,))],
         megabytes=32,
+        aliases={3: 8},
     )(core, fourth, swap(fourth), item_base, item_project, tower_up)
     conv_grads[3] = conv_grads[3].T
     conv_grads[7] = conv_grads[7].T

time: 129 us -> 128 us (level)
    unnamed x53 -> x51, local copies, waits for them, and re-layouts: 4.99 us -> 3.99 us
where the time goes in v6:
time: 128 us; the launch traced here: 127 us
  Pallas kernels  41.9 us (33%)
  starting transfers between devices  28.2 us (22%)
  waiting for transfers between devices  27.3 us (21%)
  blocking collectives  24.5 us (19%)
  local copies, waits for them, and re-layouts  3.99 us (3%)
    pallas_call x9, Pallas kernels, run(): pl.pallas_call(body, out_shape=outs, in_specs=[pl.BlockSpec(memory_space=...  41.9 us
    all_to_all x1, blocking collectives, across_chips(): lax.all_to_all(v, AXES, 0, 0, axis_index_groups=same_core, tiled=True)  24.5 us
    all_to_all x2, starting transfers between devices, across_chips(): lax.all_to_all(v, AXES, 0, 0, axis_index_groups=same_core, tiled=True)  16.6 us
    all_to_all x2, waiting for transfers between devices, across_chips(): lax.all_to_all(v, AXES, 0, 0, axis_index_groups=same_core, tiled=True)  16.1 us
    ppermute x5, starting transfers between devices, swap(): return lax.ppermute(v, 'seq', [(i, i ^ 1) for i in range(8)])  7.67 us
    ppermute x5, waiting for transfers between devices, swap(): return lax.ppermute(v, 'seq', [(i, i ^ 1) for i in range(8)])  5.64 us
    all_to_all x1, waiting for transfers between devices, local(): back = lax.all_to_all(sent, AXES, 0, 0, tiled=True)  5.55 us
    unnamed x51, local copies, waits for them, and re-layouts  3.99 us
  transfers between devices with their start and end apart: 8, of which 6 were waited for; matrix products, arithmetic and copies ran while one was open for 0% of the time, Pallas kernels for 15%

profile of v6, /device:TPU:1, one launch (start us, length us, event | category | flops | bytes accessed | tf_op | source)
XLA Modules:
  0.0 127.2 jit_solution(2509927983466837084)
XLA Ops:
  0.6 0.0 copy-start.7
  0.7 0.0 copy-start.8
  0.7 0.0 copy-start.17
  0.7 0.0 copy-start.15
  0.7 0.0 copy-start.12
  0.7 0.0 copy-start.16
  0.7 0.0 copy-start.14
  0.7 0.0 copy-start.10
  0.7 0.0 copy-start.13
  0.8 0.0 copy-start.11
  0.8 0.0 copy-start.18
  0.8 2.0 %copy.29 = bf16[32,4,4,4,192]{4,0,3,2,1:T(8,128)(2,1)S(1)} copy(bf16[32,4,4,4,192]{4,3,2,1,0:T(4,128)(2,1)} %param.16) | data formatting | bytes 1572864 | tf_op args[0]
  2.7 0.0 copy-start
  2.9 4.4 %shard_map.247 = bf16[64,64,128]{2,1,0:T(8,128)(2,1)} custom-call(s32[4]{0:T(128)S(1)} %copy-done.8, bf16[64,32,192]{2,1,0:T(8,128)(2,1)S(1)} %bitcast.9, s32[1,32]{1,0:T(1,128)S(1)} %bitcast.17, f32[4,512]{1,0:T(4,128)S(1)} %copy-done.7, bf16[192,432]{1,0:T(8,128)(2,1)S(1)} %copy-done.10, bf16[9,432]{1,0:T(8,128)(2,1)S(1)} %copy-done.14, ...), custom_call_target="tpu_custom_call" | custom-call | flops 1000000000 | bytes 10000000 | tf_op jit(solution)/shard_map/pallas_call | solution.py:516
  7.3 12.0 %all-to-all-start = ((bf16[64,64,128]{2,1,0:T(8,128)(2,1)}), bf16[64,64,128]{2,1,0:T(8,128)(2,1)S(1)}, u32[]{:S(2)}, u32[]{:S(2)}) async-start(bf16[64,64,128]{2,1,0:T(8,128)(2,1)} %shard_map.247), calls=%async_computation | async-start | bytes 2097152 | tf_op jit(solution)/shard_map/all_to_all | solution.py:540
  19.3 9.3 %shard_map.248 = (f32[56,432]{1,0:T(8,128)}, bf16[576,432]{1,0:T(8,128)(2,1)}, bf16[128,32,432]{2,1,0:T(8,128)(2,1)}, bf16[92,32,432]{2,1,0:T(8,128)(2,1)}, bf16[512,192]{1,0:T(8,128)(2,1)}) custom-call(s32[4]{0:T(128)} %refs_1_.3, bf16[64,32,192]{2,1,0:T(8,128)(2,1)} %bitcast.10, s32[1,32]{1,0:T(1,128)} %bitcast.16, f32[4,512]{1,0:T(4,128)} %refs_3_.5, ...), custom_call_target="tpu_custom_call" | custom-call | flops 1000000000 | bytes 10000000 | tf_op jit(solution)/shard_map/pallas_call | solution.py:516
  28.6 7.9 %all-to-all-done.refs_2_.refs_0_ = bf16[64,64,128]{2,1,0:T(8,128)(2,1)S(1)} async-done(((bf16[64,64,128]{2,1,0:T(8,128)(2,1)}), bf16[64,64,128]{2,1,0:T(8,128)(2,1)S(1)}, u32[]{:S(2)}, u32[]{:S(2)}) %all-to-all-start) | async-done | bytes 1048608 | tf_op jit(solution)/shard_map/all_to_all | solution.py:540
  36.5 2.5 %collective-permute-start = (bf16[64,64,128]{2,1,0:T(8,128)(2,1)S(1)}, bf16[64,64,128]{2,1,0:T(8,128)(2,1)S(1)}, u32[]{:S(2)}, u32[]{:S(2)}) collective-permute-start(bf16[64,64,128]{2,1,0:T(8,128)(2,1)S(1)} %all-to-all-done.refs_2_.refs_0_), channel_id=1, source_target_pairs={{0,1},{1,0},{2,3},{3,2},{4,5},{5,4},{6,7},{7,6},{8,9},{9,8},{10,11... | collective-permute-start | bytes 3145736 | tf_op jit(solution)/shard_map/ppermute | solution.py:543
  39.0 2.3 %collective-permute-done.refs_3_.refs_1_ = bf16[64,64,128]{2,1,0:T(8,128)(2,1)S(1)} collective-permute-done((bf16[64,64,128]{2,1,0:T(8,128)(2,1)S(1)}, bf16[64,64,128]{2,1,0:T(8,128)(2,1)S(1)}, u32[]{:S(2)}, u32[]{:S(2)}) %collective-permute-start) | collective-permute-done | bytes 1048608 | tf_op jit(solution)/shard_map/ppermute | solution.py:543
  41.3 1.1 copy-done.22
  42.3 7.2 %shard_map.249 = (bf16[128,8,128]{2,1,0:T(8,128)(2,1)}, bf16[256,256]{1,0:T(8,128)(2,1)}) custom-call(s32[1]{0:T(128)} %bitcast.refs_0_, s32[4]{0:T(128)} %refs_1_.3, bf16[64,64,128]{2,1,0:T(8,128)(2,1)} %copy-done.21, bf16[64,64,128]{2,1,0:T(8,128)(2,1)} %copy-done.22, s32[4,64]{1,0:T(4,128)} %refs_4_.7, f32[4,512]{1,0:T(4,128)} %refs_3_.5, ...), custom_call_target="tpu_custom_call" | custom-call | flops 1000000000 | bytes 10000000 | tf_op jit(solution)/shard_map/pallas_call | solution.py:516
  49.5 0.0 copy-start.1
  49.5 0.0 copy-start.4
  49.6 3.9 %all-to-all-start.1 = ((bf16[128,8,128]{2,1,0:T(8,128)(2,1)}), bf16[128,8,128]{2,1,0:T(8,128)(2,1)S(1)}, u32[]{:S(2)}, u32[]{:S(2)}) async-start(bf16[128,8,128]{2,1,0:T(8,128)(2,1)} %get-tuple-element.57), calls=%async_computation.1 | async-start | bytes 524288 | tf_op jit(solution)/shard_map/all_to_all | solution.py:569
  53.5 5.5 %shard_map.250 = (bf16[1024,128]{1,0:T(8,128)(2,1)}, bf16[1024,128]{1,0:T(8,128)(2,1)}, bf16[48,128]{1,0:T(8,128)(2,1)}, f32[4,512]{1,0:T(4,128)}) custom-call(s32[1]{0:T(128)} %bitcast.refs_0_, s32[4]{0:T(128)} %refs_1_.3, bf16[256,256]{1,0:T(8,128)(2,1)} %get-tuple-element.55.refs_2_, f32[4,512]{1,0:T(4,128)} %refs_3_.5, bf16[192,512]{1,0:T(8,128)(2,1)} %refs_4_.9, ...), custom_call_target="tpu_custom_call" | custom-call | flops 1000000000 | bytes 10000000 | tf_op jit(solution)/shard_map/pallas_call | solution.py:516
  59.0 5.5 %all-to-all-done.1.refs_1_ = bf16[128,8,128]{2,1,0:T(8,128)(2,1)S(1)} async-done(((bf16[128,8,128]{2,1,0:T(8,128)(2,1)}), bf16[128,8,128]{2,1,0:T(8,128)(2,1)S(1)}, u32[]{:S(2)}, u32[]{:S(2)}) %all-to-all-start.1) | async-done | bytes 262176 | tf_op jit(solution)/shard_map/all_to_all | solution.py:569
  64.6 0.0 copy-start.24
  64.6 0.0 copy-start.19
  64.6 0.0 copy-start.20
  64.6 5.0 %shard_map.251 = (bf16[1536,128]{1,0:T(8,128)(2,1)S(1)}, bf16[1536,128]{1,0:T(8,128)(2,1)S(1)}) custom-call(s32[1]{0:T(128)} %bitcast.refs_0_, bf16[128,8,128]{2,1,0:T(8,128)(2,1)S(1)} %all-to-all-done.1.refs_1_, bf16[92,32,432]{2,1,0:T(8,128)(2,1)} %get-tuple-element.60.refs_2_, f32[56,432]{1,0:T(8,128)S(1)} %copy-done.6, bf16[576,432]{1,0:T(8,128)(2,1)S(1)} %copy-done.3, ...), custom_call_target="tpu_custom_call" | custom-call | flops 1000000000 | bytes 10000000 | tf_op jit(solution)/shard_map/pallas_call | solution.py:516
  69.6 1.2 collective-permute-start.1
  70.8 0.1 collective-permute-start.2
  70.9 1.6 %collective-permute-done.2.refs_3_ = bf16[1024,128]{1,0:T(8,128)(2,1)S(1)} collective-permute-done((bf16[1024,128]{1,0:T(8,128)(2,1)S(1)}, bf16[1024,128]{1,0:T(8,128)(2,1)S(1)}, u32[]{:S(2)}, u32[]{:S(2)}) %collective-permute-start.2) | collective-permute-done | bytes 262176 | tf_op jit(solution)/shard_map/ppermute | solution.py:543
  72.5 0.0 collective-permute-done.1.refs_1_
  72.5 0.3 shard_map.252
  72.8 24.5 %all_to_all.20.refs_0_ = bf16[64,80,128]{2,1,0:T(8,128)(2,1)S(1)} all-to-all(bf16[64,80,128]{2,1,0:T(8,128)(2,1)S(1)} %shard_map.252), channel_id=1, replica_groups={{0,2,4,6,8,10,12,14,16,18,20,22,24,26,28,30,32,34,36,38,40,42,44,46,48,..., dimensions={0} | all-to-all | bytes 2621440 | tf_op jit(solution)/shard_map/all_to_all | solution.py:540
  97.3 1.3 shard_map.253
  98.6 2.3 %collective-permute-start.3 = (bf16[64,40,128]{2,1,0:T(8,128)(2,1)S(1)}, bf16[64,40,128]{2,1,0:T(8,128)(2,1)S(1)}, u32[]{:S(2)}, u32[]{:S(2)}) collective-permute-start(bf16[64,40,128]{2,1,0:T(8,128)(2,1)S(1)} %get-tuple-element.71.refs_2_), channel_id=1, source_target_pairs={{0,1},{1,0},{2,3},{3,2},{4,5},{5,4},{6,7},{7,6},{8,9},{9,8},{10,11... | collective-permute-start | bytes 1966088 | tf_op jit(solution)/shard_map/ppermute | solution.py:543
  100.9 4.6 %all-to-all-start.3 = ((bf16[64,40,128]{2,1,0:T(8,128)(2,1)}), bf16[64,40,128]{2,1,0:T(8,128)(2,1)S(1)}, u32[]{:S(2)}, u32[]{:S(2)}) async-start(bf16[64,40,128]{2,1,0:T(8,128)(2,1)} %get-tuple-element.70), calls=%async_computation.3 | async-start | bytes 1310720 | tf_op jit(solution)/shard_map/all_to_all | solution.py:540
  105.6 0.0 copy-start.2
  105.6 0.0 copy-start.5
  105.6 0.0 collective-permute-done.3.refs_3_
  105.6 0.8 copy-done.23
  106.4 4.9 %shard_map.254 = (f32[1024,512]{1,0:T(8,128)}, f32[192,512]{1,0:T(8,128)}) custom-call(bf16[64,64,128]{2,1,0:T(8,128)(2,1)} %copy-done.21, bf16[64,64,128]{2,1,0:T(8,128)(2,1)} %copy-done.22, bf16[64,40,128]{2,1,0:T(8,128)(2,1)} %copy-done.9, bf16[64,40,128]{2,1,0:T(8,128)(2,1)} %copy-done.23), custom_call_target="tpu_custom_call" | custom-call | flops 1000000000 | bytes 10000000 | tf_op jit(solution)/shard_map/pallas_call | solution.py:516
  111.4 8.2 %all-to-all-done.3.refs_1_ = bf16[64,40,128]{2,1,0:T(8,128)(2,1)S(1)} async-done(((bf16[64,40,128]{2,1,0:T(8,128)(2,1)}), bf16[64,40,128]{2,1,0:T(8,128)(2,1)S(1)}, u32[]{:S(2)}, u32[]{:S(2)}) %all-to-all-start.3) | async-done | bytes 655392 | tf_op jit(solution)/shard_map/all_to_all | solution.py:540
  119.6 1.6 %collective-permute-start.4 = (bf16[64,40,128]{2,1,0:T(8,128)(2,1)S(1)}, bf16[64,40,128]{2,1,0:T(8,128)(2,1)S(1)}, u32[]{:S(2)}, u32[]{:S(2)}) collective-permute-start(bf16[64,40,128]{2,1,0:T(8,128)(2,1)S(1)} %all-to-all-done.3.refs_1_), channel_id=1, source_target_pairs={{0,1},{1,0},{2,3},{3,2},{4,5},{5,4},{6,7},{7,6},{8,9},{9,8},{10,11... | collective-permute-start | bytes 1966088 | tf_op jit(solution)/shard_map/ppermute | solution.py:543
  121.2 1.7 %collective-permute-done.4.refs_2_ = bf16[64,40,128]{2,1,0:T(8,128)(2,1)S(1)} collective-permute-done((bf16[64,40,128]{2,1,0:T(8,128)(2,1)S(1)}, bf16[64,40,128]{2,1,0:T(8,128)(2,1)S(1)}, u32[]{:S(2)}, u32[]{:S(2)}) %collective-permute-start.4) | collective-permute-done | bytes 655392 | tf_op jit(solution)/shard_map/ppermute | solution.py:543
  122.9 4.1 %shard_map.255 = (f32[192,432]{1,0:T(8,128)}, f32[9,432]{1,0:T(8,128)}, f32[3,432]{1,0:T(4,128)}, f32[192,432]{1,0:T(8,128)}, f32[192,432]{1,0:T(8,128)}, /*inde...) custom-call(s32[1]{0:T(128)} %bitcast.refs_0_, ...), custom_call_target="tpu_custom_call", output_to_operand_aliasing={{8}: (3, {})} | custom-call | flops 1000000000 | bytes 10000000 | tf_op jit(solution)/shard_map/pallas_call | solution.py:516
  (29 shorter events, 0.1 us)
Async XLA Ops:
  0.6 2.1 %copy-start.7 = (f32[4,512]{1,0:T(4,128)S(1)}, f32[4,512]{1,0:T(4,128)}, u32[]{:S(2)}) copy-start(f32[4,512]{1,0:T(4,128)} %refs_3_.5) | copy-start | bytes 24580
  0.7 2.1 %copy-start.8 = (s32[4]{0:T(128)S(1)}, s32[4]{0:T(128)}, u32[]{:S(2)}) copy-start(s32[4]{0:T(128)} %refs_1_.3) | copy-start | bytes 52
  0.7 2.1 %copy-start.17 = (bf16[3,432]{1,0:T(4,128)(2,1)S(1)}, bf16[3,432]{1,0:T(4,128)(2,1)}, u32[]{:S(2)}) copy-start(bf16[3,432]{1,0:T(4,128)(2,1)} %refs_10_.3) | copy-start | bytes 7780
  0.7 2.1 %copy-start.15 = (bf16[9,432]{1,0:T(8,128)(2,1)S(1)}, bf16[9,432]{1,0:T(8,128)(2,1)}, u32[]{:S(2)}) copy-start(bf16[9,432]{1,0:T(8,128)(2,1)} %refs_9_.3) | copy-start | bytes 23332
  0.7 2.1 %copy-start.12 = (bf16[192,432]{1,0:T(8,128)(2,1)S(1)}, bf16[192,432]{1,0:T(8,128)(2,1)}, u32[]{:S(2)}) copy-start(bf16[192,432]{1,0:T(8,128)(2,1)} %refs_8_.4) | copy-start | bytes 497668
  0.7 2.1 %copy-start.16 = (bf16[3,432]{1,0:T(4,128)(2,1)S(1)}, bf16[3,432]{1,0:T(4,128)(2,1)}, u32[]{:S(2)}) copy-start(bf16[3,432]{1,0:T(4,128)(2,1)} %refs_6_.5) | copy-start | bytes 7780
  0.7 2.1 %copy-start.14 = (bf16[9,432]{1,0:T(8,128)(2,1)S(1)}, bf16[9,432]{1,0:T(8,128)(2,1)}, u32[]{:S(2)}) copy-start(bf16[9,432]{1,0:T(8,128)(2,1)} %refs_5_.6) | copy-start | bytes 23332
  0.7 2.1 %copy-start.10 = (bf16[192,432]{1,0:T(8,128)(2,1)S(1)}, bf16[192,432]{1,0:T(8,128)(2,1)}, u32[]{:S(2)}) copy-start(bf16[192,432]{1,0:T(8,128)(2,1)} %refs_4_.6) | copy-start | bytes 497668
  0.7 2.1 %copy-start.13 = (bf16[432,192]{0,1:T(8,128)(2,1)S(1)}, bf16[432,192]{0,1:T(8,128)(2,1)}, u32[]{:S(2)}) copy-start(bf16[432,192]{0,1:T(8,128)(2,1)} %param.28) | copy-start | bytes 497668
  0.8 2.1 %copy-start.11 = (bf16[432,192]{0,1:T(8,128)(2,1)S(1)}, bf16[432,192]{0,1:T(8,128)(2,1)}, u32[]{:S(2)}) copy-start(bf16[432,192]{0,1:T(8,128)(2,1)} %param.24) | copy-start | bytes 497668
  0.8 2.1 %copy-start.18 = (s32[32]{0:T(128)S(1)}, s32[32]{0:T(128)}, u32[]{:S(2)}) copy-start(s32[32]{0:T(128)} %param.17) | copy-start | bytes 388
  2.7 4.6 %copy-start = (bf16[32,4,4,4,192]{4,0,3,2,1:T(8,128)(2,1)}, bf16[32,4,4,4,192]{4,0,3,2,1:T(8,128)(2,1)S(1)}, u32[]{:S(2)}) copy-start(bf16[32,4,4,4,192]{4,0,3,2,1:T(8,128)(2,1)S(1)} %copy.29) | copy-start | bytes 2359300
  7.3 29.2 %all-to-all-start = ((bf16[64,64,128]{2,1,0:T(8,128)(2,1)}), bf16[64,64,128]{2,1,0:T(8,128)(2,1)S(1)}, u32[]{:S(2)}, u32[]{:S(2)}) async-start(bf16[64,64,128]{2,1,0:T(8,128)(2,1)} %shard_map.247), calls=%async_computation | async-start | bytes 2097152 | tf_op jit(solution)/shard_map/all_to_all | solution.py:540
  36.5 4.8 %copy-start.21 = (bf16[64,64,128]{2,1,0:T(8,128)(2,1)}, bf16[64,64,128]{2,1,0:T(8,128)(2,1)S(1)}, u32[]{:S(2)}) copy-start(bf16[64,64,128]{2,1,0:T(8,128)(2,1)S(1)} %all-to-all-done.refs_2_.refs_0_) | copy-start | bytes 3145732
  36.5 4.7 %collective-permute-start = (bf16[64,64,128]{2,1,0:T(8,128)(2,1)S(1)}, bf16[64,64,128]{2,1,0:T(8,128)(2,1)S(1)}, u32[]{:S(2)}, u32[]{:S(2)}) collective-permute-start(bf16[64,64,128]{2,1,0:T(8,128)(2,1)S(1)} %all-to-all-done.refs_2_.refs_0_), channel_id=1, source_target_pairs={{0,1},{1,0},{2,3},{3,2},{4,5},{5,4},{6,7},{7,6},{8,9},{9,8},{10,11... | collective-permute-start | bytes 3145736 | tf_op jit(solution)/shard_map/ppermute | solution.py:543
  41.3 1.1 copy-start.22
  49.5 15.0 %copy-start.1 = (bf16[32,4,4,4,192]{4,0,3,2,1:T(8,128)(2,1)S(1)}, bf16[32,4,4,4,192]{4,0,3,2,1:T(8,128)(2,1)}, u32[]{:S(2)}) copy-start(bf16[32,4,4,4,192]{4,0,3,2,1:T(8,128)(2,1)} %copy-done) | copy-start | bytes 2359300
  49.5 15.0 %copy-start.3 = (bf16[576,432]{1,0:T(8,128)(2,1)S(1)}, bf16[576,432]{1,0:T(8,128)(2,1)}, u32[]{:S(2)}) copy-start(bf16[576,432]{1,0:T(8,128)(2,1)} %get-tuple-element.62.refs_4_) | copy-start | bytes 1492996
  49.5 15.0 %copy-start.4 = (bf16[512,192]{1,0:T(8,128)(2,1)S(1)}, bf16[512,192]{1,0:T(8,128)(2,1)}, u32[]{:S(2)}) copy-start(bf16[512,192]{1,0:T(8,128)(2,1)} %get-tuple-element.63.refs_5_) | copy-start | bytes 589828
  49.6 15.0 %copy-start.6 = (f32[56,432]{1,0:T(8,128)S(1)}, f32[56,432]{1,0:T(8,128)}, u32[]{:S(2)}) copy-start(f32[56,432]{1,0:T(8,128)} %get-tuple-element.61.refs_3_) | copy-start | bytes 290308
  49.6 15.0 %all-to-all-start.1 = ((bf16[128,8,128]{2,1,0:T(8,128)(2,1)}), bf16[128,8,128]{2,1,0:T(8,128)(2,1)S(1)}, u32[]{:S(2)}, u32[]{:S(2)}) async-start(bf16[128,8,128]{2,1,0:T(8,128)(2,1)} %get-tuple-element.57), calls=%async_computation.1 | async-start | bytes 524288 | tf_op jit(solution)/shard_map/all_to_all | solution.py:569
  64.6 6.3 %copy-start.24 = (bf16[1024,128]{1,0:T(8,128)(2,1)S(1)}, bf16[1024,128]{1,0:T(8,128)(2,1)}, u32[]{:S(2)}) copy-start(bf16[1024,128]{1,0:T(8,128)(2,1)} %get-tuple-element.68) | copy-start | bytes 786436
  64.6 8.0 %copy-start.19 = (bf16[1024,128]{1,0:T(8,128)(2,1)S(1)}, bf16[1024,128]{1,0:T(8,128)(2,1)}, u32[]{:S(2)}) copy-start(bf16[1024,128]{1,0:T(8,128)(2,1)} %get-tuple-element.67.refs_2_) | copy-start | bytes 786436
  64.6 8.0 %copy-start.20 = (bf16[48,128]{1,0:T(8,128)(2,1)S(1)}, bf16[48,128]{1,0:T(8,128)(2,1)}, u32[]{:S(2)}) copy-start(bf16[48,128]{1,0:T(8,128)(2,1)} %get-tuple-element.69.refs_4_) | copy-start | bytes 36868
  69.6 2.9 %collective-permute-start.1 = (bf16[1536,128]{1,0:T(8,128)(2,1)S(1)}, bf16[1536,128]{1,0:T(8,128)(2,1)S(1)}, u32[]{:S(2)}, u32[]{:S(2)}) collective-permute-start(bf16[1536,128]{1,0:T(8,128)(2,1)S(1)} %get-tuple-element.66), channel_id=1, source_target_pairs={{0,1},{1,0},{2,3},{3,2},{4,5},{5,4},{6,7},{7,6},{8,9},{9,8},{10,11... | collective-permute-start | bytes 1179656 | tf_op jit(solution)/shard_map/ppermute | solution.py:543
  70.8 1.7 %collective-permute-start.2 = (bf16[1024,128]{1,0:T(8,128)(2,1)S(1)}, bf16[1024,128]{1,0:T(8,128)(2,1)S(1)}, u32[]{:S(2)}, u32[]{:S(2)}) collective-permute-start(bf16[1024,128]{1,0:T(8,128)(2,1)S(1)} %copy-done.24), channel_id=1, source_target_pairs={{0,1},{1,0},{2,3},{3,2},{4,5},{5,4},{6,7},{7,6},{8,9},{9,8},{10,11... | collective-permute-start | bytes 786440 | tf_op jit(solution)/shard_map/ppermute | solution.py:543
  98.6 7.0 %copy-start.9 = (bf16[64,40,128]{2,1,0:T(8,128)(2,1)}, bf16[64,40,128]{2,1,0:T(8,128)(2,1)S(1)}, u32[]{:S(2)}) copy-start(bf16[64,40,128]{2,1,0:T(8,128)(2,1)S(1)} %get-tuple-element.71.refs_2_) | copy-start | bytes 1966084
  98.6 7.0 %collective-permute-start.3 = (bf16[64,40,128]{2,1,0:T(8,128)(2,1)S(1)}, bf16[64,40,128]{2,1,0:T(8,128)(2,1)S(1)}, u32[]{:S(2)}, u32[]{:S(2)}) collective-permute-start(bf16[64,40,128]{2,1,0:T(8,128)(2,1)S(1)} %get-tuple-element.71.refs_2_), channel_id=1, source_target_pairs={{0,1},{1,0},{2,3},{3,2},{4,5},{5,4},{6,7},{7,6},{8,9},{9,8},{10,11... | collective-permute-start | bytes 1966088 | tf_op jit(solution)/shard_map/ppermute | solution.py:543
  100.9 18.6 %all-to-all-start.3 = ((bf16[64,40,128]{2,1,0:T(8,128)(2,1)}), bf16[64,40,128]{2,1,0:T(8,128)(2,1)S(1)}, u32[]{:S(2)}, u32[]{:S(2)}) async-start(bf16[64,40,128]{2,1,0:T(8,128)(2,1)} %get-tuple-element.70), calls=%async_computation.3 | async-start | bytes 1310720 | tf_op jit(solution)/shard_map/all_to_all | solution.py:540
  105.6 17.3 %copy-start.2 = (bf16[512,1024]{1,0:T(8,128)(2,1)S(1)}, bf16[512,1024]{1,0:T(8,128)(2,1)}, u32[]{:S(2)}) copy-start(bf16[512,1024]{1,0:T(8,128)(2,1)} %refs_5_.9) | copy-start | bytes 3145732
  105.6 17.3 %copy-start.5 = (bf16[192,512]{1,0:T(8,128)(2,1)S(1)}, bf16[192,512]{1,0:T(8,128)(2,1)}, u32[]{:S(2)}) copy-start(bf16[192,512]{1,0:T(8,128)(2,1)} %refs_4_.9) | copy-start | bytes 589828
  105.6 0.8 copy-start.23
  119.6 3.3 %collective-permute-start.4 = (bf16[64,40,128]{2,1,0:T(8,128)(2,1)S(1)}, bf16[64,40,128]{2,1,0:T(8,128)(2,1)S(1)}, u32[]{:S(2)}, u32[]{:S(2)}) collective-permute-start(bf16[64,40,128]{2,1,0:T(8,128)(2,1)S(1)} %all-to-all-done.3.refs_1_), channel_id=1, source_target_pairs={{0,1},{1,0},{2,3},{3,2},{4,5},{5,4},{6,7},{7,6},{8,9},{9,8},{10,11... | collective-permute-start | bytes 1966088 | tf_op jit(solution)/shard_map/ppermute | solution.py:543

commit v7 on v6

--- a/solution.py
+++ b/solution.py
@@ -60,6 +60,18 @@
     return user, length
 
 
+def prepare_tower(lengths, cot, project, up, down, mixer, rows):
+    mixer[...] = dot_nn(project[...], up[...]).astype(BF)
+    _, length = per_user(lengths)
+    shared = cot[...] / length[0:4].astype(F32)
+    shared = jnp.concatenate([shared, shared], axis=0)
+    coarse = shared.astype(BF)
+    fine = (shared - coarse.astype(F32)).astype(BF)
+    rows[:, 0:FH] = dot_nt(coarse, down[...])
+    for at, part in ((FH, project[0:128]), (FH + 128, project[64:192])):
+        rows[:, at : at + 128] = dot_nt(coarse, part) + dot_nt(fine, part)
+
+
 def conv_forward(
     lengths, x, counts_row, cot, e1, s1, t1, p1, e2, s2, t2, p2, *rest,
 ):
@@ -68,6 +80,8 @@
     if len(kept) == 1:
         (block,) = kept
     else:
+        project, up, down, mixer, per_user_rows, *kept = kept
+        prepare_tower(lengths, cot, project, up, down, mixer, per_user_rows)
         taps, weights, outer, inner, o1 = kept
     counts = column_of(counts_row[...])
     zero4 = jnp.zeros((HALF * HALF, ITEMS_HERE, E), F32)
@@ -164,31 +178,21 @@
     block[...] = jnp.broadcast_to(rows[None], (CHIPS, 64, 128))
 
 
-def tower_middle(picked, lengths, cot, project, up, down):
-    fetched = dot_nn(picked[:, 0:C], project[...]).astype(BF)
-    pre = dot_nn(fetched, up[...])
+def gelu_and_slope(v):
     scale = 0.7978845608028654
-    square = pre * pre
-    bent = jnp.tanh(scale * pre * (1.0 + 0.044715 * square))
+    square = v * v
+    bent = jnp.tanh(scale * v * (1.0 + 0.044715 * square))
     gate = 0.5 * (1.0 + bent)
-    act = (pre * gate).astype(BF)
-    slope = gate + 0.5 * pre * (1.0 - bent * bent) * (scale * (1.0 + 3 * 0.044715 * square))
-    _, length = per_user(lengths)
-    shared = cot[...] / length[0:4].astype(F32)
-    shared_half = shared.astype(BF)
-    act_grad = dot_nt(jnp.concatenate([shared_half, shared_half], axis=0), down[...])
+    return v * gate, gate + 0.5 * v * (1.0 - bent * bent) * (scale * (1.0 + 3 * 0.044715 * square))
+
+
+def for_live_rows(lengths, per_row):
     position = lax.broadcasted_iota(jnp.int32, (LENGTH, 1), 0)
-    pre_parts, base_parts = [], []
-    for u in range(USERS_HERE):
-        alive = (position < lengths[u]).astype(F32)
-        pre_parts.append(alive * act_grad[u : u + 1] * slope[u * LENGTH : (u + 1) * LENGTH])
-        base_parts.append(alive * shared[u : u + 1])
-    pre_grad = jnp.concatenate(pre_parts, axis=0).astype(BF)
-    return fetched, act, pre_grad, jnp.concatenate(base_parts, axis=0)
+    return jnp.concatenate([(position < lengths[u]).astype(F32) * per_row(u) for u in range(USERS_HERE)], axis=0)
 
 
 def tower(
-    core, lengths, own, other, ids_ref, cot, project, up, down,
+    core, lengths, own, other, ids_ref, mixer, rows,
     sent, picked_out,
 ):
     ids = jnp.concatenate([column_of(ids_ref[u : u + 1]) for u in range(USERS_HERE)], axis=0)
@@ -219,12 +223,10 @@
     picked = (dot_nn(pick_own, rows_of(own)) + dot_nn(pick_other, rows_of(other))).astype(BF)
     picked_out[...] = picked
     picked_out.leave()
-    _, _, pre_grad, base = tower_middle(picked, lengths, cot, project, up, down)
-    rows_grad = base + dot_nt(pre_grad, up[...])
-    rows_coarse = rows_grad.astype(BF)
-    rows_fine = (rows_grad - rows_coarse.astype(F32)).astype(BF)
-    low = dot_nt(rows_coarse, project[0:128]) + dot_nt(rows_fine, project[0:128])
-    high = dot_nt(rows_coarse, project[64:192]) + dot_nt(rows_fine, project[64:192])
+    _, slope = gelu_and_slope(dot_nn(picked[:, 0:C], mixer[...]))
+    pre_grad = for_live_rows(lengths, lambda u: rows[u : u + 1, 0:FH] * slope[u * LENGTH : (u + 1) * LENGTH]).astype(BF)
+    low = dot_nt(pre_grad, mixer[0:128]) + for_live_rows(lengths, lambda u: rows[u : u + 1, FH : FH + 128])
+    high = dot_nt(pre_grad, mixer[64:192]) + for_live_rows(lengths, lambda u: rows[u : u + 1, FH + 128 : FH + 256])
     lane = lax.broadcasted_iota(jnp.int32, (ROWS, 128), 1)
     tag = within.astype(F32)
     low = jnp.where(lane < 96, low, jnp.where(lane == 96, tag, 0.0)).astype(BF)
@@ -235,12 +237,15 @@
 
 
 def tower_sums(
-    core, lengths, picked, cot, project, up, down,
+    core, lengths, picked, rows, project, up, down,
     up_keep, up_send, factors, user_vec,
     halves,
 ):
     picked = picked[...]
-    fetched, act, pre_grad, _ = tower_middle(picked, lengths, cot, project, up, down)
+    fetched = dot_nn(picked[:, 0:C], project[...]).astype(BF)
+    act, slope = gelu_and_slope(dot_nn(fetched, up[...]))
+    act = act.astype(BF)
+    pre_grad = for_live_rows(lengths, lambda u: rows[u : u + 1, 0:FH] * slope[u * LENGTH : (u + 1) * LENGTH]).astype(BF)
     user, length = per_user(lengths)
     at = lax.broadcasted_iota(jnp.int32, (8, ROWS), 1)
     live = ((at // LENGTH == user) & (at - user * LENGTH < length)).astype(F32).astype(BF)
@@ -555,26 +560,29 @@
     )
     kept = call(
         conv_forward,
-        [shape((56, E), F32), shape((576, E)), shape((2 * 64, n, E)), shape((INNER, n, E)), shape((512, C))],
-        "shvvhvvhhvvh",
-        "h" * 5,
+        [
+            shape((C, FH)), shape((8, FH + 256), F32),
+            shape((56, E), F32), shape((576, E)), shape((2 * 64, n, E)), shape((INNER, n, E)), shape((512, C)),
+        ],
+        "shvvhvvhhvvhhhh",
+        "h" * 7,
         framed,
-    )(lengths, x, counts, user_cotangent, expand_first, *weights)
+    )(lengths, x, counts, user_cotangent, expand_first, *weights, item_project, tower_up, tower_down)
     own = across_chips(block)
-    own, (taps, kept_weights, outer, inner, o1) = lax.optimization_barrier((own, kept))
+    own, (mixer, user_rows, taps, kept_weights, outer, inner, o1) = lax.optimization_barrier((own, kept))
     other = swap(own)
-    sent, picked = call(tower, [shape((DEVICES, 8, 128)), shape((ROWS, 256))], "sshhvvhhh", "hh")(
-        core, lengths, own, other, histories, user_cotangent, item_project, tower_up, tower_down
+    sent, picked = call(tower, [shape((DEVICES, 8, 128)), shape((ROWS, 256))], "sshhvhh", "hh")(
+        core, lengths, own, other, histories, mixer, user_rows
     )
     back = lax.all_to_all(sent, AXES, 0, 0, tiled=True)
     up_keep, up_send, factors, user_vec = call(
         tower_sums,
         [shape((1024, 128)), shape((1024, 128)), shape((48, 128)), shape((USERS_HERE, D), F32)],
-        "sshvhhh",
+        "sshhhhh",
         "hhhv",
         [pltpu.VMEM((2, 1024, 128), BF)],
         unstaged=(0, 1),
-    )(core, lengths, picked, user_cotangent, item_project, tower_up, tower_down)
+    )(core, lengths, picked, user_rows, item_project, tower_up, tower_down)
     back, up_send = lax.optimization_barrier((back, up_send))
     up_other = swap(up_send)
     conv_keep, conv_send = call(

time: 128 us -> 127 us (level)
  transfers between devices with their start and end apart: 8 -> 8, of which waited for: 6 -> 6; matrix products, arithmetic and copies ran while one was open for 0% -> 0% of each run, Pallas kernels for 15% -> 17%
where the time goes in v7:
time: 127 us; the launch traced here: 126 us
  Pallas kernels  42.6 us (34%)
  starting transfers between devices  27.9 us (22%)
  waiting for transfers between devices  26.2 us (21%)
  blocking collectives  24.5 us (19%)
  local copies, waits for them, and re-layouts  4.01 us (3%)
    pallas_call x9, Pallas kernels, run(): pl.pallas_call(body, out_shape=outs, in_specs=[pl.BlockSpec(memory_space=...  42.6 us
    all_to_all x1, blocking collectives, across_chips(): lax.all_to_all(v, AXES, 0, 0, axis_index_groups=same_core, tiled=True)  24.5 us
    all_to_all x2, starting transfers between devices, across_chips(): lax.all_to_all(v, AXES, 0, 0, axis_index_groups=same_core, tiled=True)  16.8 us
    all_to_all x2, waiting for transfers between devices, across_chips(): lax.all_to_all(v, AXES, 0, 0, axis_index_groups=same_core, tiled=True)  14.9 us
    ppermute x5, starting transfers between devices, swap(): return lax.ppermute(v, 'seq', [(i, i ^ 1) for i in range(8)])  7.12 us
    ppermute x5, waiting for transfers between devices, swap(): return lax.ppermute(v, 'seq', [(i, i ^ 1) for i in range(8)])  5.64 us
    all_to_all x1, waiting for transfers between devices, local(): back = lax.all_to_all(sent, AXES, 0, 0, tiled=True)  5.62 us
    unnamed x51, local copies, waits for them, and re-layouts  4.01 us
  transfers between devices with their start and end apart: 8, of which 6 were waited for; matrix products, arithmetic and copies ran while one was open for 0% of the time, Pallas kernels for 17%

profile of v7, /device:TPU:1, one launch (start us, length us, event | category | flops | bytes accessed | tf_op | source)
XLA Modules:
  0.0 126.4 jit_solution(604890767805925123)
XLA Ops:
  0.6 0.0 copy-start.17
  0.7 0.0 copy-start.15
  0.7 0.0 copy-start.12
  0.7 0.0 copy-start.7
  0.7 0.0 copy-start.14
  0.7 0.0 copy-start.11
  0.7 0.0 copy-start.5
  0.7 0.0 copy-start.13
  0.7 0.0 copy-start.8
  0.8 0.0 copy-start.6
  0.8 0.0 copy-start.16
  0.8 2.0 %copy.29 = bf16[32,4,4,4,192]{4,0,3,2,1:T(8,128)(2,1)S(1)} copy(bf16[32,4,4,4,192]{4,3,2,1,0:T(4,128)(2,1)} %param.16) | data formatting | bytes 1572864 | tf_op args[0]
  2.8 0.0 copy-start
  2.9 4.4 %shard_map.247 = bf16[64,64,128]{2,1,0:T(8,128)(2,1)} custom-call(s32[4]{0:T(128)S(1)} %copy-done.17, bf16[64,32,192]{2,1,0:T(8,128)(2,1)S(1)} %bitcast.9, s32[1,32]{1,0:T(1,128)S(1)} %bitcast.17, f32[4,512]{1,0:T(4,128)S(1)} %copy-done.13, bf16[192,432]{1,0:T(8,128)(2,1)S(1)} %copy-done.5, bf16[9,432]{1,0:T(8,128)(2,1)S(1)} %copy-done.11, ...), custom_call_target="tpu_custom_call" | custom-call | flops 1000000000 | bytes 10000000 | tf_op jit(solution)/shard_map/pallas_call | solution.py:521
  7.3 12.0 %all-to-all-start = ((bf16[64,64,128]{2,1,0:T(8,128)(2,1)}), bf16[64,64,128]{2,1,0:T(8,128)(2,1)S(1)}, u32[]{:S(2)}, u32[]{:S(2)}) async-start(bf16[64,64,128]{2,1,0:T(8,128)(2,1)} %shard_map.247), calls=%async_computation | async-start | bytes 2097152 | tf_op jit(solution)/shard_map/all_to_all | solution.py:545
  19.3 11.0 %shard_map.248 = (bf16[192,1024]{1,0:T(8,128)(2,1)}, f32[8,1280]{1,0:T(8,128)}, f32[56,432]{1,0:T(8,128)}, bf16[576,432]{1,0:T(8,128)(2,1)}, bf16[128,32,432]{2,...) custom-call(s32[4]{0:T(128)} %refs_1_.3, bf16[64,32,192]{2,1,0:T(8,128)(2,1)} %bitcast.10, ...), custom_call_target="tpu_custom_call" | custom-call | flops 1000000000 | bytes 10000000 | tf_op jit(solution)/shard_map/pallas_call | solution.py:521
  30.3 6.2 %all-to-all-done.refs_2_.refs_0_ = bf16[64,64,128]{2,1,0:T(8,128)(2,1)S(1)} async-done(((bf16[64,64,128]{2,1,0:T(8,128)(2,1)}), bf16[64,64,128]{2,1,0:T(8,128)(2,1)S(1)}, u32[]{:S(2)}, u32[]{:S(2)}) %all-to-all-start) | async-done | bytes 1048608 | tf_op jit(solution)/shard_map/all_to_all | solution.py:545
  36.5 2.5 %collective-permute-start = (bf16[64,64,128]{2,1,0:T(8,128)(2,1)S(1)}, bf16[64,64,128]{2,1,0:T(8,128)(2,1)S(1)}, u32[]{:S(2)}, u32[]{:S(2)}) collective-permute-start(bf16[64,64,128]{2,1,0:T(8,128)(2,1)S(1)} %all-to-all-done.refs_2_.refs_0_), channel_id=1, source_target_pairs={{0,1},{1,0},{2,3},{3,2},{4,5},{5,4},{6,7},{7,6},{8,9},{9,8},{10,11... | collective-permute-start | bytes 3145736 | tf_op jit(solution)/shard_map/ppermute | solution.py:548
  39.0 2.3 %collective-permute-done.refs_3_.refs_1_ = bf16[64,64,128]{2,1,0:T(8,128)(2,1)S(1)} collective-permute-done((bf16[64,64,128]{2,1,0:T(8,128)(2,1)S(1)}, bf16[64,64,128]{2,1,0:T(8,128)(2,1)S(1)}, u32[]{:S(2)}, u32[]{:S(2)}) %collective-permute-start) | collective-permute-done | bytes 1048608 | tf_op jit(solution)/shard_map/ppermute | solution.py:548
  41.3 1.1 copy-done.22
  42.4 6.2 %shard_map.249 = (bf16[128,8,128]{2,1,0:T(8,128)(2,1)}, bf16[256,256]{1,0:T(8,128)(2,1)}) custom-call(s32[1]{0:T(128)} %bitcast.refs_0_, s32[4]{0:T(128)} %refs_1_.3, bf16[64,64,128]{2,1,0:T(8,128)(2,1)} %copy-done.21, bf16[64,64,128]{2,1,0:T(8,128)(2,1)} %copy-done.22, s32[4,64]{1,0:T(4,128)} %refs_4_.7, bf16[192,1024]{1,0:T(8,128)(2,1)} %get-tuple-element.61.refs_5_, ...), custom_call_target="tpu_custom_call" | custom-call | flops 1000000000 | bytes 10000000 | tf_op jit(solution)/shard_map/pallas_call | solution.py:521
  48.6 0.0 copy-start.1
  48.6 0.0 copy-start.4
  48.6 3.9 %all-to-all-start.1 = ((bf16[128,8,128]{2,1,0:T(8,128)(2,1)}), bf16[128,8,128]{2,1,0:T(8,128)(2,1)S(1)}, u32[]{:S(2)}, u32[]{:S(2)}) async-start(bf16[128,8,128]{2,1,0:T(8,128)(2,1)} %get-tuple-element.65), calls=%async_computation.1 | async-start | bytes 524288 | tf_op jit(solution)/shard_map/all_to_all | solution.py:577
  52.6 5.4 %shard_map.250 = (bf16[1024,128]{1,0:T(8,128)(2,1)}, bf16[1024,128]{1,0:T(8,128)(2,1)}, bf16[48,128]{1,0:T(8,128)(2,1)}, f32[4,512]{1,0:T(4,128)}) custom-call(s32[1]{0:T(128)} %bitcast.refs_0_, s32[4]{0:T(128)} %refs_1_.3, bf16[256,256]{1,0:T(8,128)(2,1)} %get-tuple-element.63.refs_2_, f32[8,1280]{1,0:T(8,128)} %get-tuple-element.62.refs_6_.refs_3_, ...), custom_call_target="tpu_custom_call" | custom-call | flops 1000000000 | bytes 10000000 | tf_op jit(solution)/shard_map/pallas_call | solution.py:521
  58.0 5.6 %all-to-all-done.1.refs_1_ = bf16[128,8,128]{2,1,0:T(8,128)(2,1)S(1)} async-done(((bf16[128,8,128]{2,1,0:T(8,128)(2,1)}), bf16[128,8,128]{2,1,0:T(8,128)(2,1)S(1)}, u32[]{:S(2)}, u32[]{:S(2)}) %all-to-all-start.1) | async-done | bytes 262176 | tf_op jit(solution)/shard_map/all_to_all | solution.py:577
  63.6 0.0 copy-start.24
  63.6 0.0 copy-start.19
  63.6 0.0 copy-start.20
  63.6 5.0 %shard_map.251 = (bf16[1536,128]{1,0:T(8,128)(2,1)S(1)}, bf16[1536,128]{1,0:T(8,128)(2,1)S(1)}) custom-call(s32[1]{0:T(128)} %bitcast.refs_0_, bf16[128,8,128]{2,1,0:T(8,128)(2,1)S(1)} %all-to-all-done.1.refs_1_, bf16[92,32,432]{2,1,0:T(8,128)(2,1)} %get-tuple-element.68.refs_2_, f32[56,432]{1,0:T(8,128)S(1)} %copy-done.10, bf16[576,432]{1,0:T(8,128)(2,1)S(1)} %copy-done.3, ...), custom_call_target="tpu_custom_call" | custom-call | flops 1000000000 | bytes 10000000 | tf_op jit(solution)/shard_map/pallas_call | solution.py:521
  68.7 1.2 collective-permute-start.1
  69.9 0.1 collective-permute-start.2
  70.0 1.6 %collective-permute-done.2.refs_3_ = bf16[1024,128]{1,0:T(8,128)(2,1)S(1)} collective-permute-done((bf16[1024,128]{1,0:T(8,128)(2,1)S(1)}, bf16[1024,128]{1,0:T(8,128)(2,1)S(1)}, u32[]{:S(2)}, u32[]{:S(2)}) %collective-permute-start.2) | collective-permute-done | bytes 262176 | tf_op jit(solution)/shard_map/ppermute | solution.py:548
  71.6 0.0 collective-permute-done.1.refs_1_
  71.6 0.3 shard_map.252
  71.9 24.5 %all_to_all.20.refs_0_ = bf16[64,80,128]{2,1,0:T(8,128)(2,1)S(1)} all-to-all(bf16[64,80,128]{2,1,0:T(8,128)(2,1)S(1)} %shard_map.252), channel_id=1, replica_groups={{0,2,4,6,8,10,12,14,16,18,20,22,24,26,28,30,32,34,36,38,40,42,44,46,48,..., dimensions={0} | all-to-all | bytes 2621440 | tf_op jit(solution)/shard_map/all_to_all | solution.py:545
  96.4 1.3 shard_map.253
  97.7 2.3 %collective-permute-start.3 = (bf16[64,40,128]{2,1,0:T(8,128)(2,1)S(1)}, bf16[64,40,128]{2,1,0:T(8,128)(2,1)S(1)}, u32[]{:S(2)}, u32[]{:S(2)}) collective-permute-start(bf16[64,40,128]{2,1,0:T(8,128)(2,1)S(1)} %get-tuple-element.79.refs_2_), channel_id=1, source_target_pairs={{0,1},{1,0},{2,3},{3,2},{4,5},{5,4},{6,7},{7,6},{8,9},{9,8},{10,11... | collective-permute-start | bytes 1966088 | tf_op jit(solution)/shard_map/ppermute | solution.py:548
  100.0 4.9 %all-to-all-start.3 = ((bf16[64,40,128]{2,1,0:T(8,128)(2,1)}), bf16[64,40,128]{2,1,0:T(8,128)(2,1)S(1)}, u32[]{:S(2)}, u32[]{:S(2)}) async-start(bf16[64,40,128]{2,1,0:T(8,128)(2,1)} %get-tuple-element.78), calls=%async_computation.3 | async-start | bytes 1310720 | tf_op jit(solution)/shard_map/all_to_all | solution.py:545
  104.8 0.0 copy-start.2
  104.8 0.0 copy-start.9
  104.9 0.0 collective-permute-done.3.refs_3_
  104.9 0.8 copy-done.23
  105.7 4.9 %shard_map.254 = (f32[1024,512]{1,0:T(8,128)}, f32[192,512]{1,0:T(8,128)}) custom-call(bf16[64,64,128]{2,1,0:T(8,128)(2,1)} %copy-done.21, bf16[64,64,128]{2,1,0:T(8,128)(2,1)} %copy-done.22, bf16[64,40,128]{2,1,0:T(8,128)(2,1)} %copy-done.18, bf16[64,40,128]{2,1,0:T(8,128)(2,1)} %copy-done.23), custom_call_target="tpu_custom_call" | custom-call | flops 1000000000 | bytes 10000000 | tf_op jit(solution)/shard_map/pallas_call | solution.py:521
  110.7 8.7 %all-to-all-done.3.refs_1_ = bf16[64,40,128]{2,1,0:T(8,128)(2,1)S(1)} async-done(((bf16[64,40,128]{2,1,0:T(8,128)(2,1)}), bf16[64,40,128]{2,1,0:T(8,128)(2,1)S(1)}, u32[]{:S(2)}, u32[]{:S(2)}) %all-to-all-start.3) | async-done | bytes 655392 | tf_op jit(solution)/shard_map/all_to_all | solution.py:545
  119.4 1.1 collective-permute-start.4
  120.4 1.7 %collective-permute-done.4.refs_2_ = bf16[64,40,128]{2,1,0:T(8,128)(2,1)S(1)} collective-permute-done((bf16[64,40,128]{2,1,0:T(8,128)(2,1)S(1)}, bf16[64,40,128]{2,1,0:T(8,128)(2,1)S(1)}, u32[]{:S(2)}, u32[]{:S(2)}) %collective-permute-start.4) | collective-permute-done | bytes 655392 | tf_op jit(solution)/shard_map/ppermute | solution.py:548
  122.2 4.1 %shard_map.255 = (f32[192,432]{1,0:T(8,128)}, f32[9,432]{1,0:T(8,128)}, f32[3,432]{1,0:T(4,128)}, f32[192,432]{1,0:T(8,128)}, f32[192,432]{1,0:T(8,128)}, /*inde...) custom-call(s32[1]{0:T(128)} %bitcast.refs_0_, ...), custom_call_target="tpu_custom_call", output_to_operand_aliasing={{8}: (3, {})} | custom-call | flops 1000000000 | bytes 10000000 | tf_op jit(solution)/shard_map/pallas_call | solution.py:521
  (29 shorter events, 0.1 us)
Async XLA Ops:
  0.6 2.1 %copy-start.17 = (s32[4]{0:T(128)S(1)}, s32[4]{0:T(128)}, u32[]{:S(2)}) copy-start(s32[4]{0:T(128)} %refs_1_.3) | copy-start | bytes 52
  0.7 2.1 %copy-start.15 = (bf16[3,432]{1,0:T(4,128)(2,1)S(1)}, bf16[3,432]{1,0:T(4,128)(2,1)}, u32[]{:S(2)}) copy-start(bf16[3,432]{1,0:T(4,128)(2,1)} %refs_10_.3) | copy-start | bytes 7780
  0.7 2.1 %copy-start.12 = (bf16[9,432]{1,0:T(8,128)(2,1)S(1)}, bf16[9,432]{1,0:T(8,128)(2,1)}, u32[]{:S(2)}) copy-start(bf16[9,432]{1,0:T(8,128)(2,1)} %refs_9_.3) | copy-start | bytes 23332
  0.7 2.1 %copy-start.7 = (bf16[192,432]{1,0:T(8,128)(2,1)S(1)}, bf16[192,432]{1,0:T(8,128)(2,1)}, u32[]{:S(2)}) copy-start(bf16[192,432]{1,0:T(8,128)(2,1)} %refs_8_.3) | copy-start | bytes 497668
  0.7 2.1 %copy-start.14 = (bf16[3,432]{1,0:T(4,128)(2,1)S(1)}, bf16[3,432]{1,0:T(4,128)(2,1)}, u32[]{:S(2)}) copy-start(bf16[3,432]{1,0:T(4,128)(2,1)} %refs_6_.4) | copy-start | bytes 7780
  0.7 2.1 %copy-start.11 = (bf16[9,432]{1,0:T(8,128)(2,1)S(1)}, bf16[9,432]{1,0:T(8,128)(2,1)}, u32[]{:S(2)}) copy-start(bf16[9,432]{1,0:T(8,128)(2,1)} %refs_5_.5) | copy-start | bytes 23332
  0.7 2.1 %copy-start.5 = (bf16[192,432]{1,0:T(8,128)(2,1)S(1)}, bf16[192,432]{1,0:T(8,128)(2,1)}, u32[]{:S(2)}) copy-start(bf16[192,432]{1,0:T(8,128)(2,1)} %refs_4_.6) | copy-start | bytes 497668
  0.7 2.1 %copy-start.13 = (f32[4,512]{1,0:T(4,128)S(1)}, f32[4,512]{1,0:T(4,128)}, u32[]{:S(2)}) copy-start(f32[4,512]{1,0:T(4,128)} %refs_3_.3) | copy-start | bytes 24580
  0.7 2.1 %copy-start.8 = (bf16[432,192]{0,1:T(8,128)(2,1)S(1)}, bf16[432,192]{0,1:T(8,128)(2,1)}, u32[]{:S(2)}) copy-start(bf16[432,192]{0,1:T(8,128)(2,1)} %param.28) | copy-start | bytes 497668
  0.8 2.1 %copy-start.6 = (bf16[432,192]{0,1:T(8,128)(2,1)S(1)}, bf16[432,192]{0,1:T(8,128)(2,1)}, u32[]{:S(2)}) copy-start(bf16[432,192]{0,1:T(8,128)(2,1)} %param.24) | copy-start | bytes 497668
  0.8 2.1 %copy-start.16 = (s32[32]{0:T(128)S(1)}, s32[32]{0:T(128)}, u32[]{:S(2)}) copy-start(s32[32]{0:T(128)} %param.17) | copy-start | bytes 388
  2.8 4.6 %copy-start = (bf16[32,4,4,4,192]{4,0,3,2,1:T(8,128)(2,1)}, bf16[32,4,4,4,192]{4,0,3,2,1:T(8,128)(2,1)S(1)}, u32[]{:S(2)}) copy-start(bf16[32,4,4,4,192]{4,0,3,2,1:T(8,128)(2,1)S(1)} %copy.29) | copy-start | bytes 2359300
  7.3 29.2 %all-to-all-start = ((bf16[64,64,128]{2,1,0:T(8,128)(2,1)}), bf16[64,64,128]{2,1,0:T(8,128)(2,1)S(1)}, u32[]{:S(2)}, u32[]{:S(2)}) async-start(bf16[64,64,128]{2,1,0:T(8,128)(2,1)} %shard_map.247), calls=%async_computation | async-start | bytes 2097152 | tf_op jit(solution)/shard_map/all_to_all | solution.py:545
  36.5 4.8 %copy-start.21 = (bf16[64,64,128]{2,1,0:T(8,128)(2,1)}, bf16[64,64,128]{2,1,0:T(8,128)(2,1)S(1)}, u32[]{:S(2)}) copy-start(bf16[64,64,128]{2,1,0:T(8,128)(2,1)S(1)} %all-to-all-done.refs_2_.refs_0_) | copy-start | bytes 3145732
  36.5 4.7 %collective-permute-start = (bf16[64,64,128]{2,1,0:T(8,128)(2,1)S(1)}, bf16[64,64,128]{2,1,0:T(8,128)(2,1)S(1)}, u32[]{:S(2)}, u32[]{:S(2)}) collective-permute-start(bf16[64,64,128]{2,1,0:T(8,128)(2,1)S(1)} %all-to-all-done.refs_2_.refs_0_), channel_id=1, source_target_pairs={{0,1},{1,0},{2,3},{3,2},{4,5},{5,4},{6,7},{7,6},{8,9},{9,8},{10,11... | collective-permute-start | bytes 3145736 | tf_op jit(solution)/shard_map/ppermute | solution.py:548
  41.3 1.1 copy-start.22
  48.6 15.0 %copy-start.1 = (bf16[32,4,4,4,192]{4,0,3,2,1:T(8,128)(2,1)S(1)}, bf16[32,4,4,4,192]{4,0,3,2,1:T(8,128)(2,1)}, u32[]{:S(2)}) copy-start(bf16[32,4,4,4,192]{4,0,3,2,1:T(8,128)(2,1)} %copy-done) | copy-start | bytes 2359300
  48.6 15.0 %copy-start.3 = (bf16[576,432]{1,0:T(8,128)(2,1)S(1)}, bf16[576,432]{1,0:T(8,128)(2,1)}, u32[]{:S(2)}) copy-start(bf16[576,432]{1,0:T(8,128)(2,1)} %get-tuple-element.70.refs_4_) | copy-start | bytes 1492996
  48.6 15.0 %copy-start.4 = (bf16[512,192]{1,0:T(8,128)(2,1)S(1)}, bf16[512,192]{1,0:T(8,128)(2,1)}, u32[]{:S(2)}) copy-start(bf16[512,192]{1,0:T(8,128)(2,1)} %get-tuple-element.71.refs_5_) | copy-start | bytes 589828
  48.6 15.0 %copy-start.10 = (f32[56,432]{1,0:T(8,128)S(1)}, f32[56,432]{1,0:T(8,128)}, u32[]{:S(2)}) copy-start(f32[56,432]{1,0:T(8,128)} %get-tuple-element.69.refs_3_) | copy-start | bytes 290308
  48.6 15.0 %all-to-all-start.1 = ((bf16[128,8,128]{2,1,0:T(8,128)(2,1)}), bf16[128,8,128]{2,1,0:T(8,128)(2,1)S(1)}, u32[]{:S(2)}, u32[]{:S(2)}) async-start(bf16[128,8,128]{2,1,0:T(8,128)(2,1)} %get-tuple-element.65), calls=%async_computation.1 | async-start | bytes 524288 | tf_op jit(solution)/shard_map/all_to_all | solution.py:577
  63.6 6.3 %copy-start.24 = (bf16[1024,128]{1,0:T(8,128)(2,1)S(1)}, bf16[1024,128]{1,0:T(8,128)(2,1)}, u32[]{:S(2)}) copy-start(bf16[1024,128]{1,0:T(8,128)(2,1)} %get-tuple-element.76) | copy-start | bytes 786436
  63.6 8.0 %copy-start.19 = (bf16[1024,128]{1,0:T(8,128)(2,1)S(1)}, bf16[1024,128]{1,0:T(8,128)(2,1)}, u32[]{:S(2)}) copy-start(bf16[1024,128]{1,0:T(8,128)(2,1)} %get-tuple-element.75.refs_2_) | copy-start | bytes 786436
  63.6 8.0 %copy-start.20 = (bf16[48,128]{1,0:T(8,128)(2,1)S(1)}, bf16[48,128]{1,0:T(8,128)(2,1)}, u32[]{:S(2)}) copy-start(bf16[48,128]{1,0:T(8,128)(2,1)} %get-tuple-element.77.refs_4_) | copy-start | bytes 36868
  68.7 2.9 %collective-permute-start.1 = (bf16[1536,128]{1,0:T(8,128)(2,1)S(1)}, bf16[1536,128]{1,0:T(8,128)(2,1)S(1)}, u32[]{:S(2)}, u32[]{:S(2)}) collective-permute-start(bf16[1536,128]{1,0:T(8,128)(2,1)S(1)} %get-tuple-element.74), channel_id=1, source_target_pairs={{0,1},{1,0},{2,3},{3,2},{4,5},{5,4},{6,7},{7,6},{8,9},{9,8},{10,11... | collective-permute-start | bytes 1179656 | tf_op jit(solution)/shard_map/ppermute | solution.py:548
  69.9 1.7 %collective-permute-start.2 = (bf16[1024,128]{1,0:T(8,128)(2,1)S(1)}, bf16[1024,128]{1,0:T(8,128)(2,1)S(1)}, u32[]{:S(2)}, u32[]{:S(2)}) collective-permute-start(bf16[1024,128]{1,0:T(8,128)(2,1)S(1)} %copy-done.24), channel_id=1, source_target_pairs={{0,1},{1,0},{2,3},{3,2},{4,5},{5,4},{6,7},{7,6},{8,9},{9,8},{10,11... | collective-permute-start | bytes 786440 | tf_op jit(solution)/shard_map/ppermute | solution.py:548
  97.6 7.2 %copy-start.18 = (bf16[64,40,128]{2,1,0:T(8,128)(2,1)}, bf16[64,40,128]{2,1,0:T(8,128)(2,1)S(1)}, u32[]{:S(2)}) copy-start(bf16[64,40,128]{2,1,0:T(8,128)(2,1)S(1)} %get-tuple-element.79.refs_2_) | copy-start | bytes 1966084
  97.7 7.2 %collective-permute-start.3 = (bf16[64,40,128]{2,1,0:T(8,128)(2,1)S(1)}, bf16[64,40,128]{2,1,0:T(8,128)(2,1)S(1)}, u32[]{:S(2)}, u32[]{:S(2)}) collective-permute-start(bf16[64,40,128]{2,1,0:T(8,128)(2,1)S(1)} %get-tuple-element.79.refs_2_), channel_id=1, source_target_pairs={{0,1},{1,0},{2,3},{3,2},{4,5},{5,4},{6,7},{7,6},{8,9},{9,8},{10,11... | collective-permute-start | bytes 1966088 | tf_op jit(solution)/shard_map/ppermute | solution.py:548
  100.0 19.4 %all-to-all-start.3 = ((bf16[64,40,128]{2,1,0:T(8,128)(2,1)}), bf16[64,40,128]{2,1,0:T(8,128)(2,1)S(1)}, u32[]{:S(2)}, u32[]{:S(2)}) async-start(bf16[64,40,128]{2,1,0:T(8,128)(2,1)} %get-tuple-element.78), calls=%async_computation.3 | async-start | bytes 1310720 | tf_op jit(solution)/shard_map/all_to_all | solution.py:545
  104.8 17.3 %copy-start.2 = (bf16[512,1024]{1,0:T(8,128)(2,1)S(1)}, bf16[512,1024]{1,0:T(8,128)(2,1)}, u32[]{:S(2)}) copy-start(bf16[512,1024]{1,0:T(8,128)(2,1)} %refs_5_.7) | copy-start | bytes 3145732
  104.8 17.3 %copy-start.9 = (bf16[192,512]{1,0:T(8,128)(2,1)S(1)}, bf16[192,512]{1,0:T(8,128)(2,1)}, u32[]{:S(2)}) copy-start(bf16[192,512]{1,0:T(8,128)(2,1)} %refs_4_.9) | copy-start | bytes 589828
  104.9 0.8 copy-start.23
  119.4 2.8 %collective-permute-start.4 = (bf16[64,40,128]{2,1,0:T(8,128)(2,1)S(1)}, bf16[64,40,128]{2,1,0:T(8,128)(2,1)S(1)}, u32[]{:S(2)}, u32[]{:S(2)}) collective-permute-start(bf16[64,40,128]{2,1,0:T(8,128)(2,1)S(1)} %all-to-all-done.3.refs_1_), channel_id=1, source_target_pairs={{0,1},{1,0},{2,3},{3,2},{4,5},{5,4},{6,7},{7,6},{8,9},{9,8},{10,11... | collective-permute-start | bytes 1966088 | tf_op jit(solution)/shard_map/ppermute | solution.py:548

commit v8 on v7

--- a/solution.py
+++ b/solution.py
@@ -220,7 +220,7 @@
     put_low = (sent_at == slot).astype(F32).astype(BF)
     put_high = (sent_at == slot + CAPACITY).astype(F32).astype(BF)
     own, other = own.ready(), other.ready()
-    picked = (dot_nn(pick_own, rows_of(own)) + dot_nn(pick_other, rows_of(other))).astype(BF)
+    picked = dot_nn(pick_own, rows_of(own)).astype(BF) + dot_nn(pick_other, rows_of(other)).astype(BF)
     picked_out[...] = picked
     picked_out.leave()
     _, slope = gelu_and_slope(dot_nn(picked[:, 0:C], mixer[...]))
@@ -430,14 +430,14 @@
     gs2[...] = small[76:85]
     gt2[...] = small[85:88]
     item = item_base[...]
-    parts = []
+    wide, parts = [], []
     for j in range(FH // 128):
-        part = halves[j // 4, :, 24:40, :].reshape(1024, 128)[(j % 4) * 256 : (j % 4) * 256 + C]
-        cut = slice(j * 128, (j + 1) * 128)
-        grad_up[:, cut] = dot_tn(project[...], part)
-        item = item + dot_nt(part, up[:, cut])
-        if j % 2:
-            parts.append(grad_up.leave_part((slice(None), pl.ds((j - 1) * 128, 256)), part_sems.at[j // 2]))
+        wide.append(halves[j // 4, :, 24:40, :].reshape(1024, 128)[(j % 4) * 256 : (j % 4) * 256 + C])
+    for j in range(4):
+        part = jnp.concatenate(wide[2 * j : 2 * j + 2], axis=1)
+        grad_up[:, j * 256 : (j + 1) * 256] = dot_tn(project[...], part)
+        parts.append(grad_up.leave_part((slice(None), pl.ds(j * 256, 256)), part_sems.at[j]))
+    item = item + dot_nt(jnp.concatenate(wide, axis=1), up[...])
     grad_item[...] = item
     grad_item.leave()
     for part in parts:

time: 127 us -> 126 us (level)
  Pallas kernels: 42.6 us -> 41.2 us
    pallas_call x9, Pallas kernels: 42.6 us -> 41.2 us  [run(): pl.pallas_call(body, out_shape=outs, in_specs=[pl.BlockSpec(memory_space=...]
where the time goes in v8:
time: 126 us; the launch traced here: 125 us
  Pallas kernels  41.2 us (33%)
  starting transfers between devices  27.9 us (22%)
  waiting for transfers between devices  26.2 us (21%)
  blocking collectives  24.5 us (19%)
  local copies, waits for them, and re-layouts  4.01 us (3%)
    pallas_call x9, Pallas kernels, run(): pl.pallas_call(body, out_shape=outs, in_specs=[pl.BlockSpec(memory_space=...  41.2 us
    all_to_all x1, blocking collectives, across_chips(): lax.all_to_all(v, AXES, 0, 0, axis_index_groups=same_core, tiled=True)  24.5 us
    all_to_all x2, starting transfers between devices, across_chips(): lax.all_to_all(v, AXES, 0, 0, axis_index_groups=same_core, tiled=True)  16.8 us
    all_to_all x2, waiting for transfers between devices, across_chips(): lax.all_to_all(v, AXES, 0, 0, axis_index_groups=same_core, tiled=True)  14.9 us
    ppermute x5, starting transfers between devices, swap(): return lax.ppermute(v, 'seq', [(i, i ^ 1) for i in range(8)])  7.12 us
    ppermute x5, waiting for transfers between devices, swap(): return lax.ppermute(v, 'seq', [(i, i ^ 1) for i in range(8)])  5.64 us
    all_to_all x1, waiting for transfers between devices, local(): back = lax.all_to_all(sent, AXES, 0, 0, tiled=True)  5.62 us
    unnamed x51, local copies, waits for them, and re-layouts  4.01 us
  transfers between devices with their start and end apart: 8, of which 6 were waited for; matrix products, arithmetic and copies ran while one was open for 0% of the time, Pallas kernels for 17%

profile of v8, /device:TPU:1, one launch (start us, length us, event | category | flops | bytes accessed | tf_op | source)
XLA Modules:
  0.0 125.1 jit_solution(36405250346115582)
XLA Ops:
  0.6 0.0 copy-start.17
  0.7 0.0 copy-start.15
  0.7 0.0 copy-start.12
  0.7 0.0 copy-start.7
  0.7 0.0 copy-start.14
  0.7 0.0 copy-start.11
  0.7 0.0 copy-start.5
  0.7 0.0 copy-start.13
  0.7 0.0 copy-start.8
  0.8 0.0 copy-start.6
  0.8 0.0 copy-start.16
  0.8 2.0 %copy.29 = bf16[32,4,4,4,192]{4,0,3,2,1:T(8,128)(2,1)S(1)} copy(bf16[32,4,4,4,192]{4,3,2,1,0:T(4,128)(2,1)} %param.16) | data formatting | bytes 1572864 | tf_op args[0]
  2.8 0.0 copy-start
  2.9 4.4 %shard_map.247 = bf16[64,64,128]{2,1,0:T(8,128)(2,1)} custom-call(s32[4]{0:T(128)S(1)} %copy-done.17, bf16[64,32,192]{2,1,0:T(8,128)(2,1)S(1)} %bitcast.9, s32[1,32]{1,0:T(1,128)S(1)} %bitcast.17, f32[4,512]{1,0:T(4,128)S(1)} %copy-done.13, bf16[192,432]{1,0:T(8,128)(2,1)S(1)} %copy-done.5, bf16[9,432]{1,0:T(8,128)(2,1)S(1)} %copy-done.11, ...), custom_call_target="tpu_custom_call" | custom-call | flops 1000000000 | bytes 10000000 | tf_op jit(solution)/shard_map/pallas_call | solution.py:521
  7.3 12.0 %all-to-all-start = ((bf16[64,64,128]{2,1,0:T(8,128)(2,1)}), bf16[64,64,128]{2,1,0:T(8,128)(2,1)S(1)}, u32[]{:S(2)}, u32[]{:S(2)}) async-start(bf16[64,64,128]{2,1,0:T(8,128)(2,1)} %shard_map.247), calls=%async_computation | async-start | bytes 2097152 | tf_op jit(solution)/shard_map/all_to_all | solution.py:545
  19.3 11.0 %shard_map.248 = (bf16[192,1024]{1,0:T(8,128)(2,1)}, f32[8,1280]{1,0:T(8,128)}, f32[56,432]{1,0:T(8,128)}, bf16[576,432]{1,0:T(8,128)(2,1)}, bf16[128,32,432]{2,...) custom-call(s32[4]{0:T(128)} %refs_1_.3, bf16[64,32,192]{2,1,0:T(8,128)(2,1)} %bitcast.10, ...), custom_call_target="tpu_custom_call" | custom-call | flops 1000000000 | bytes 10000000 | tf_op jit(solution)/shard_map/pallas_call | solution.py:521
  30.3 6.2 %all-to-all-done.refs_2_.refs_0_ = bf16[64,64,128]{2,1,0:T(8,128)(2,1)S(1)} async-done(((bf16[64,64,128]{2,1,0:T(8,128)(2,1)}), bf16[64,64,128]{2,1,0:T(8,128)(2,1)S(1)}, u32[]{:S(2)}, u32[]{:S(2)}) %all-to-all-start) | async-done | bytes 1048608 | tf_op jit(solution)/shard_map/all_to_all | solution.py:545
  36.5 2.5 %collective-permute-start = (bf16[64,64,128]{2,1,0:T(8,128)(2,1)S(1)}, bf16[64,64,128]{2,1,0:T(8,128)(2,1)S(1)}, u32[]{:S(2)}, u32[]{:S(2)}) collective-permute-start(bf16[64,64,128]{2,1,0:T(8,128)(2,1)S(1)} %all-to-all-done.refs_2_.refs_0_), channel_id=1, source_target_pairs={{0,1},{1,0},{2,3},{3,2},{4,5},{5,4},{6,7},{7,6},{8,9},{9,8},{10,11... | collective-permute-start | bytes 3145736 | tf_op jit(solution)/shard_map/ppermute | solution.py:548
  39.0 2.3 %collective-permute-done.refs_3_.refs_1_ = bf16[64,64,128]{2,1,0:T(8,128)(2,1)S(1)} collective-permute-done((bf16[64,64,128]{2,1,0:T(8,128)(2,1)S(1)}, bf16[64,64,128]{2,1,0:T(8,128)(2,1)S(1)}, u32[]{:S(2)}, u32[]{:S(2)}) %collective-permute-start) | collective-permute-done | bytes 1048608 | tf_op jit(solution)/shard_map/ppermute | solution.py:548
  41.3 1.1 copy-done.22
  42.4 5.3 %shard_map.249 = (bf16[128,8,128]{2,1,0:T(8,128)(2,1)}, bf16[256,256]{1,0:T(8,128)(2,1)}) custom-call(s32[1]{0:T(128)} %bitcast.refs_0_, s32[4]{0:T(128)} %refs_1_.3, bf16[64,64,128]{2,1,0:T(8,128)(2,1)} %copy-done.21, bf16[64,64,128]{2,1,0:T(8,128)(2,1)} %copy-done.22, s32[4,64]{1,0:T(4,128)} %refs_4_.7, bf16[192,1024]{1,0:T(8,128)(2,1)} %get-tuple-element.61.refs_5_, ...), custom_call_target="tpu_custom_call" | custom-call | flops 1000000000 | bytes 10000000 | tf_op jit(solution)/shard_map/pallas_call | solution.py:521
  47.7 0.0 copy-start.1
  47.7 0.0 copy-start.4
  47.7 3.9 %all-to-all-start.1 = ((bf16[128,8,128]{2,1,0:T(8,128)(2,1)}), bf16[128,8,128]{2,1,0:T(8,128)(2,1)S(1)}, u32[]{:S(2)}, u32[]{:S(2)}) async-start(bf16[128,8,128]{2,1,0:T(8,128)(2,1)} %get-tuple-element.65), calls=%async_computation.1 | async-start | bytes 524288 | tf_op jit(solution)/shard_map/all_to_all | solution.py:577
  51.7 5.4 %shard_map.250 = (bf16[1024,128]{1,0:T(8,128)(2,1)}, bf16[1024,128]{1,0:T(8,128)(2,1)}, bf16[48,128]{1,0:T(8,128)(2,1)}, f32[4,512]{1,0:T(4,128)}) custom-call(s32[1]{0:T(128)} %bitcast.refs_0_, s32[4]{0:T(128)} %refs_1_.3, bf16[256,256]{1,0:T(8,128)(2,1)} %get-tuple-element.63.refs_2_, f32[8,1280]{1,0:T(8,128)} %get-tuple-element.62.refs_6_.refs_3_, ...), custom_call_target="tpu_custom_call" | custom-call | flops 1000000000 | bytes 10000000 | tf_op jit(solution)/shard_map/pallas_call | solution.py:521
  57.1 5.6 %all-to-all-done.1.refs_1_ = bf16[128,8,128]{2,1,0:T(8,128)(2,1)S(1)} async-done(((bf16[128,8,128]{2,1,0:T(8,128)(2,1)}), bf16[128,8,128]{2,1,0:T(8,128)(2,1)S(1)}, u32[]{:S(2)}, u32[]{:S(2)}) %all-to-all-start.1) | async-done | bytes 262176 | tf_op jit(solution)/shard_map/all_to_all | solution.py:577
  62.7 0.0 copy-start.24
  62.7 0.0 copy-start.19
  62.7 0.0 copy-start.20
  62.7 5.0 %shard_map.251 = (bf16[1536,128]{1,0:T(8,128)(2,1)S(1)}, bf16[1536,128]{1,0:T(8,128)(2,1)S(1)}) custom-call(s32[1]{0:T(128)} %bitcast.refs_0_, bf16[128,8,128]{2,1,0:T(8,128)(2,1)S(1)} %all-to-all-done.1.refs_1_, bf16[92,32,432]{2,1,0:T(8,128)(2,1)} %get-tuple-element.68.refs_2_, f32[56,432]{1,0:T(8,128)S(1)} %copy-done.10, bf16[576,432]{1,0:T(8,128)(2,1)S(1)} %copy-done.3, ...), custom_call_target="tpu_custom_call" | custom-call | flops 1000000000 | bytes 10000000 | tf_op jit(solution)/shard_map/pallas_call | solution.py:521
  67.8 1.2 collective-permute-start.1
  69.0 0.1 collective-permute-start.2
  69.1 1.6 %collective-permute-done.2.refs_3_ = bf16[1024,128]{1,0:T(8,128)(2,1)S(1)} collective-permute-done((bf16[1024,128]{1,0:T(8,128)(2,1)S(1)}, bf16[1024,128]{1,0:T(8,128)(2,1)S(1)}, u32[]{:S(2)}, u32[]{:S(2)}) %collective-permute-start.2) | collective-permute-done | bytes 262176 | tf_op jit(solution)/shard_map/ppermute | solution.py:548
  70.7 0.0 collective-permute-done.1.refs_1_
  70.7 0.3 shard_map.252
  71.0 24.5 %all_to_all.20.refs_0_ = bf16[64,80,128]{2,1,0:T(8,128)(2,1)S(1)} all-to-all(bf16[64,80,128]{2,1,0:T(8,128)(2,1)S(1)} %shard_map.252), channel_id=1, replica_groups={{0,2,4,6,8,10,12,14,16,18,20,22,24,26,28,30,32,34,36,38,40,42,44,46,48,..., dimensions={0} | all-to-all | bytes 2621440 | tf_op jit(solution)/shard_map/all_to_all | solution.py:545
  95.5 1.3 %shard_map.253 = (bf16[64,40,128]{2,1,0:T(8,128)(2,1)}, bf16[64,40,128]{2,1,0:T(8,128)(2,1)S(1)}) custom-call(bf16[64,80,128]{2,1,0:T(8,128)(2,1)S(1)} %all_to_all.20.refs_0_), custom_call_target="tpu_custom_call" | custom-call | flops 1000000000 | bytes 10000000 | tf_op jit(solution)/shard_map/pallas_call | solution.py:521
  96.8 2.3 %collective-permute-start.3 = (bf16[64,40,128]{2,1,0:T(8,128)(2,1)S(1)}, bf16[64,40,128]{2,1,0:T(8,128)(2,1)S(1)}, u32[]{:S(2)}, u32[]{:S(2)}) collective-permute-start(bf16[64,40,128]{2,1,0:T(8,128)(2,1)S(1)} %get-tuple-element.79.refs_2_), channel_id=1, source_target_pairs={{0,1},{1,0},{2,3},{3,2},{4,5},{5,4},{6,7},{7,6},{8,9},{9,8},{10,11... | collective-permute-start | bytes 1966088 | tf_op jit(solution)/shard_map/ppermute | solution.py:548
  99.1 4.9 %all-to-all-start.3 = ((bf16[64,40,128]{2,1,0:T(8,128)(2,1)}), bf16[64,40,128]{2,1,0:T(8,128)(2,1)S(1)}, u32[]{:S(2)}, u32[]{:S(2)}) async-start(bf16[64,40,128]{2,1,0:T(8,128)(2,1)} %get-tuple-element.78), calls=%async_computation.3 | async-start | bytes 1310720 | tf_op jit(solution)/shard_map/all_to_all | solution.py:545
  103.9 0.0 copy-start.2
  103.9 0.0 copy-start.9
  104.0 0.0 collective-permute-done.3.refs_3_
  104.0 0.8 copy-done.23
  104.8 4.9 %shard_map.254 = (f32[1024,512]{1,0:T(8,128)}, f32[192,512]{1,0:T(8,128)}) custom-call(bf16[64,64,128]{2,1,0:T(8,128)(2,1)} %copy-done.21, bf16[64,64,128]{2,1,0:T(8,128)(2,1)} %copy-done.22, bf16[64,40,128]{2,1,0:T(8,128)(2,1)} %copy-done.18, bf16[64,40,128]{2,1,0:T(8,128)(2,1)} %copy-done.23), custom_call_target="tpu_custom_call" | custom-call | flops 1000000000 | bytes 10000000 | tf_op jit(solution)/shard_map/pallas_call | solution.py:521
  109.8 8.7 %all-to-all-done.3.refs_1_ = bf16[64,40,128]{2,1,0:T(8,128)(2,1)S(1)} async-done(((bf16[64,40,128]{2,1,0:T(8,128)(2,1)}), bf16[64,40,128]{2,1,0:T(8,128)(2,1)S(1)}, u32[]{:S(2)}, u32[]{:S(2)}) %all-to-all-start.3) | async-done | bytes 655392 | tf_op jit(solution)/shard_map/all_to_all | solution.py:545
  118.5 1.1 collective-permute-start.4
  119.5 1.7 %collective-permute-done.4.refs_2_ = bf16[64,40,128]{2,1,0:T(8,128)(2,1)S(1)} collective-permute-done((bf16[64,40,128]{2,1,0:T(8,128)(2,1)S(1)}, bf16[64,40,128]{2,1,0:T(8,128)(2,1)S(1)}, u32[]{:S(2)}, u32[]{:S(2)}) %collective-permute-start.4) | collective-permute-done | bytes 655392 | tf_op jit(solution)/shard_map/ppermute | solution.py:548
  121.3 3.6 %shard_map.255 = (f32[192,432]{1,0:T(8,128)}, f32[9,432]{1,0:T(8,128)}, f32[3,432]{1,0:T(4,128)}, f32[192,432]{1,0:T(8,128)}, f32[192,432]{1,0:T(8,128)}, /*inde...) custom-call(s32[1]{0:T(128)} %bitcast.refs_0_, ...), custom_call_target="tpu_custom_call", output_to_operand_aliasing={{8}: (3, {})} | custom-call | flops 1000000000 | bytes 10000000 | tf_op jit(solution)/shard_map/pallas_call | solution.py:521
  (29 shorter events, 0.1 us)
Async XLA Ops:
  0.6 2.1 %copy-start.17 = (s32[4]{0:T(128)S(1)}, s32[4]{0:T(128)}, u32[]{:S(2)}) copy-start(s32[4]{0:T(128)} %refs_1_.3) | copy-start | bytes 52
  0.7 2.1 %copy-start.15 = (bf16[3,432]{1,0:T(4,128)(2,1)S(1)}, bf16[3,432]{1,0:T(4,128)(2,1)}, u32[]{:S(2)}) copy-start(bf16[3,432]{1,0:T(4,128)(2,1)} %refs_10_.3) | copy-start | bytes 7780
  0.7 2.1 %copy-start.12 = (bf16[9,432]{1,0:T(8,128)(2,1)S(1)}, bf16[9,432]{1,0:T(8,128)(2,1)}, u32[]{:S(2)}) copy-start(bf16[9,432]{1,0:T(8,128)(2,1)} %refs_9_.3) | copy-start | bytes 23332
  0.7 2.1 %copy-start.7 = (bf16[192,432]{1,0:T(8,128)(2,1)S(1)}, bf16[192,432]{1,0:T(8,128)(2,1)}, u32[]{:S(2)}) copy-start(bf16[192,432]{1,0:T(8,128)(2,1)} %refs_8_.3) | copy-start | bytes 497668
  0.7 2.1 %copy-start.14 = (bf16[3,432]{1,0:T(4,128)(2,1)S(1)}, bf16[3,432]{1,0:T(4,128)(2,1)}, u32[]{:S(2)}) copy-start(bf16[3,432]{1,0:T(4,128)(2,1)} %refs_6_.4) | copy-start | bytes 7780
  0.7 2.1 %copy-start.11 = (bf16[9,432]{1,0:T(8,128)(2,1)S(1)}, bf16[9,432]{1,0:T(8,128)(2,1)}, u32[]{:S(2)}) copy-start(bf16[9,432]{1,0:T(8,128)(2,1)} %refs_5_.5) | copy-start | bytes 23332
  0.7 2.1 %copy-start.5 = (bf16[192,432]{1,0:T(8,128)(2,1)S(1)}, bf16[192,432]{1,0:T(8,128)(2,1)}, u32[]{:S(2)}) copy-start(bf16[192,432]{1,0:T(8,128)(2,1)} %refs_4_.6) | copy-start | bytes 497668
  0.7 2.1 %copy-start.13 = (f32[4,512]{1,0:T(4,128)S(1)}, f32[4,512]{1,0:T(4,128)}, u32[]{:S(2)}) copy-start(f32[4,512]{1,0:T(4,128)} %refs_3_.3) | copy-start | bytes 24580
  0.7 2.1 %copy-start.8 = (bf16[432,192]{0,1:T(8,128)(2,1)S(1)}, bf16[432,192]{0,1:T(8,128)(2,1)}, u32[]{:S(2)}) copy-start(bf16[432,192]{0,1:T(8,128)(2,1)} %param.28) | copy-start | bytes 497668
  0.8 2.1 %copy-start.6 = (bf16[432,192]{0,1:T(8,128)(2,1)S(1)}, bf16[432,192]{0,1:T(8,128)(2,1)}, u32[]{:S(2)}) copy-start(bf16[432,192]{0,1:T(8,128)(2,1)} %param.24) | copy-start | bytes 497668
  0.8 2.1 %copy-start.16 = (s32[32]{0:T(128)S(1)}, s32[32]{0:T(128)}, u32[]{:S(2)}) copy-start(s32[32]{0:T(128)} %param.17) | copy-start | bytes 388
  2.8 4.6 %copy-start = (bf16[32,4,4,4,192]{4,0,3,2,1:T(8,128)(2,1)}, bf16[32,4,4,4,192]{4,0,3,2,1:T(8,128)(2,1)S(1)}, u32[]{:S(2)}) copy-start(bf16[32,4,4,4,192]{4,0,3,2,1:T(8,128)(2,1)S(1)} %copy.29) | copy-start | bytes 2359300
  7.3 29.2 %all-to-all-start = ((bf16[64,64,128]{2,1,0:T(8,128)(2,1)}), bf16[64,64,128]{2,1,0:T(8,128)(2,1)S(1)}, u32[]{:S(2)}, u32[]{:S(2)}) async-start(bf16[64,64,128]{2,1,0:T(8,128)(2,1)} %shard_map.247), calls=%async_computation | async-start | bytes 2097152 | tf_op jit(solution)/shard_map/all_to_all | solution.py:545
  36.5 4.8 %copy-start.21 = (bf16[64,64,128]{2,1,0:T(8,128)(2,1)}, bf16[64,64,128]{2,1,0:T(8,128)(2,1)S(1)}, u32[]{:S(2)}) copy-start(bf16[64,64,128]{2,1,0:T(8,128)(2,1)S(1)} %all-to-all-done.refs_2_.refs_0_) | copy-start | bytes 3145732
  36.5 4.7 %collective-permute-start = (bf16[64,64,128]{2,1,0:T(8,128)(2,1)S(1)}, bf16[64,64,128]{2,1,0:T(8,128)(2,1)S(1)}, u32[]{:S(2)}, u32[]{:S(2)}) collective-permute-start(bf16[64,64,128]{2,1,0:T(8,128)(2,1)S(1)} %all-to-all-done.refs_2_.refs_0_), channel_id=1, source_target_pairs={{0,1},{1,0},{2,3},{3,2},{4,5},{5,4},{6,7},{7,6},{8,9},{9,8},{10,11... | collective-permute-start | bytes 3145736 | tf_op jit(solution)/shard_map/ppermute | solution.py:548
  41.3 1.1 copy-start.22
  47.7 15.0 %copy-start.1 = (bf16[32,4,4,4,192]{4,0,3,2,1:T(8,128)(2,1)S(1)}, bf16[32,4,4,4,192]{4,0,3,2,1:T(8,128)(2,1)}, u32[]{:S(2)}) copy-start(bf16[32,4,4,4,192]{4,0,3,2,1:T(8,128)(2,1)} %copy-done) | copy-start | bytes 2359300
  47.7 15.0 %copy-start.3 = (bf16[576,432]{1,0:T(8,128)(2,1)S(1)}, bf16[576,432]{1,0:T(8,128)(2,1)}, u32[]{:S(2)}) copy-start(bf16[576,432]{1,0:T(8,128)(2,1)} %get-tuple-element.70.refs_4_) | copy-start | bytes 1492996
  47.7 15.0 %copy-start.4 = (bf16[512,192]{1,0:T(8,128)(2,1)S(1)}, bf16[512,192]{1,0:T(8,128)(2,1)}, u32[]{:S(2)}) copy-start(bf16[512,192]{1,0:T(8,128)(2,1)} %get-tuple-element.71.refs_5_) | copy-start | bytes 589828
  47.7 15.0 %copy-start.10 = (f32[56,432]{1,0:T(8,128)S(1)}, f32[56,432]{1,0:T(8,128)}, u32[]{:S(2)}) copy-start(f32[56,432]{1,0:T(8,128)} %get-tuple-element.69.refs_3_) | copy-start | bytes 290308
  47.7 14.9 %all-to-all-start.1 = ((bf16[128,8,128]{2,1,0:T(8,128)(2,1)}), bf16[128,8,128]{2,1,0:T(8,128)(2,1)S(1)}, u32[]{:S(2)}, u32[]{:S(2)}) async-start(bf16[128,8,128]{2,1,0:T(8,128)(2,1)} %get-tuple-element.65), calls=%async_computation.1 | async-start | bytes 524288 | tf_op jit(solution)/shard_map/all_to_all | solution.py:577
  62.7 6.3 %copy-start.24 = (bf16[1024,128]{1,0:T(8,128)(2,1)S(1)}, bf16[1024,128]{1,0:T(8,128)(2,1)}, u32[]{:S(2)}) copy-start(bf16[1024,128]{1,0:T(8,128)(2,1)} %get-tuple-element.76) | copy-start | bytes 786436
  62.7 8.0 %copy-start.19 = (bf16[1024,128]{1,0:T(8,128)(2,1)S(1)}, bf16[1024,128]{1,0:T(8,128)(2,1)}, u32[]{:S(2)}) copy-start(bf16[1024,128]{1,0:T(8,128)(2,1)} %get-tuple-element.75.refs_2_) | copy-start | bytes 786436
  62.7 8.0 %copy-start.20 = (bf16[48,128]{1,0:T(8,128)(2,1)S(1)}, bf16[48,128]{1,0:T(8,128)(2,1)}, u32[]{:S(2)}) copy-start(bf16[48,128]{1,0:T(8,128)(2,1)} %get-tuple-element.77.refs_4_) | copy-start | bytes 36868
  67.8 2.9 %collective-permute-start.1 = (bf16[1536,128]{1,0:T(8,128)(2,1)S(1)}, bf16[1536,128]{1,0:T(8,128)(2,1)S(1)}, u32[]{:S(2)}, u32[]{:S(2)}) collective-permute-start(bf16[1536,128]{1,0:T(8,128)(2,1)S(1)} %get-tuple-element.74), channel_id=1, source_target_pairs={{0,1},{1,0},{2,3},{3,2},{4,5},{5,4},{6,7},{7,6},{8,9},{9,8},{10,11... | collective-permute-start | bytes 1179656 | tf_op jit(solution)/shard_map/ppermute | solution.py:548
  69.0 1.7 %collective-permute-start.2 = (bf16[1024,128]{1,0:T(8,128)(2,1)S(1)}, bf16[1024,128]{1,0:T(8,128)(2,1)S(1)}, u32[]{:S(2)}, u32[]{:S(2)}) collective-permute-start(bf16[1024,128]{1,0:T(8,128)(2,1)S(1)} %copy-done.24), channel_id=1, source_target_pairs={{0,1},{1,0},{2,3},{3,2},{4,5},{5,4},{6,7},{7,6},{8,9},{9,8},{10,11... | collective-permute-start | bytes 786440 | tf_op jit(solution)/shard_map/ppermute | solution.py:548
  96.8 7.2 %copy-start.18 = (bf16[64,40,128]{2,1,0:T(8,128)(2,1)}, bf16[64,40,128]{2,1,0:T(8,128)(2,1)S(1)}, u32[]{:S(2)}) copy-start(bf16[64,40,128]{2,1,0:T(8,128)(2,1)S(1)} %get-tuple-element.79.refs_2_) | copy-start | bytes 1966084
  96.8 7.2 %collective-permute-start.3 = (bf16[64,40,128]{2,1,0:T(8,128)(2,1)S(1)}, bf16[64,40,128]{2,1,0:T(8,128)(2,1)S(1)}, u32[]{:S(2)}, u32[]{:S(2)}) collective-permute-start(bf16[64,40,128]{2,1,0:T(8,128)(2,1)S(1)} %get-tuple-element.79.refs_2_), channel_id=1, source_target_pairs={{0,1},{1,0},{2,3},{3,2},{4,5},{5,4},{6,7},{7,6},{8,9},{9,8},{10,11... | collective-permute-start | bytes 1966088 | tf_op jit(solution)/shard_map/ppermute | solution.py:548
  99.1 19.4 %all-to-all-start.3 = ((bf16[64,40,128]{2,1,0:T(8,128)(2,1)}), bf16[64,40,128]{2,1,0:T(8,128)(2,1)S(1)}, u32[]{:S(2)}, u32[]{:S(2)}) async-start(bf16[64,40,128]{2,1,0:T(8,128)(2,1)} %get-tuple-element.78), calls=%async_computation.3 | async-start | bytes 1310720 | tf_op jit(solution)/shard_map/all_to_all | solution.py:545
  103.9 17.3 %copy-start.2 = (bf16[512,1024]{1,0:T(8,128)(2,1)S(1)}, bf16[512,1024]{1,0:T(8,128)(2,1)}, u32[]{:S(2)}) copy-start(bf16[512,1024]{1,0:T(8,128)(2,1)} %refs_5_.7) | copy-start | bytes 3145732
  103.9 17.3 %copy-start.9 = (bf16[192,512]{1,0:T(8,128)(2,1)S(1)}, bf16[192,512]{1,0:T(8,128)(2,1)}, u32[]{:S(2)}) copy-start(bf16[192,512]{1,0:T(8,128)(2,1)} %refs_4_.9) | copy-start | bytes 589828
  104.0 0.8 copy-start.23
  118.5 2.8 %collective-permute-start.4 = (bf16[64,40,128]{2,1,0:T(8,128)(2,1)S(1)}, bf16[64,40,128]{2,1,0:T(8,128)(2,1)S(1)}, u32[]{:S(2)}, u32[]{:S(2)}) collective-permute-start(bf16[64,40,128]{2,1,0:T(8,128)(2,1)S(1)} %all-to-all-done.3.refs_1_), channel_id=1, source_target_pairs={{0,1},{1,0},{2,3},{3,2},{4,5},{5,4},{6,7},{7,6},{8,9},{9,8},{10,11... | collective-permute-start | bytes 1966088 | tf_op jit(solution)/shard_map/ppermute | solution.py:548

commit v9 on v8

--- a/solution.py
+++ b/solution.py
@@ -90,7 +90,7 @@
     zero1 = jnp.zeros((ITEMS_HERE, E), F32)
     framed2[0] = zero1
     framed2[FRAMES + 1] = zero1
-    taps1 = s1[...].astype(F32)
+    half_taps = s1[...]
     taps2 = s2[...].astype(F32)
     frame1 = t1[...].astype(F32)
     frame2 = t2[...].astype(F32)
@@ -113,9 +113,11 @@
         if block is None:
             outer[pl.ds(f * CELLS, CELLS)] = value
             outer[pl.ds((FRAMES + f) * CELLS, CELLS)] = slope.astype(BF).reshape(CELLS, ITEMS_HERE, E)
-        outs = [jnp.zeros((ITEMS_HERE, E), F32)] * 4
+        outs = [None] * 4
         for out_cell, in_cell, tap in LINKS_FIRST:
-            outs[out_cell] = outs[out_cell] + value[in_cell].astype(F32) * taps1[tap]
+            term = value[in_cell] * half_taps[tap]
+            outs[out_cell] = term if outs[out_cell] is None else outs[out_cell] + term
+        outs = [v.astype(F32) for v in outs]
         for out_cell in range(4):
             framed1[f + 1, out_cell] = outs[out_cell]
             if block is None:

time: 126 us -> 125 us (level)
  no operation moved by 1% of the time
where the time goes in v9:
time: 125 us
  Pallas kernels  40.5 us (32%)
  starting transfers between devices  28.4 us (23%)
  waiting for transfers between devices  25.9 us (21%)
  blocking collectives  24.5 us (20%)
  local copies, waits for them, and re-layouts  4.01 us (3%)
    pallas_call x9, Pallas kernels, run(): pl.pallas_call(body, out_shape=outs, in_specs=[pl.BlockSpec(memory_space=...  40.5 us
    all_to_all x1, blocking collectives, across_chips(): lax.all_to_all(v, AXES, 0, 0, axis_index_groups=same_core, tiled=True)  24.5 us
    all_to_all x2, starting transfers between devices, across_chips(): lax.all_to_all(v, AXES, 0, 0, axis_index_groups=same_core, tiled=True)  16.6 us
    all_to_all x2, waiting for transfers between devices, across_chips(): lax.all_to_all(v, AXES, 0, 0, axis_index_groups=same_core, tiled=True)  14.7 us
    ppermute x5, starting transfers between devices, swap(): return lax.ppermute(v, 'seq', [(i, i ^ 1) for i in range(8)])  7.66 us
    ppermute x5, waiting for transfers between devices, swap(): return lax.ppermute(v, 'seq', [(i, i ^ 1) for i in range(8)])  5.64 us
    all_to_all x1, waiting for transfers between devices, local(): back = lax.all_to_all(sent, AXES, 0, 0, tiled=True)  5.62 us
    all_to_all x1, starting transfers between devices, local(): back = lax.all_to_all(sent, AXES, 0, 0, tiled=True)  4.12 us
  transfers between devices with their start and end apart: 8, of which 6 were waited for; matrix products, arithmetic and copies ran while one was open for 0% of the time, Pallas kernels for 17%

profile of v9, /device:TPU:1, one launch (start us, length us, event | category | flops | bytes accessed | tf_op | source)
XLA Modules:
  0.0 124.6 jit_solution(4000328007938177553)
XLA Ops:
  0.6 0.0 copy-start.17
  0.7 0.0 copy-start.15
  0.7 0.0 copy-start.12
  0.7 0.0 copy-start.7
  0.7 0.0 copy-start.14
  0.7 0.0 copy-start.11
  0.7 0.0 copy-start.5
  0.7 0.0 copy-start.13
  0.7 0.0 copy-start.8
  0.8 0.0 copy-start.6
  0.8 0.0 copy-start.16
  0.8 2.0 %copy.29 = bf16[32,4,4,4,192]{4,0,3,2,1:T(8,128)(2,1)S(1)} copy(bf16[32,4,4,4,192]{4,3,2,1,0:T(4,128)(2,1)} %param.16) | data formatting | bytes 1572864 | tf_op args[0]
  2.8 0.0 copy-start
  2.9 4.0 %shard_map.247 = bf16[64,64,128]{2,1,0:T(8,128)(2,1)} custom-call(s32[4]{0:T(128)S(1)} %copy-done.17, bf16[64,32,192]{2,1,0:T(8,128)(2,1)S(1)} %bitcast.9, s32[1,32]{1,0:T(1,128)S(1)} %bitcast.17, f32[4,512]{1,0:T(4,128)S(1)} %copy-done.13, bf16[192,432]{1,0:T(8,128)(2,1)S(1)} %copy-done.5, bf16[9,432]{1,0:T(8,128)(2,1)S(1)} %copy-done.11, ...), custom_call_target="tpu_custom_call" | custom-call | flops 1000000000 | bytes 10000000 | tf_op jit(solution)/shard_map/pallas_call | solution.py:523
  6.9 12.0 %all-to-all-start = ((bf16[64,64,128]{2,1,0:T(8,128)(2,1)}), bf16[64,64,128]{2,1,0:T(8,128)(2,1)S(1)}, u32[]{:S(2)}, u32[]{:S(2)}) async-start(bf16[64,64,128]{2,1,0:T(8,128)(2,1)} %shard_map.247), calls=%async_computation | async-start | bytes 2097152 | tf_op jit(solution)/shard_map/all_to_all | solution.py:547
  18.9 10.7 %shard_map.248 = (bf16[192,1024]{1,0:T(8,128)(2,1)}, f32[8,1280]{1,0:T(8,128)}, f32[56,432]{1,0:T(8,128)}, bf16[576,432]{1,0:T(8,128)(2,1)}, bf16[128,32,432]{2,...) custom-call(s32[4]{0:T(128)} %refs_1_.3, bf16[64,32,192]{2,1,0:T(8,128)(2,1)} %bitcast.10, ...), custom_call_target="tpu_custom_call" | custom-call | flops 1000000000 | bytes 10000000 | tf_op jit(solution)/shard_map/pallas_call | solution.py:523
  29.6 6.5 %all-to-all-done.refs_2_.refs_0_ = bf16[64,64,128]{2,1,0:T(8,128)(2,1)S(1)} async-done(((bf16[64,64,128]{2,1,0:T(8,128)(2,1)}), bf16[64,64,128]{2,1,0:T(8,128)(2,1)S(1)}, u32[]{:S(2)}, u32[]{:S(2)}) %all-to-all-start) | async-done | bytes 1048608 | tf_op jit(solution)/shard_map/all_to_all | solution.py:547
  36.1 2.5 %collective-permute-start = (bf16[64,64,128]{2,1,0:T(8,128)(2,1)S(1)}, bf16[64,64,128]{2,1,0:T(8,128)(2,1)S(1)}, u32[]{:S(2)}, u32[]{:S(2)}) collective-permute-start(bf16[64,64,128]{2,1,0:T(8,128)(2,1)S(1)} %all-to-all-done.refs_2_.refs_0_), channel_id=1, source_target_pairs={{0,1},{1,0},{2,3},{3,2},{4,5},{5,4},{6,7},{7,6},{8,9},{9,8},{10,11... | collective-permute-start | bytes 3145736 | tf_op jit(solution)/shard_map/ppermute | solution.py:550
  38.6 2.3 %collective-permute-done.refs_3_.refs_1_ = bf16[64,64,128]{2,1,0:T(8,128)(2,1)S(1)} collective-permute-done((bf16[64,64,128]{2,1,0:T(8,128)(2,1)S(1)}, bf16[64,64,128]{2,1,0:T(8,128)(2,1)S(1)}, u32[]{:S(2)}, u32[]{:S(2)}) %collective-permute-start) | collective-permute-done | bytes 1048608 | tf_op jit(solution)/shard_map/ppermute | solution.py:550
  40.9 1.1 copy-done.22
  41.9 5.3 %shard_map.249 = (bf16[128,8,128]{2,1,0:T(8,128)(2,1)}, bf16[256,256]{1,0:T(8,128)(2,1)}) custom-call(s32[1]{0:T(128)} %bitcast.refs_0_, s32[4]{0:T(128)} %refs_1_.3, bf16[64,64,128]{2,1,0:T(8,128)(2,1)} %copy-done.21, bf16[64,64,128]{2,1,0:T(8,128)(2,1)} %copy-done.22, s32[4,64]{1,0:T(4,128)} %refs_4_.7, bf16[192,1024]{1,0:T(8,128)(2,1)} %get-tuple-element.61.refs_5_, ...), custom_call_target="tpu_custom_call" | custom-call | flops 1000000000 | bytes 10000000 | tf_op jit(solution)/shard_map/pallas_call | solution.py:523
  47.3 0.0 copy-start.1
  47.3 0.0 copy-start.4
  47.3 4.1 %all-to-all-start.1 = ((bf16[128,8,128]{2,1,0:T(8,128)(2,1)}), bf16[128,8,128]{2,1,0:T(8,128)(2,1)S(1)}, u32[]{:S(2)}, u32[]{:S(2)}) async-start(bf16[128,8,128]{2,1,0:T(8,128)(2,1)} %get-tuple-element.65), calls=%async_computation.1 | async-start | bytes 524288 | tf_op jit(solution)/shard_map/all_to_all | solution.py:579
  51.4 5.4 %shard_map.250 = (bf16[1024,128]{1,0:T(8,128)(2,1)}, bf16[1024,128]{1,0:T(8,128)(2,1)}, bf16[48,128]{1,0:T(8,128)(2,1)}, f32[4,512]{1,0:T(4,128)}) custom-call(s32[1]{0:T(128)} %bitcast.refs_0_, s32[4]{0:T(128)} %refs_1_.3, bf16[256,256]{1,0:T(8,128)(2,1)} %get-tuple-element.63.refs_2_, f32[8,1280]{1,0:T(8,128)} %get-tuple-element.62.refs_6_.refs_3_, ...), custom_call_target="tpu_custom_call" | custom-call | flops 1000000000 | bytes 10000000 | tf_op jit(solution)/shard_map/pallas_call | solution.py:523
  56.8 5.6 %all-to-all-done.1.refs_1_ = bf16[128,8,128]{2,1,0:T(8,128)(2,1)S(1)} async-done(((bf16[128,8,128]{2,1,0:T(8,128)(2,1)}), bf16[128,8,128]{2,1,0:T(8,128)(2,1)S(1)}, u32[]{:S(2)}, u32[]{:S(2)}) %all-to-all-start.1) | async-done | bytes 262176 | tf_op jit(solution)/shard_map/all_to_all | solution.py:579
  62.5 0.0 copy-start.24
  62.5 0.0 copy-start.19
  62.5 0.0 copy-start.20
  62.5 5.0 %shard_map.251 = (bf16[1536,128]{1,0:T(8,128)(2,1)S(1)}, bf16[1536,128]{1,0:T(8,128)(2,1)S(1)}) custom-call(s32[1]{0:T(128)} %bitcast.refs_0_, bf16[128,8,128]{2,1,0:T(8,128)(2,1)S(1)} %all-to-all-done.1.refs_1_, bf16[92,32,432]{2,1,0:T(8,128)(2,1)} %get-tuple-element.68.refs_2_, f32[56,432]{1,0:T(8,128)S(1)} %copy-done.10, bf16[576,432]{1,0:T(8,128)(2,1)S(1)} %copy-done.3, ...), custom_call_target="tpu_custom_call" | custom-call | flops 1000000000 | bytes 10000000 | tf_op jit(solution)/shard_map/pallas_call | solution.py:523
  67.5 1.2 collective-permute-start.1
  68.7 0.1 collective-permute-start.2
  68.8 1.6 %collective-permute-done.2.refs_3_ = bf16[1024,128]{1,0:T(8,128)(2,1)S(1)} collective-permute-done((bf16[1024,128]{1,0:T(8,128)(2,1)S(1)}, bf16[1024,128]{1,0:T(8,128)(2,1)S(1)}, u32[]{:S(2)}, u32[]{:S(2)}) %collective-permute-start.2) | collective-permute-done | bytes 262176 | tf_op jit(solution)/shard_map/ppermute | solution.py:550
  70.5 0.0 collective-permute-done.1.refs_1_
  70.5 0.3 shard_map.252
  70.7 24.5 %all_to_all.20.refs_0_ = bf16[64,80,128]{2,1,0:T(8,128)(2,1)S(1)} all-to-all(bf16[64,80,128]{2,1,0:T(8,128)(2,1)S(1)} %shard_map.252), channel_id=1, replica_groups={{0,2,4,6,8,10,12,14,16,18,20,22,24,26,28,30,32,34,36,38,40,42,44,46,48,..., dimensions={0} | all-to-all | bytes 2621440 | tf_op jit(solution)/shard_map/all_to_all | solution.py:547
  95.3 1.3 %shard_map.253 = (bf16[64,40,128]{2,1,0:T(8,128)(2,1)}, bf16[64,40,128]{2,1,0:T(8,128)(2,1)S(1)}) custom-call(bf16[64,80,128]{2,1,0:T(8,128)(2,1)S(1)} %all_to_all.20.refs_0_), custom_call_target="tpu_custom_call" | custom-call | flops 1000000000 | bytes 10000000 | tf_op jit(solution)/shard_map/pallas_call | solution.py:523
  96.5 2.3 %collective-permute-start.3 = (bf16[64,40,128]{2,1,0:T(8,128)(2,1)S(1)}, bf16[64,40,128]{2,1,0:T(8,128)(2,1)S(1)}, u32[]{:S(2)}, u32[]{:S(2)}) collective-permute-start(bf16[64,40,128]{2,1,0:T(8,128)(2,1)S(1)} %get-tuple-element.79.refs_2_), channel_id=1, source_target_pairs={{0,1},{1,0},{2,3},{3,2},{4,5},{5,4},{6,7},{7,6},{8,9},{9,8},{10,11... | collective-permute-start | bytes 1966088 | tf_op jit(solution)/shard_map/ppermute | solution.py:550
  98.8 4.6 %all-to-all-start.3 = ((bf16[64,40,128]{2,1,0:T(8,128)(2,1)}), bf16[64,40,128]{2,1,0:T(8,128)(2,1)S(1)}, u32[]{:S(2)}, u32[]{:S(2)}) async-start(bf16[64,40,128]{2,1,0:T(8,128)(2,1)} %get-tuple-element.78), calls=%async_computation.3 | async-start | bytes 1310720 | tf_op jit(solution)/shard_map/all_to_all | solution.py:547
  103.5 0.0 copy-start.2
  103.5 0.0 copy-start.9
  103.5 0.0 collective-permute-done.3.refs_3_
  103.5 0.8 copy-done.23
  104.4 4.9 %shard_map.254 = (f32[1024,512]{1,0:T(8,128)}, f32[192,512]{1,0:T(8,128)}) custom-call(bf16[64,64,128]{2,1,0:T(8,128)(2,1)} %copy-done.21, bf16[64,64,128]{2,1,0:T(8,128)(2,1)} %copy-done.22, bf16[64,40,128]{2,1,0:T(8,128)(2,1)} %copy-done.18, bf16[64,40,128]{2,1,0:T(8,128)(2,1)} %copy-done.23), custom_call_target="tpu_custom_call" | custom-call | flops 1000000000 | bytes 10000000 | tf_op jit(solution)/shard_map/pallas_call | solution.py:523
  109.3 8.2 %all-to-all-done.3.refs_1_ = bf16[64,40,128]{2,1,0:T(8,128)(2,1)S(1)} async-done(((bf16[64,40,128]{2,1,0:T(8,128)(2,1)}), bf16[64,40,128]{2,1,0:T(8,128)(2,1)S(1)}, u32[]{:S(2)}, u32[]{:S(2)}) %all-to-all-start.3) | async-done | bytes 655392 | tf_op jit(solution)/shard_map/all_to_all | solution.py:547
  117.5 1.6 %collective-permute-start.4 = (bf16[64,40,128]{2,1,0:T(8,128)(2,1)S(1)}, bf16[64,40,128]{2,1,0:T(8,128)(2,1)S(1)}, u32[]{:S(2)}, u32[]{:S(2)}) collective-permute-start(bf16[64,40,128]{2,1,0:T(8,128)(2,1)S(1)} %all-to-all-done.3.refs_1_), channel_id=1, source_target_pairs={{0,1},{1,0},{2,3},{3,2},{4,5},{5,4},{6,7},{7,6},{8,9},{9,8},{10,11... | collective-permute-start | bytes 1966088 | tf_op jit(solution)/shard_map/ppermute | solution.py:550
  119.1 1.7 %collective-permute-done.4.refs_2_ = bf16[64,40,128]{2,1,0:T(8,128)(2,1)S(1)} collective-permute-done((bf16[64,40,128]{2,1,0:T(8,128)(2,1)S(1)}, bf16[64,40,128]{2,1,0:T(8,128)(2,1)S(1)}, u32[]{:S(2)}, u32[]{:S(2)}) %collective-permute-start.4) | collective-permute-done | bytes 655392 | tf_op jit(solution)/shard_map/ppermute | solution.py:550
  120.8 3.6 %shard_map.255 = (f32[192,432]{1,0:T(8,128)}, f32[9,432]{1,0:T(8,128)}, f32[3,432]{1,0:T(4,128)}, f32[192,432]{1,0:T(8,128)}, f32[192,432]{1,0:T(8,128)}, /*inde...) custom-call(s32[1]{0:T(128)} %bitcast.refs_0_, ...), custom_call_target="tpu_custom_call", output_to_operand_aliasing={{8}: (3, {})} | custom-call | flops 1000000000 | bytes 10000000 | tf_op jit(solution)/shard_map/pallas_call | solution.py:523
  (29 shorter events, 0.1 us)
Async XLA Ops:
  0.6 2.1 %copy-start.17 = (s32[4]{0:T(128)S(1)}, s32[4]{0:T(128)}, u32[]{:S(2)}) copy-start(s32[4]{0:T(128)} %refs_1_.3) | copy-start | bytes 52
  0.7 2.1 %copy-start.15 = (bf16[3,432]{1,0:T(4,128)(2,1)S(1)}, bf16[3,432]{1,0:T(4,128)(2,1)}, u32[]{:S(2)}) copy-start(bf16[3,432]{1,0:T(4,128)(2,1)} %refs_10_.3) | copy-start | bytes 7780
  0.7 2.1 %copy-start.12 = (bf16[9,432]{1,0:T(8,128)(2,1)S(1)}, bf16[9,432]{1,0:T(8,128)(2,1)}, u32[]{:S(2)}) copy-start(bf16[9,432]{1,0:T(8,128)(2,1)} %refs_9_.3) | copy-start | bytes 23332
  0.7 2.1 %copy-start.7 = (bf16[192,432]{1,0:T(8,128)(2,1)S(1)}, bf16[192,432]{1,0:T(8,128)(2,1)}, u32[]{:S(2)}) copy-start(bf16[192,432]{1,0:T(8,128)(2,1)} %refs_8_.3) | copy-start | bytes 497668
  0.7 2.1 %copy-start.14 = (bf16[3,432]{1,0:T(4,128)(2,1)S(1)}, bf16[3,432]{1,0:T(4,128)(2,1)}, u32[]{:S(2)}) copy-start(bf16[3,432]{1,0:T(4,128)(2,1)} %refs_6_.4) | copy-start | bytes 7780
  0.7 2.1 %copy-start.11 = (bf16[9,432]{1,0:T(8,128)(2,1)S(1)}, bf16[9,432]{1,0:T(8,128)(2,1)}, u32[]{:S(2)}) copy-start(bf16[9,432]{1,0:T(8,128)(2,1)} %refs_5_.5) | copy-start | bytes 23332
  0.7 2.1 %copy-start.5 = (bf16[192,432]{1,0:T(8,128)(2,1)S(1)}, bf16[192,432]{1,0:T(8,128)(2,1)}, u32[]{:S(2)}) copy-start(bf16[192,432]{1,0:T(8,128)(2,1)} %refs_4_.6) | copy-start | bytes 497668
  0.7 2.1 %copy-start.13 = (f32[4,512]{1,0:T(4,128)S(1)}, f32[4,512]{1,0:T(4,128)}, u32[]{:S(2)}) copy-start(f32[4,512]{1,0:T(4,128)} %refs_3_.3) | copy-start | bytes 24580
  0.7 2.1 %copy-start.8 = (bf16[432,192]{0,1:T(8,128)(2,1)S(1)}, bf16[432,192]{0,1:T(8,128)(2,1)}, u32[]{:S(2)}) copy-start(bf16[432,192]{0,1:T(8,128)(2,1)} %param.28) | copy-start | bytes 497668
  0.8 2.1 %copy-start.6 = (bf16[432,192]{0,1:T(8,128)(2,1)S(1)}, bf16[432,192]{0,1:T(8,128)(2,1)}, u32[]{:S(2)}) copy-start(bf16[432,192]{0,1:T(8,128)(2,1)} %param.24) | copy-start | bytes 497668
  0.8 2.1 %copy-start.16 = (s32[32]{0:T(128)S(1)}, s32[32]{0:T(128)}, u32[]{:S(2)}) copy-start(s32[32]{0:T(128)} %param.17) | copy-start | bytes 388
  2.8 4.2 %copy-start = (bf16[32,4,4,4,192]{4,0,3,2,1:T(8,128)(2,1)}, bf16[32,4,4,4,192]{4,0,3,2,1:T(8,128)(2,1)S(1)}, u32[]{:S(2)}) copy-start(bf16[32,4,4,4,192]{4,0,3,2,1:T(8,128)(2,1)S(1)} %copy.29) | copy-start | bytes 2359300
  6.9 29.2 %all-to-all-start = ((bf16[64,64,128]{2,1,0:T(8,128)(2,1)}), bf16[64,64,128]{2,1,0:T(8,128)(2,1)S(1)}, u32[]{:S(2)}, u32[]{:S(2)}) async-start(bf16[64,64,128]{2,1,0:T(8,128)(2,1)} %shard_map.247), calls=%async_computation | async-start | bytes 2097152 | tf_op jit(solution)/shard_map/all_to_all | solution.py:547
  36.1 4.8 %copy-start.21 = (bf16[64,64,128]{2,1,0:T(8,128)(2,1)}, bf16[64,64,128]{2,1,0:T(8,128)(2,1)S(1)}, u32[]{:S(2)}) copy-start(bf16[64,64,128]{2,1,0:T(8,128)(2,1)S(1)} %all-to-all-done.refs_2_.refs_0_) | copy-start | bytes 3145732
  36.1 4.7 %collective-permute-start = (bf16[64,64,128]{2,1,0:T(8,128)(2,1)S(1)}, bf16[64,64,128]{2,1,0:T(8,128)(2,1)S(1)}, u32[]{:S(2)}, u32[]{:S(2)}) collective-permute-start(bf16[64,64,128]{2,1,0:T(8,128)(2,1)S(1)} %all-to-all-done.refs_2_.refs_0_), channel_id=1, source_target_pairs={{0,1},{1,0},{2,3},{3,2},{4,5},{5,4},{6,7},{7,6},{8,9},{9,8},{10,11... | collective-permute-start | bytes 3145736 | tf_op jit(solution)/shard_map/ppermute | solution.py:550
  40.9 1.1 copy-start.22
  47.3 15.2 %copy-start.1 = (bf16[32,4,4,4,192]{4,0,3,2,1:T(8,128)(2,1)S(1)}, bf16[32,4,4,4,192]{4,0,3,2,1:T(8,128)(2,1)}, u32[]{:S(2)}) copy-start(bf16[32,4,4,4,192]{4,0,3,2,1:T(8,128)(2,1)} %copy-done) | copy-start | bytes 2359300
  47.3 15.2 %copy-start.3 = (bf16[576,432]{1,0:T(8,128)(2,1)S(1)}, bf16[576,432]{1,0:T(8,128)(2,1)}, u32[]{:S(2)}) copy-start(bf16[576,432]{1,0:T(8,128)(2,1)} %get-tuple-element.70.refs_4_) | copy-start | bytes 1492996
  47.3 15.2 %copy-start.4 = (bf16[512,192]{1,0:T(8,128)(2,1)S(1)}, bf16[512,192]{1,0:T(8,128)(2,1)}, u32[]{:S(2)}) copy-start(bf16[512,192]{1,0:T(8,128)(2,1)} %get-tuple-element.71.refs_5_) | copy-start | bytes 589828
  47.3 15.2 %copy-start.10 = (f32[56,432]{1,0:T(8,128)S(1)}, f32[56,432]{1,0:T(8,128)}, u32[]{:S(2)}) copy-start(f32[56,432]{1,0:T(8,128)} %get-tuple-element.69.refs_3_) | copy-start | bytes 290308
  47.3 15.1 %all-to-all-start.1 = ((bf16[128,8,128]{2,1,0:T(8,128)(2,1)}), bf16[128,8,128]{2,1,0:T(8,128)(2,1)S(1)}, u32[]{:S(2)}, u32[]{:S(2)}) async-start(bf16[128,8,128]{2,1,0:T(8,128)(2,1)} %get-tuple-element.65), calls=%async_computation.1 | async-start | bytes 524288 | tf_op jit(solution)/shard_map/all_to_all | solution.py:579
  62.5 6.3 %copy-start.24 = (bf16[1024,128]{1,0:T(8,128)(2,1)S(1)}, bf16[1024,128]{1,0:T(8,128)(2,1)}, u32[]{:S(2)}) copy-start(bf16[1024,128]{1,0:T(8,128)(2,1)} %get-tuple-element.76) | copy-start | bytes 786436
  62.5 8.0 %copy-start.19 = (bf16[1024,128]{1,0:T(8,128)(2,1)S(1)}, bf16[1024,128]{1,0:T(8,128)(2,1)}, u32[]{:S(2)}) copy-start(bf16[1024,128]{1,0:T(8,128)(2,1)} %get-tuple-element.75.refs_2_) | copy-start | bytes 786436
  62.5 8.0 %copy-start.20 = (bf16[48,128]{1,0:T(8,128)(2,1)S(1)}, bf16[48,128]{1,0:T(8,128)(2,1)}, u32[]{:S(2)}) copy-start(bf16[48,128]{1,0:T(8,128)(2,1)} %get-tuple-element.77.refs_4_) | copy-start | bytes 36868
  67.5 2.9 %collective-permute-start.1 = (bf16[1536,128]{1,0:T(8,128)(2,1)S(1)}, bf16[1536,128]{1,0:T(8,128)(2,1)S(1)}, u32[]{:S(2)}, u32[]{:S(2)}) collective-permute-start(bf16[1536,128]{1,0:T(8,128)(2,1)S(1)} %get-tuple-element.74), channel_id=1, source_target_pairs={{0,1},{1,0},{2,3},{3,2},{4,5},{5,4},{6,7},{7,6},{8,9},{9,8},{10,11... | collective-permute-start | bytes 1179656 | tf_op jit(solution)/shard_map/ppermute | solution.py:550
  68.7 1.7 %collective-permute-start.2 = (bf16[1024,128]{1,0:T(8,128)(2,1)S(1)}, bf16[1024,128]{1,0:T(8,128)(2,1)S(1)}, u32[]{:S(2)}, u32[]{:S(2)}) collective-permute-start(bf16[1024,128]{1,0:T(8,128)(2,1)S(1)} %copy-done.24), channel_id=1, source_target_pairs={{0,1},{1,0},{2,3},{3,2},{4,5},{5,4},{6,7},{7,6},{8,9},{9,8},{10,11... | collective-permute-start | bytes 786440 | tf_op jit(solution)/shard_map/ppermute | solution.py:550
  96.5 7.0 %copy-start.18 = (bf16[64,40,128]{2,1,0:T(8,128)(2,1)}, bf16[64,40,128]{2,1,0:T(8,128)(2,1)S(1)}, u32[]{:S(2)}) copy-start(bf16[64,40,128]{2,1,0:T(8,128)(2,1)S(1)} %get-tuple-element.79.refs_2_) | copy-start | bytes 1966084
  96.5 7.0 %collective-permute-start.3 = (bf16[64,40,128]{2,1,0:T(8,128)(2,1)S(1)}, bf16[64,40,128]{2,1,0:T(8,128)(2,1)S(1)}, u32[]{:S(2)}, u32[]{:S(2)}) collective-permute-start(bf16[64,40,128]{2,1,0:T(8,128)(2,1)S(1)} %get-tuple-element.79.refs_2_), channel_id=1, source_target_pairs={{0,1},{1,0},{2,3},{3,2},{4,5},{5,4},{6,7},{7,6},{8,9},{9,8},{10,11... | collective-permute-start | bytes 1966088 | tf_op jit(solution)/shard_map/ppermute | solution.py:550
  98.8 18.6 %all-to-all-start.3 = ((bf16[64,40,128]{2,1,0:T(8,128)(2,1)}), bf16[64,40,128]{2,1,0:T(8,128)(2,1)S(1)}, u32[]{:S(2)}, u32[]{:S(2)}) async-start(bf16[64,40,128]{2,1,0:T(8,128)(2,1)} %get-tuple-element.78), calls=%async_computation.3 | async-start | bytes 1310720 | tf_op jit(solution)/shard_map/all_to_all | solution.py:547
  103.5 17.3 %copy-start.2 = (bf16[512,1024]{1,0:T(8,128)(2,1)S(1)}, bf16[512,1024]{1,0:T(8,128)(2,1)}, u32[]{:S(2)}) copy-start(bf16[512,1024]{1,0:T(8,128)(2,1)} %refs_5_.7) | copy-start | bytes 3145732
  103.5 17.3 %copy-start.9 = (bf16[192,512]{1,0:T(8,128)(2,1)S(1)}, bf16[192,512]{1,0:T(8,128)(2,1)}, u32[]{:S(2)}) copy-start(bf16[192,512]{1,0:T(8,128)(2,1)} %refs_4_.9) | copy-start | bytes 589828
  103.5 0.8 copy-start.23
  117.5 3.3 %collective-permute-start.4 = (bf16[64,40,128]{2,1,0:T(8,128)(2,1)S(1)}, bf16[64,40,128]{2,1,0:T(8,128)(2,1)S(1)}, u32[]{:S(2)}, u32[]{:S(2)}) collective-permute-start(bf16[64,40,128]{2,1,0:T(8,128)(2,1)S(1)} %all-to-all-done.3.refs_1_), channel_id=1, source_target_pairs={{0,1},{1,0},{2,3},{3,2},{4,5},{5,4},{6,7},{7,6},{8,9},{9,8},{10,11... | collective-permute-start | bytes 1966088 | tf_op jit(solution)/shard_map/ppermute | solution.py:550
